TPU v7x, 768 devices: a whole 4x8x12 slice. The times are simulated.
768 devices in a mesh: row: 32 (over x_lo, y, core), col: 24 (over x_hi, z).
Axes of the slice: x: 4 (x_hi: 2, x_lo: 2; x = x_hi * 2 + x_lo), y: 8, z: 12, core: 2. Of those that a mesh axis runs over, the one named last changes fastest.
Arguments:
- p_blocks: bfloat16 [36864, 128, 128], P(('row', 'col')), may hold values from -6 to 6
- p_positions: int32 [36864], P(('row', 'col')), may hold values from 0 to 127, as said below
- h_blocks: bfloat16 [192, 128, 128], P('col'), may hold values from -0.1875 to 0.1875
- h_rows: int32 [192], replicated, may hold values from 0 to 63, as said below
- keep_mask: int32 [1536, 24], P(('row', 'col')), may hold values 0 or 1
- owner_ids: int32 [1536, 24, 1], P(('row', 'col')), may hold values from 0 to 31; in each aligned block of 48 rows (0 to 47, 48 to 95, ..., all dimensions but the last counted through in order) at most 2 rows name the same one
Outputs:
- owned: bfloat16 [24576, 2, 128, 128], P(('row', 'col'))
Inputs may be any that keep to these rules, and one draw needn't show every extreme that they name: `p_positions`: within each group of 48 entries no value repeats. `h_rows`: within each group of 8 entries no value repeats. `owner_ids`: among the 48 blocks of one group of 2 block rows no owner appears more than 2 times.
All inputs are finite; a program needn't handle non-finite values. No bound on the sum of `keep_mask` on one device may be relied on, other than what follows from the above.
Results may differ from a plain program's by a relative error of at most 0.012.
Values may be sent and summed in bfloat16 or wider, within the bound.
No kernel may reach another device: no remote copies, remote signals or barrier semaphores. Data moves between devices by JAX's collectives and lax.ppermute only.
A program may use at most 64 MiB of HBM per device.

v0:
```python
import jax
import jax.numpy as jnp
from jax import lax
from jax.sharding import PartitionSpec as P

RB = 2
KB = 64
SEND_CAP = 2


def shifted(value, axis, steps):
    count = lax.axis_size(axis)
    pairs = [(source, (source + steps) % count) for source in range(count)]
    return lax.ppermute(value, axis, pairs)


def advance(panel_blocks):
    return shifted(panel_blocks, "col", 1)


def local(p_blocks, p_positions, h_blocks, h_rows, keep_mask, owner_ids):
    cycle_size = lax.axis_size("col")
    owner_count = lax.axis_size("row")
    position = lax.axis_index("col")
    block_size = p_blocks.shape[-1]
    listed = h_blocks.shape[0]
    anchor = jnp.int32(0)
    slot_ids = p_positions % KB * RB + p_positions // KB
    dense_panel = (
        jnp.zeros((KB * RB, block_size, block_size), jnp.bfloat16).at[slot_ids].set(p_blocks)
    )
    dense_panel = dense_panel.reshape(KB, RB, block_size, block_size)

    def panel_term(panel_blocks, column):
        inner_rows = lax.dynamic_slice_in_dim(h_rows, column * listed, listed)
        columns = jnp.take(dense_panel, inner_rows, axis=0)
        return jnp.einsum(
            "nrab,nbc->rac", columns, panel_blocks, preferred_element_type=jnp.float32
        )

    def store_panel(totals, product, column):
        return lax.dynamic_update_slice(
            totals, product.astype(jnp.bfloat16)[:, None], (anchor, column, anchor, anchor)
        )

    totals = jnp.zeros((RB, cycle_size, block_size, block_size), jnp.bfloat16)
    totals = store_panel(totals, panel_term(h_blocks, position), position)

    def single_turn(turn_index, state):
        running, current = state
        current = advance(current)
        column = (position - turn_index) % cycle_size
        return (store_panel(running, panel_term(current, column), column), current)

    totals, current = lax.fori_loop(1, cycle_size, single_turn, (totals, h_blocks))
    kept_blocks = jnp.where(keep_mask[:, :, None, None] == 1, totals, jnp.zeros_like(totals))
    kept_blocks = kept_blocks.reshape(-1, block_size, block_size)
    target_owner = owner_ids.reshape(-1)
    onehot = (target_owner[:, None] == jnp.arange(owner_count, dtype=jnp.int32)[None, :]).astype(
        jnp.int32
    )
    rank_of = jnp.sum((jnp.cumsum(onehot, axis=0) - onehot) * onehot, axis=1)
    slot_match = (rank_of[:, None] == jnp.arange(SEND_CAP, dtype=jnp.int32)[None, :]).astype(
        jnp.int32
    )
    selector = (onehot[:, :, None] * slot_match[:, None, :]).astype(jnp.bfloat16)
    outgoing = jnp.einsum(
        "bos,bxy->osxy", selector, kept_blocks, preferred_element_type=jnp.float32
    ).astype(jnp.bfloat16)
    return lax.all_to_all(outgoing, "row", split_axis=0, concat_axis=0, tiled=True)


def solution(mesh):
    return jax.shard_map(
        local,
        mesh=mesh,
        in_specs=(
            P(("row", "col"), None, None),
            P(("row", "col")),
            P("col", None, None),
            P(),
            P(("row", "col"), None),
            P(("row", "col"), None, None),
        ),
        out_specs=P(("row", "col"), None, None, None),
        check_vma=False,
    )
```

profile of v0, /device:TPU:8, one launch (start us, length us, event | category | flops | bytes accessed | tf_op | source)
XLA Modules:
  0.0 389.1 jit_solution(16064788210936731180)
XLA Ops:
  5.6 3.0 broadcast_in_dim.43
  8.5 6.6 %scatter_fusion = bf16[128,128,128]{2,1,0:T(8,128)(2,1)} fusion(bf16[128,128,128]{2,1,0:T(8,128)(2,1)} %broadcast_in_dim.43, s32[48]{0:T(128)S(1)} %compare_select_fusion.2, bf16[48,128,128]{2,1,0:T(8,128)(2,1)S(1)} %copy-done), kind=kCustom, calls=%fused_computation.2 | custom fusion | bytes 4718784 | tf_op jit(solution)/shard_map/scatter | solution.py:30
  15.2 2.8 gather_fusion.1
  18.8 307.5 %while.17 = (s32[]{:T(128)}, bf16[2,24,128,128]{3,2,1,0:T(8,128)(2,1)S(1)}, bf16[8,128,128]{2,1,0:T(8,128)(2,1)S(1)}, s32[]{:T(128)}, s32[192]{0:T(256)S(1)}, /*...) while((s32[]{:T(128)}, ...), condition=%wide.region_4.6_spmd, body=%wide.region_3.5_spmd.sunk | while | flops 67404864 | bytes 3478459 | solution.py:55
  18.8 4.3 %collective-permute-start = (bf16[8,128,128]{2,1,0:T(8,128)(2,1)S(1)}, bf16[8,128,128]{2,1,0:T(8,128)(2,1)S(1)}, u32[]{:S(2)}, u32[]{:S(2)}) collective-permute-start(bf16[8,128,128]{2,1,0:T(8,128)(2,1)S(1)} %get-tuple-element.244), channel_id=1, source_target_pairs={{0,1},{1,2},{2,3},{3,4},{4,5},{5,6},{6,7},{7,8},{8,9},{9,10},{10,1... | collective-permute-start | bytes 786440 | tf_op jit(solution)/shard_map/while/body/eval_jaxpr/ppermute | solution.py:14
  23.2 2.8 gather_fusion
  26.0 16.1 %collective-permute-done = bf16[8,128,128]{2,1,0:T(8,128)(2,1)S(1)} collective-permute-done((bf16[8,128,128]{2,1,0:T(8,128)(2,1)S(1)}, bf16[8,128,128]{2,1,0:T(8,128)(2,1)S(1)}, u32[]{:S(2)}, u32[]{:S(2)}) %collective-permute-start) | collective-permute-done | bytes 262176 | tf_op jit(solution)/shard_map/while/body/eval_jaxpr/ppermute | solution.py:14
  42.5 1.9 collective-permute-start
  44.6 2.8 gather_fusion
  47.4 8.1 %collective-permute-done = bf16[8,128,128]{2,1,0:T(8,128)(2,1)S(1)} collective-permute-done((bf16[8,128,128]{2,1,0:T(8,128)(2,1)S(1)}, bf16[8,128,128]{2,1,0:T(8,128)(2,1)S(1)}, u32[]{:S(2)}, u32[]{:S(2)}) %collective-permute-start) | collective-permute-done | bytes 262176 | tf_op jit(solution)/shard_map/while/body/eval_jaxpr/ppermute | solution.py:14
  55.9 1.9 collective-permute-start
  58.0 2.8 gather_fusion
  60.8 7.2 %collective-permute-done = bf16[8,128,128]{2,1,0:T(8,128)(2,1)S(1)} collective-permute-done((bf16[8,128,128]{2,1,0:T(8,128)(2,1)S(1)}, bf16[8,128,128]{2,1,0:T(8,128)(2,1)S(1)}, u32[]{:S(2)}, u32[]{:S(2)}) %collective-permute-start) | collective-permute-done | bytes 262176 | tf_op jit(solution)/shard_map/while/body/eval_jaxpr/ppermute | solution.py:14
  68.4 1.9 collective-permute-start
  70.5 2.8 gather_fusion
  73.3 7.0 %collective-permute-done = bf16[8,128,128]{2,1,0:T(8,128)(2,1)S(1)} collective-permute-done((bf16[8,128,128]{2,1,0:T(8,128)(2,1)S(1)}, bf16[8,128,128]{2,1,0:T(8,128)(2,1)S(1)}, u32[]{:S(2)}, u32[]{:S(2)}) %collective-permute-start) | collective-permute-done | bytes 262176 | tf_op jit(solution)/shard_map/while/body/eval_jaxpr/ppermute | solution.py:14
  82.8 2.8 gather_fusion
  85.6 7.0 %collective-permute-done = bf16[8,128,128]{2,1,0:T(8,128)(2,1)S(1)} collective-permute-done((bf16[8,128,128]{2,1,0:T(8,128)(2,1)S(1)}, bf16[8,128,128]{2,1,0:T(8,128)(2,1)S(1)}, u32[]{:S(2)}, u32[]{:S(2)}) %collective-permute-start) | collective-permute-done | bytes 262176 | tf_op jit(solution)/shard_map/while/body/eval_jaxpr/ppermute | solution.py:14
  95.0 2.8 gather_fusion
  97.9 7.0 %collective-permute-done = bf16[8,128,128]{2,1,0:T(8,128)(2,1)S(1)} collective-permute-done((bf16[8,128,128]{2,1,0:T(8,128)(2,1)S(1)}, bf16[8,128,128]{2,1,0:T(8,128)(2,1)S(1)}, u32[]{:S(2)}, u32[]{:S(2)}) %collective-permute-start) | collective-permute-done | bytes 262176 | tf_op jit(solution)/shard_map/while/body/eval_jaxpr/ppermute | solution.py:14
  107.3 2.8 gather_fusion
  110.2 7.0 %collective-permute-done = bf16[8,128,128]{2,1,0:T(8,128)(2,1)S(1)} collective-permute-done((bf16[8,128,128]{2,1,0:T(8,128)(2,1)S(1)}, bf16[8,128,128]{2,1,0:T(8,128)(2,1)S(1)}, u32[]{:S(2)}, u32[]{:S(2)}) %collective-permute-start) | collective-permute-done | bytes 262176 | tf_op jit(solution)/shard_map/while/body/eval_jaxpr/ppermute | solution.py:14
  117.6 1.9 collective-permute-start
  119.6 2.8 gather_fusion
  122.5 7.0 %collective-permute-done = bf16[8,128,128]{2,1,0:T(8,128)(2,1)S(1)} collective-permute-done((bf16[8,128,128]{2,1,0:T(8,128)(2,1)S(1)}, bf16[8,128,128]{2,1,0:T(8,128)(2,1)S(1)}, u32[]{:S(2)}, u32[]{:S(2)}) %collective-permute-start) | collective-permute-done | bytes 262176 | tf_op jit(solution)/shard_map/while/body/eval_jaxpr/ppermute | solution.py:14
  129.9 1.9 collective-permute-start
  131.9 2.8 gather_fusion
  134.7 7.9 %collective-permute-done = bf16[8,128,128]{2,1,0:T(8,128)(2,1)S(1)} collective-permute-done((bf16[8,128,128]{2,1,0:T(8,128)(2,1)S(1)}, bf16[8,128,128]{2,1,0:T(8,128)(2,1)S(1)}, u32[]{:S(2)}, u32[]{:S(2)}) %collective-permute-start) | collective-permute-done | bytes 262176 | tf_op jit(solution)/shard_map/while/body/eval_jaxpr/ppermute | solution.py:14
  145.1 2.8 gather_fusion
  147.9 9.1 %collective-permute-done = bf16[8,128,128]{2,1,0:T(8,128)(2,1)S(1)} collective-permute-done((bf16[8,128,128]{2,1,0:T(8,128)(2,1)S(1)}, bf16[8,128,128]{2,1,0:T(8,128)(2,1)S(1)}, u32[]{:S(2)}, u32[]{:S(2)}) %collective-permute-start) | collective-permute-done | bytes 262176 | tf_op jit(solution)/shard_map/while/body/eval_jaxpr/ppermute | solution.py:14
  157.4 1.9 collective-permute-start
  159.4 2.8 gather_fusion
  162.3 9.4 %collective-permute-done = bf16[8,128,128]{2,1,0:T(8,128)(2,1)S(1)} collective-permute-done((bf16[8,128,128]{2,1,0:T(8,128)(2,1)S(1)}, bf16[8,128,128]{2,1,0:T(8,128)(2,1)S(1)}, u32[]{:S(2)}, u32[]{:S(2)}) %collective-permute-start) | collective-permute-done | bytes 262176 | tf_op jit(solution)/shard_map/while/body/eval_jaxpr/ppermute | solution.py:14
  172.1 1.9 collective-permute-start
  174.1 2.8 gather_fusion
  177.0 8.6 %collective-permute-done = bf16[8,128,128]{2,1,0:T(8,128)(2,1)S(1)} collective-permute-done((bf16[8,128,128]{2,1,0:T(8,128)(2,1)S(1)}, bf16[8,128,128]{2,1,0:T(8,128)(2,1)S(1)}, u32[]{:S(2)}, u32[]{:S(2)}) %collective-permute-start) | collective-permute-done | bytes 262176 | tf_op jit(solution)/shard_map/while/body/eval_jaxpr/ppermute | solution.py:14
  188.0 2.8 gather_fusion
  190.9 7.7 %collective-permute-done = bf16[8,128,128]{2,1,0:T(8,128)(2,1)S(1)} collective-permute-done((bf16[8,128,128]{2,1,0:T(8,128)(2,1)S(1)}, bf16[8,128,128]{2,1,0:T(8,128)(2,1)S(1)}, u32[]{:S(2)}, u32[]{:S(2)}) %collective-permute-start) | collective-permute-done | bytes 262176 | tf_op jit(solution)/shard_map/while/body/eval_jaxpr/ppermute | solution.py:14
  201.1 2.8 gather_fusion
  203.9 7.0 %collective-permute-done = bf16[8,128,128]{2,1,0:T(8,128)(2,1)S(1)} collective-permute-done((bf16[8,128,128]{2,1,0:T(8,128)(2,1)S(1)}, bf16[8,128,128]{2,1,0:T(8,128)(2,1)S(1)}, u32[]{:S(2)}, u32[]{:S(2)}) %collective-permute-start) | collective-permute-done | bytes 262176 | tf_op jit(solution)/shard_map/while/body/eval_jaxpr/ppermute | solution.py:14
  211.3 1.9 collective-permute-start
  213.3 2.8 gather_fusion
  216.2 7.0 %collective-permute-done = bf16[8,128,128]{2,1,0:T(8,128)(2,1)S(1)} collective-permute-done((bf16[8,128,128]{2,1,0:T(8,128)(2,1)S(1)}, bf16[8,128,128]{2,1,0:T(8,128)(2,1)S(1)}, u32[]{:S(2)}, u32[]{:S(2)}) %collective-permute-start) | collective-permute-done | bytes 262176 | tf_op jit(solution)/shard_map/while/body/eval_jaxpr/ppermute | solution.py:14
  225.6 2.8 gather_fusion
  228.5 7.0 %collective-permute-done = bf16[8,128,128]{2,1,0:T(8,128)(2,1)S(1)} collective-permute-done((bf16[8,128,128]{2,1,0:T(8,128)(2,1)S(1)}, bf16[8,128,128]{2,1,0:T(8,128)(2,1)S(1)}, u32[]{:S(2)}, u32[]{:S(2)}) %collective-permute-start) | collective-permute-done | bytes 262176 | tf_op jit(solution)/shard_map/while/body/eval_jaxpr/ppermute | solution.py:14
  237.9 2.8 gather_fusion
  240.8 7.0 %collective-permute-done = bf16[8,128,128]{2,1,0:T(8,128)(2,1)S(1)} collective-permute-done((bf16[8,128,128]{2,1,0:T(8,128)(2,1)S(1)}, bf16[8,128,128]{2,1,0:T(8,128)(2,1)S(1)}, u32[]{:S(2)}, u32[]{:S(2)}) %collective-permute-start) | collective-permute-done | bytes 262176 | tf_op jit(solution)/shard_map/while/body/eval_jaxpr/ppermute | solution.py:14
  250.2 2.8 gather_fusion
  253.1 7.0 %collective-permute-done = bf16[8,128,128]{2,1,0:T(8,128)(2,1)S(1)} collective-permute-done((bf16[8,128,128]{2,1,0:T(8,128)(2,1)S(1)}, bf16[8,128,128]{2,1,0:T(8,128)(2,1)S(1)}, u32[]{:S(2)}, u32[]{:S(2)}) %collective-permute-start) | collective-permute-done | bytes 262176 | tf_op jit(solution)/shard_map/while/body/eval_jaxpr/ppermute | solution.py:14
  260.4 1.9 collective-permute-start
  262.5 2.8 gather_fusion
  265.3 7.3 %collective-permute-done = bf16[8,128,128]{2,1,0:T(8,128)(2,1)S(1)} collective-permute-done((bf16[8,128,128]{2,1,0:T(8,128)(2,1)S(1)}, bf16[8,128,128]{2,1,0:T(8,128)(2,1)S(1)}, u32[]{:S(2)}, u32[]{:S(2)}) %collective-permute-start) | collective-permute-done | bytes 262176 | tf_op jit(solution)/shard_map/while/body/eval_jaxpr/ppermute | solution.py:14
  273.1 1.9 collective-permute-start
  275.1 2.8 gather_fusion
  278.0 8.4 %collective-permute-done = bf16[8,128,128]{2,1,0:T(8,128)(2,1)S(1)} collective-permute-done((bf16[8,128,128]{2,1,0:T(8,128)(2,1)S(1)}, bf16[8,128,128]{2,1,0:T(8,128)(2,1)S(1)}, u32[]{:S(2)}, u32[]{:S(2)}) %collective-permute-start) | collective-permute-done | bytes 262176 | tf_op jit(solution)/shard_map/while/body/eval_jaxpr/ppermute | solution.py:14
  286.8 1.9 collective-permute-start
  288.9 2.8 gather_fusion
  291.7 9.6 %collective-permute-done = bf16[8,128,128]{2,1,0:T(8,128)(2,1)S(1)} collective-permute-done((bf16[8,128,128]{2,1,0:T(8,128)(2,1)S(1)}, bf16[8,128,128]{2,1,0:T(8,128)(2,1)S(1)}, u32[]{:S(2)}, u32[]{:S(2)}) %collective-permute-start) | collective-permute-done | bytes 262176 | tf_op jit(solution)/shard_map/while/body/eval_jaxpr/ppermute | solution.py:14
  301.7 1.9 collective-permute-start
  303.7 2.8 gather_fusion
  306.6 7.0 %collective-permute-done = bf16[8,128,128]{2,1,0:T(8,128)(2,1)S(1)} collective-permute-done((bf16[8,128,128]{2,1,0:T(8,128)(2,1)S(1)}, bf16[8,128,128]{2,1,0:T(8,128)(2,1)S(1)}, u32[]{:S(2)}, u32[]{:S(2)}) %collective-permute-start) | collective-permute-done | bytes 262176 | tf_op jit(solution)/shard_map/while/body/eval_jaxpr/ppermute | solution.py:14
  316.0 2.8 gather_fusion
  318.9 7.0 %collective-permute-done = bf16[8,128,128]{2,1,0:T(8,128)(2,1)S(1)} collective-permute-done((bf16[8,128,128]{2,1,0:T(8,128)(2,1)S(1)}, bf16[8,128,128]{2,1,0:T(8,128)(2,1)S(1)}, u32[]{:S(2)}, u32[]{:S(2)}) %collective-permute-start) | collective-permute-done | bytes 262176 | tf_op jit(solution)/shard_map/while/body/eval_jaxpr/ppermute | solution.py:14
  328.7 59.1 %all_to_all.5 = bf16[32,2,128,128]{3,2,1,0:T(8,128)(2,1)S(1)} all-to-all(bf16[32,2,128,128]{3,2,1,0:T(8,128)(2,1)S(1)} %copy.25), channel_id=1, replica_groups=mesh['row'=32,'col'=24] {'row'}, dimensions={0} | all-to-all | bytes 4194304 | tf_op jit(solution)/shard_map/all_to_all | solution.py:70
  (125 shorter events, 40.2 us)
Async XLA Ops:
  5.6 3.0 copy-start
  18.0 0.8 copy-start.1
  18.8 23.3 %collective-permute-start = (bf16[8,128,128]{2,1,0:T(8,128)(2,1)S(1)}, bf16[8,128,128]{2,1,0:T(8,128)(2,1)S(1)}, u32[]{:S(2)}, u32[]{:S(2)}) collective-permute-start(bf16[8,128,128]{2,1,0:T(8,128)(2,1)S(1)} %get-tuple-element.244), channel_id=1, source_target_pairs={{0,1},{1,2},{2,3},{3,4},{4,5},{5,6},{6,7},{7,8},{8,9},{9,10},{10,1... | collective-permute-start | bytes 786440 | tf_op jit(solution)/shard_map/while/body/eval_jaxpr/ppermute | solution.py:14
  42.5 13.0 %collective-permute-start = (bf16[8,128,128]{2,1,0:T(8,128)(2,1)S(1)}, bf16[8,128,128]{2,1,0:T(8,128)(2,1)S(1)}, u32[]{:S(2)}, u32[]{:S(2)}) collective-permute-start(bf16[8,128,128]{2,1,0:T(8,128)(2,1)S(1)} %get-tuple-element.244), channel_id=1, source_target_pairs={{0,1},{1,2},{2,3},{3,4},{4,5},{5,6},{6,7},{7,8},{8,9},{9,10},{10,1... | collective-permute-start | bytes 786440 | tf_op jit(solution)/shard_map/while/body/eval_jaxpr/ppermute | solution.py:14
  55.9 12.1 %collective-permute-start = (bf16[8,128,128]{2,1,0:T(8,128)(2,1)S(1)}, bf16[8,128,128]{2,1,0:T(8,128)(2,1)S(1)}, u32[]{:S(2)}, u32[]{:S(2)}) collective-permute-start(bf16[8,128,128]{2,1,0:T(8,128)(2,1)S(1)} %get-tuple-element.244), channel_id=1, source_target_pairs={{0,1},{1,2},{2,3},{3,4},{4,5},{5,6},{6,7},{7,8},{8,9},{9,10},{10,1... | collective-permute-start | bytes 786440 | tf_op jit(solution)/shard_map/while/body/eval_jaxpr/ppermute | solution.py:14
  68.4 11.9 %collective-permute-start = (bf16[8,128,128]{2,1,0:T(8,128)(2,1)S(1)}, bf16[8,128,128]{2,1,0:T(8,128)(2,1)S(1)}, u32[]{:S(2)}, u32[]{:S(2)}) collective-permute-start(bf16[8,128,128]{2,1,0:T(8,128)(2,1)S(1)} %get-tuple-element.244), channel_id=1, source_target_pairs={{0,1},{1,2},{2,3},{3,4},{4,5},{5,6},{6,7},{7,8},{8,9},{9,10},{10,1... | collective-permute-start | bytes 786440 | tf_op jit(solution)/shard_map/while/body/eval_jaxpr/ppermute | solution.py:14
  80.7 11.9 %collective-permute-start = (bf16[8,128,128]{2,1,0:T(8,128)(2,1)S(1)}, bf16[8,128,128]{2,1,0:T(8,128)(2,1)S(1)}, u32[]{:S(2)}, u32[]{:S(2)}) collective-permute-start(bf16[8,128,128]{2,1,0:T(8,128)(2,1)S(1)} %get-tuple-element.244), channel_id=1, source_target_pairs={{0,1},{1,2},{2,3},{3,4},{4,5},{5,6},{6,7},{7,8},{8,9},{9,10},{10,1... | collective-permute-start | bytes 786440 | tf_op jit(solution)/shard_map/while/body/eval_jaxpr/ppermute | solution.py:14
  93.0 11.9 %collective-permute-start = (bf16[8,128,128]{2,1,0:T(8,128)(2,1)S(1)}, bf16[8,128,128]{2,1,0:T(8,128)(2,1)S(1)}, u32[]{:S(2)}, u32[]{:S(2)}) collective-permute-start(bf16[8,128,128]{2,1,0:T(8,128)(2,1)S(1)} %get-tuple-element.244), channel_id=1, source_target_pairs={{0,1},{1,2},{2,3},{3,4},{4,5},{5,6},{6,7},{7,8},{8,9},{9,10},{10,1... | collective-permute-start | bytes 786440 | tf_op jit(solution)/shard_map/while/body/eval_jaxpr/ppermute | solution.py:14
  105.3 11.9 %collective-permute-start = (bf16[8,128,128]{2,1,0:T(8,128)(2,1)S(1)}, bf16[8,128,128]{2,1,0:T(8,128)(2,1)S(1)}, u32[]{:S(2)}, u32[]{:S(2)}) collective-permute-start(bf16[8,128,128]{2,1,0:T(8,128)(2,1)S(1)} %get-tuple-element.244), channel_id=1, source_target_pairs={{0,1},{1,2},{2,3},{3,4},{4,5},{5,6},{6,7},{7,8},{8,9},{9,10},{10,1... | collective-permute-start | bytes 786440 | tf_op jit(solution)/shard_map/while/body/eval_jaxpr/ppermute | solution.py:14
  117.6 11.9 %collective-permute-start = (bf16[8,128,128]{2,1,0:T(8,128)(2,1)S(1)}, bf16[8,128,128]{2,1,0:T(8,128)(2,1)S(1)}, u32[]{:S(2)}, u32[]{:S(2)}) collective-permute-start(bf16[8,128,128]{2,1,0:T(8,128)(2,1)S(1)} %get-tuple-element.244), channel_id=1, source_target_pairs={{0,1},{1,2},{2,3},{3,4},{4,5},{5,6},{6,7},{7,8},{8,9},{9,10},{10,1... | collective-permute-start | bytes 786440 | tf_op jit(solution)/shard_map/while/body/eval_jaxpr/ppermute | solution.py:14
  129.9 12.8 %collective-permute-start = (bf16[8,128,128]{2,1,0:T(8,128)(2,1)S(1)}, bf16[8,128,128]{2,1,0:T(8,128)(2,1)S(1)}, u32[]{:S(2)}, u32[]{:S(2)}) collective-permute-start(bf16[8,128,128]{2,1,0:T(8,128)(2,1)S(1)} %get-tuple-element.244), channel_id=1, source_target_pairs={{0,1},{1,2},{2,3},{3,4},{4,5},{5,6},{6,7},{7,8},{8,9},{9,10},{10,1... | collective-permute-start | bytes 786440 | tf_op jit(solution)/shard_map/while/body/eval_jaxpr/ppermute | solution.py:14
  143.0 14.0 %collective-permute-start = (bf16[8,128,128]{2,1,0:T(8,128)(2,1)S(1)}, bf16[8,128,128]{2,1,0:T(8,128)(2,1)S(1)}, u32[]{:S(2)}, u32[]{:S(2)}) collective-permute-start(bf16[8,128,128]{2,1,0:T(8,128)(2,1)S(1)} %get-tuple-element.244), channel_id=1, source_target_pairs={{0,1},{1,2},{2,3},{3,4},{4,5},{5,6},{6,7},{7,8},{8,9},{9,10},{10,1... | collective-permute-start | bytes 786440 | tf_op jit(solution)/shard_map/while/body/eval_jaxpr/ppermute | solution.py:14
  157.4 14.3 %collective-permute-start = (bf16[8,128,128]{2,1,0:T(8,128)(2,1)S(1)}, bf16[8,128,128]{2,1,0:T(8,128)(2,1)S(1)}, u32[]{:S(2)}, u32[]{:S(2)}) collective-permute-start(bf16[8,128,128]{2,1,0:T(8,128)(2,1)S(1)} %get-tuple-element.244), channel_id=1, source_target_pairs={{0,1},{1,2},{2,3},{3,4},{4,5},{5,6},{6,7},{7,8},{8,9},{9,10},{10,1... | collective-permute-start | bytes 786440 | tf_op jit(solution)/shard_map/while/body/eval_jaxpr/ppermute | solution.py:14
  172.1 13.5 %collective-permute-start = (bf16[8,128,128]{2,1,0:T(8,128)(2,1)S(1)}, bf16[8,128,128]{2,1,0:T(8,128)(2,1)S(1)}, u32[]{:S(2)}, u32[]{:S(2)}) collective-permute-start(bf16[8,128,128]{2,1,0:T(8,128)(2,1)S(1)} %get-tuple-element.244), channel_id=1, source_target_pairs={{0,1},{1,2},{2,3},{3,4},{4,5},{5,6},{6,7},{7,8},{8,9},{9,10},{10,1... | collective-permute-start | bytes 786440 | tf_op jit(solution)/shard_map/while/body/eval_jaxpr/ppermute | solution.py:14
  186.0 12.6 %collective-permute-start = (bf16[8,128,128]{2,1,0:T(8,128)(2,1)S(1)}, bf16[8,128,128]{2,1,0:T(8,128)(2,1)S(1)}, u32[]{:S(2)}, u32[]{:S(2)}) collective-permute-start(bf16[8,128,128]{2,1,0:T(8,128)(2,1)S(1)} %get-tuple-element.244), channel_id=1, source_target_pairs={{0,1},{1,2},{2,3},{3,4},{4,5},{5,6},{6,7},{7,8},{8,9},{9,10},{10,1... | collective-permute-start | bytes 786440 | tf_op jit(solution)/shard_map/while/body/eval_jaxpr/ppermute | solution.py:14
  199.0 11.9 %collective-permute-start = (bf16[8,128,128]{2,1,0:T(8,128)(2,1)S(1)}, bf16[8,128,128]{2,1,0:T(8,128)(2,1)S(1)}, u32[]{:S(2)}, u32[]{:S(2)}) collective-permute-start(bf16[8,128,128]{2,1,0:T(8,128)(2,1)S(1)} %get-tuple-element.244), channel_id=1, source_target_pairs={{0,1},{1,2},{2,3},{3,4},{4,5},{5,6},{6,7},{7,8},{8,9},{9,10},{10,1... | collective-permute-start | bytes 786440 | tf_op jit(solution)/shard_map/while/body/eval_jaxpr/ppermute | solution.py:14
  211.3 11.9 %collective-permute-start = (bf16[8,128,128]{2,1,0:T(8,128)(2,1)S(1)}, bf16[8,128,128]{2,1,0:T(8,128)(2,1)S(1)}, u32[]{:S(2)}, u32[]{:S(2)}) collective-permute-start(bf16[8,128,128]{2,1,0:T(8,128)(2,1)S(1)} %get-tuple-element.244), channel_id=1, source_target_pairs={{0,1},{1,2},{2,3},{3,4},{4,5},{5,6},{6,7},{7,8},{8,9},{9,10},{10,1... | collective-permute-start | bytes 786440 | tf_op jit(solution)/shard_map/while/body/eval_jaxpr/ppermute | solution.py:14
  223.6 11.9 %collective-permute-start = (bf16[8,128,128]{2,1,0:T(8,128)(2,1)S(1)}, bf16[8,128,128]{2,1,0:T(8,128)(2,1)S(1)}, u32[]{:S(2)}, u32[]{:S(2)}) collective-permute-start(bf16[8,128,128]{2,1,0:T(8,128)(2,1)S(1)} %get-tuple-element.244), channel_id=1, source_target_pairs={{0,1},{1,2},{2,3},{3,4},{4,5},{5,6},{6,7},{7,8},{8,9},{9,10},{10,1... | collective-permute-start | bytes 786440 | tf_op jit(solution)/shard_map/while/body/eval_jaxpr/ppermute | solution.py:14
  235.9 11.9 %collective-permute-start = (bf16[8,128,128]{2,1,0:T(8,128)(2,1)S(1)}, bf16[8,128,128]{2,1,0:T(8,128)(2,1)S(1)}, u32[]{:S(2)}, u32[]{:S(2)}) collective-permute-start(bf16[8,128,128]{2,1,0:T(8,128)(2,1)S(1)} %get-tuple-element.244), channel_id=1, source_target_pairs={{0,1},{1,2},{2,3},{3,4},{4,5},{5,6},{6,7},{7,8},{8,9},{9,10},{10,1... | collective-permute-start | bytes 786440 | tf_op jit(solution)/shard_map/while/body/eval_jaxpr/ppermute | solution.py:14
  248.2 11.9 %collective-permute-start = (bf16[8,128,128]{2,1,0:T(8,128)(2,1)S(1)}, bf16[8,128,128]{2,1,0:T(8,128)(2,1)S(1)}, u32[]{:S(2)}, u32[]{:S(2)}) collective-permute-start(bf16[8,128,128]{2,1,0:T(8,128)(2,1)S(1)} %get-tuple-element.244), channel_id=1, source_target_pairs={{0,1},{1,2},{2,3},{3,4},{4,5},{5,6},{6,7},{7,8},{8,9},{9,10},{10,1... | collective-permute-start | bytes 786440 | tf_op jit(solution)/shard_map/while/body/eval_jaxpr/ppermute | solution.py:14
  260.4 12.2 %collective-permute-start = (bf16[8,128,128]{2,1,0:T(8,128)(2,1)S(1)}, bf16[8,128,128]{2,1,0:T(8,128)(2,1)S(1)}, u32[]{:S(2)}, u32[]{:S(2)}) collective-permute-start(bf16[8,128,128]{2,1,0:T(8,128)(2,1)S(1)} %get-tuple-element.244), channel_id=1, source_target_pairs={{0,1},{1,2},{2,3},{3,4},{4,5},{5,6},{6,7},{7,8},{8,9},{9,10},{10,1... | collective-permute-start | bytes 786440 | tf_op jit(solution)/shard_map/while/body/eval_jaxpr/ppermute | solution.py:14
  273.1 13.3 %collective-permute-start = (bf16[8,128,128]{2,1,0:T(8,128)(2,1)S(1)}, bf16[8,128,128]{2,1,0:T(8,128)(2,1)S(1)}, u32[]{:S(2)}, u32[]{:S(2)}) collective-permute-start(bf16[8,128,128]{2,1,0:T(8,128)(2,1)S(1)} %get-tuple-element.244), channel_id=1, source_target_pairs={{0,1},{1,2},{2,3},{3,4},{4,5},{5,6},{6,7},{7,8},{8,9},{9,10},{10,1... | collective-permute-start | bytes 786440 | tf_op jit(solution)/shard_map/while/body/eval_jaxpr/ppermute | solution.py:14
  286.8 14.5 %collective-permute-start = (bf16[8,128,128]{2,1,0:T(8,128)(2,1)S(1)}, bf16[8,128,128]{2,1,0:T(8,128)(2,1)S(1)}, u32[]{:S(2)}, u32[]{:S(2)}) collective-permute-start(bf16[8,128,128]{2,1,0:T(8,128)(2,1)S(1)} %get-tuple-element.244), channel_id=1, source_target_pairs={{0,1},{1,2},{2,3},{3,4},{4,5},{5,6},{6,7},{7,8},{8,9},{9,10},{10,1... | collective-permute-start | bytes 786440 | tf_op jit(solution)/shard_map/while/body/eval_jaxpr/ppermute | solution.py:14
  301.7 11.9 %collective-permute-start = (bf16[8,128,128]{2,1,0:T(8,128)(2,1)S(1)}, bf16[8,128,128]{2,1,0:T(8,128)(2,1)S(1)}, u32[]{:S(2)}, u32[]{:S(2)}) collective-permute-start(bf16[8,128,128]{2,1,0:T(8,128)(2,1)S(1)} %get-tuple-element.244), channel_id=1, source_target_pairs={{0,1},{1,2},{2,3},{3,4},{4,5},{5,6},{6,7},{7,8},{8,9},{9,10},{10,1... | collective-permute-start | bytes 786440 | tf_op jit(solution)/shard_map/while/body/eval_jaxpr/ppermute | solution.py:14
  314.0 11.9 %collective-permute-start = (bf16[8,128,128]{2,1,0:T(8,128)(2,1)S(1)}, bf16[8,128,128]{2,1,0:T(8,128)(2,1)S(1)}, u32[]{:S(2)}, u32[]{:S(2)}) collective-permute-start(bf16[8,128,128]{2,1,0:T(8,128)(2,1)S(1)} %get-tuple-element.244), channel_id=1, source_target_pairs={{0,1},{1,2},{2,3},{3,4},{4,5},{5,6},{6,7},{7,8},{8,9},{9,10},{10,1... | collective-permute-start | bytes 786440 | tf_op jit(solution)/shard_map/while/body/eval_jaxpr/ppermute | solution.py:14
where the time goes:
time: 391 us; the launch traced here: 389 us
  waiting for transfers between devices  183 us (47%)
  local copies, waits for them, and re-layouts  82.2 us (21%)
  blocking collectives  59.1 us (15%)
  starting transfers between devices  46.5 us (12%)
  matrix products  10.4 us (3%)
  other arithmetic  6.03 us (2%)
    ppermute x23, waiting for transfers between devices, shifted(): return lax.ppermute(value, axis, pairs)  183 us
    gather x24, local copies, waits for them, and re-layouts, panel_term(): columns = jnp.take(dense_panel, inner_rows, axis=0)  68 us
    all_to_all x1, blocking collectives, local(): lax.all_to_all(outgoing, 'row', split_axis=0, concat_axis=0, tiled=True)  59.1 us
    ppermute x23, starting transfers between devices, shifted(): return lax.ppermute(value, axis, pairs)  46.5 us
    dot_general x24, matrix products, panel_term(): jnp.einsum('nrab,nbc->rac', columns, panel_blocks, preferred_element_type...  8.92 us
  transfers between devices with their start and end apart: 23, of which 23 were waited for; matrix products, arithmetic and copies ran while one was open for 17% of the time, Pallas kernels for 0%

commit v1 on v0

v1 whole, which is shorter than its diff:
```python
import functools

import jax
import jax.numpy as jnp
import numpy as np
from jax import lax
from jax.experimental import pallas as pl
from jax.experimental.pallas import tpu as pltpu
from jax.sharding import PartitionSpec as P

NX, NY, NZ = 4, 8, 12
BS = 128
KB = 64
RB = 2
NH = 8
NCB = 24
NRG = 32
NP = 48
CAP = 2
BOTH = ("row", "col")


def device_of(x, y, z, core):
    x, y, z = x % NX, y % NY, z % NZ
    return ((x % 2) * 2 * NY + y * 2 + core) * NCB + (x // 2) * NZ + z


def pull(steps):
    return [
        (device_of(x + steps[k][0], y + steps[k][1], z + steps[k][2], k), device_of(x, y, z, k))
        for x in range(NX)
        for y in range(NY)
        for z in range(NZ)
        for k in range(2)
    ]


PLUS_ONE = pull(((1, 0, 0), (0, 0, 1)))
MINUS_ONE = pull(((0, 0, -1), (-1, 0, 0)))
PLUS_TWO = pull(((0, 1, 0), (0, -1, 0)))
OTHER_CORE = [(r, r ^ 1) for r in range(NRG)]


def colour(x, y, z):
    return lax.rem(x + 2 * y + z, 4)


def pick_kernel(where, h_ref, out_ref):
    row = where[0]
    x_lo, y, core = row // (2 * NY), (row // 2) % NY, row % 2
    for d in range(NCB):
        c = colour(2 * (d // NZ) + x_lo, y, d % NZ)
        out_ref[d] = h_ref[2 * c + core]


def product_kernel(where, pos, rows, keep, owner, p_hbm, *refs):
    panels, (out_ref, p_all, place, slot, count, sem) = refs[:8], refs[8:]
    load = pltpu.make_async_copy(p_hbm, p_all.at[pl.ds(0, NP)], sem)
    load.start()
    p_all[NP] = jnp.zeros((BS, BS), jnp.bfloat16)
    out_ref[...] = jnp.zeros_like(out_ref)

    row, col = where[0], where[1]
    x, y, z, core = 2 * (col // NZ) + row // (2 * NY), (row // 2) % NY, col % NZ, row % 2
    c = colour(x, y, z)
    listed = []
    for k in (core, 1 - core):
        for step in (0, 1, 3, 2):
            listed.append(2 * lax.rem(c + step, 4) + k)

    def clear(i, carry):
        place[i] = NP
        return carry

    lax.fori_loop(0, RB * KB, clear, 0)

    def note(i, carry):
        place[pos[i]] = i
        return carry

    lax.fori_loop(0, NP, note, 0)

    def reset(i, carry):
        count[i] = 0
        return carry

    lax.fori_loop(0, NRG, reset, 0)

    def rank(i, carry):
        to = owner[i // NCB, i % NCB]
        used = count[to]
        count[to] = used + 1
        slot[i] = to * CAP + used
        return carry

    lax.fori_loop(0, RB * NCB, rank, 0)
    load.wait()

    def column(j, carry):
        inner = [rows[j * NH + n] for n in listed]
        right = jnp.concatenate([panel[j] for panel in panels], axis=0)
        for i in range(RB):
            left = jnp.concatenate([p_all[place[i * KB + r]] for r in inner], axis=1)
            block = jnp.dot(left, right, preferred_element_type=jnp.float32).astype(jnp.bfloat16)
            out_ref[slot[i * NCB + j]] = jnp.where(keep[i, j] == 1, block, jnp.zeros_like(block))
        return carry

    lax.fori_loop(0, NCB, column, 0)


def local(p_blocks, p_positions, h_blocks, h_rows, keep_mask, owner_ids):
    where = jnp.stack([lax.axis_index("row"), lax.axis_index("col")])
    smem = pl.BlockSpec(memory_space=pltpu.SMEM)
    vmem = pl.BlockSpec(memory_space=pltpu.VMEM)
    panel = jax.ShapeDtypeStruct((NCB, BS, BS), jnp.bfloat16)
    picked = pl.pallas_call(
        pick_kernel, out_shape=panel, in_specs=[smem, vmem], out_specs=vmem, name="pick"
    )(where, h_blocks)
    own = lax.all_to_all(picked, "col", split_axis=0, concat_axis=0, tiled=True)
    mine = [own] + [lax.ppermute(own, BOTH, pairs) for pairs in (PLUS_ONE, MINUS_ONE, PLUS_TWO)]
    theirs = [lax.ppermute(block, "row", OTHER_CORE) for block in mine]
    outgoing = pl.pallas_call(
        product_kernel,
        out_shape=jax.ShapeDtypeStruct((NRG * CAP, BS, BS), jnp.bfloat16),
        in_specs=[smem] * 5 + [pl.BlockSpec(memory_space=pl.ANY)] + [vmem] * 8,
        out_specs=vmem,
        scratch_shapes=[
            pltpu.VMEM((NP + 1, BS, BS), jnp.bfloat16),
            pltpu.SMEM((RB * KB,), jnp.int32),
            pltpu.SMEM((RB * NCB,), jnp.int32),
            pltpu.SMEM((NRG,), jnp.int32),
            pltpu.SemaphoreType.DMA,
        ],
        compiler_params=pltpu.CompilerParams(vmem_limit_bytes=24 * 1024 * 1024),
        name="product",
    )(where, p_positions, h_rows, keep_mask, owner_ids.reshape(RB, NCB), p_blocks, *mine, *theirs)
    outgoing = outgoing.reshape(NRG, CAP, BS, BS)
    return lax.all_to_all(outgoing, "row", split_axis=0, concat_axis=0, tiled=True)


def solution(mesh):
    return jax.shard_map(
        local,
        mesh=mesh,
        in_specs=(
            P(("row", "col"), None, None),
            P(("row", "col")),
            P("col", None, None),
            P(),
            P(("row", "col"), None),
            P(("row", "col"), None, None),
        ),
        out_specs=P(("row", "col"), None, None, None),
        check_vma=False,
    )
```

time: 391 us -> 148 us (0.38)
  waiting for transfers between devices: 183 us -> 7.49 us
  local copies, waits for them, and re-layouts: 82.2 us -> 1.34 us
  blocking collectives: 59.1 us -> 110 us
  starting transfers between devices: 46.5 us -> 16.1 us
  Pallas kernels: 0 us -> 12.3 us
  matrix products: 10.4 us -> 0 us
  other arithmetic: 6.03 us -> 0.59 us
    ppermute x23 -> x7, waiting for transfers between devices: 183 us -> 7.49 us  [the longest x3 5.63 us: local(): lax.ppermute(own, BOTH, pairs)]
    gather x24 -> x0, local copies, waits for them, and re-layouts: 68 us -> none  [panel_term(): columns = jnp.take(dense_panel, inner_rows, axis=0)]
    all_to_all x0 -> x1, blocking collectives: none -> 50.7 us  [local(): own = lax.all_to_all(picked, 'col', split_axis=0, concat_axis=0, tiled=True)]
    ppermute x23 -> x7, starting transfers between devices: 46.5 us -> 16.1 us  [the longest x4 8.14 us: local(): theirs = [lax.ppermute(block, 'row', OTHER_CORE) for block in mine]]
    pallas_call x0 -> x2, Pallas kernels: none -> 12.3 us  [the longest x1 10.4 us: local(): pl.pallas_call(product_kernel, out_shape=jax.ShapeDtypeStruct((NRG * CAP,...]
    dot_general x25 -> x0, matrix products: 10.4 us -> none  [the longest x24 8.92 us: panel_term(): jnp.einsum('nrab,nbc->rac', columns, panel_blocks, preferred_element_type...]
    scatter x1 -> x0, local copies, waits for them, and re-layouts: 6.61 us -> none  [local(): jnp.zeros((KB * RB, block_size, block_size), jnp.bfloat16).at[slot_ids]]
  transfers between devices with their start and end apart: 23 -> 7, of which waited for: 23 -> 3; matrix products, arithmetic and copies ran while one was open for 17% -> 0% of each run, Pallas kernels for 0% -> 0%
where the time goes in v1:
time: 148 us
  blocking collectives  110 us (74%)
  starting transfers between devices  16.1 us (11%)
  Pallas kernels  12.3 us (8%)
  waiting for transfers between devices  7.49 us (5%)
    all_to_all x1, blocking collectives, local(): lax.all_to_all(outgoing, 'row', split_axis=0, concat_axis=0, tiled=True)  59.1 us
    all_to_all x1, blocking collectives, local(): own = lax.all_to_all(picked, 'col', split_axis=0, concat_axis=0, tiled=True)  50.7 us
    pallas_call x1, Pallas kernels, local(): pl.pallas_call(product_kernel, out_shape=jax.ShapeDtypeStruct((NRG * CAP,...  10.4 us
    ppermute x4, starting transfers between devices, local(): theirs = [lax.ppermute(block, 'row', OTHER_CORE) for block in mine]  8.14 us
    ppermute x3, starting transfers between devices, local(): lax.ppermute(own, BOTH, pairs)  7.96 us
    ppermute x3, waiting for transfers between devices, local(): lax.ppermute(own, BOTH, pairs)  5.63 us
  transfers between devices with their start and end apart: 7, of which 3 were waited for; matrix products, arithmetic and copies ran while one was open for 0% of the time, Pallas kernels for 0%

profile of v1, /device:TPU:8, one launch (start us, length us, event | category | flops | bytes accessed | tf_op | source)
XLA Modules:
  0.0 147.8 jit_solution(16934234176534289843)
XLA Ops:
  0.0 0.0 copy-start.4
  0.0 0.0 copy-start.3
  0.0 0.0 copy-start.2
  0.0 0.0 copy-start.5
  0.0 0.0 copy-start
  0.0 0.6 pad_add_fusion.where
  0.6 0.0 copy-start.1
  0.6 1.9 %pick.1 = bf16[24,128,128]{2,1,0:T(8,128)(2,1)} custom-call(s32[2]{0:T(128)} %pad_add_fusion.where, bf16[8,128,128]{2,1,0:T(8,128)(2,1)} %h_ref.1), custom_call_target="tpu_custom_call" | custom-call | tf_op jit(solution)/shard_map/pick/pallas_call | solution.py:116
  2.6 50.7 %all_to_all.10.refs_0_ = bf16[24,128,128]{2,1,0:T(8,128)(2,1)S(1)} all-to-all(bf16[24,128,128]{2,1,0:T(8,128)(2,1)} %pick.1), channel_id=1, replica_groups=mesh['row'=32,'col'=24] {'col'}, dimensions={0} | all-to-all | bytes 1572864 | tf_op jit(solution)/shard_map/all_to_all | solution.py:119
  53.3 2.3 %collective-permute-start.2 = (bf16[24,128,128]{2,1,0:T(8,128)(2,1)S(1)}, bf16[24,128,128]{2,1,0:T(8,128)(2,1)S(1)}, u32[]{:S(2)}, u32[]{:S(2)}) collective-permute-start(bf16[24,128,128]{2,1,0:T(8,128)(2,1)S(1)} %all_to_all.10.refs_0_), channel_id=1, source_target_pairs={{48,0},{360,24},{49,1},{361,25},{50,2},{362,26},{51,3},{363,27},{5... | collective-permute-start | bytes 2359304 | tf_op jit(solution)/shard_map/ppermute | solution.py:120
  55.6 1.9 %collective-permute-start.1 = (bf16[24,128,128]{2,1,0:T(8,128)(2,1)S(1)}, bf16[24,128,128]{2,1,0:T(8,128)(2,1)S(1)}, u32[]{:S(2)}, u32[]{:S(2)}) collective-permute-start(bf16[24,128,128]{2,1,0:T(8,128)(2,1)S(1)} %all_to_all.10.refs_0_), channel_id=1, source_target_pairs={{11,0},{420,24},{0,1},{421,25},{1,2},{422,26},{2,3},{423,27},{3,4}... | collective-permute-start | bytes 2359304 | tf_op jit(solution)/shard_map/ppermute | solution.py:120
  57.6 3.7 %collective-permute-start = (bf16[24,128,128]{2,1,0:T(8,128)(2,1)S(1)}, bf16[24,128,128]{2,1,0:T(8,128)(2,1)S(1)}, u32[]{:S(2)}, u32[]{:S(2)}) collective-permute-start(bf16[24,128,128]{2,1,0:T(8,128)(2,1)S(1)} %all_to_all.10.refs_0_), channel_id=1, source_target_pairs={{384,0},{25,24},{385,1},{26,25},{386,2},{27,26},{387,3},{28,27},{3... | collective-permute-start | bytes 2359304 | tf_op jit(solution)/shard_map/ppermute | solution.py:120
  61.3 1.9 %collective-permute-start.3 = (bf16[24,128,128]{2,1,0:T(8,128)(2,1)S(1)}, bf16[24,128,128]{2,1,0:T(8,128)(2,1)S(1)}, u32[]{:S(2)}, u32[]{:S(2)}) collective-permute-start(bf16[24,128,128]{2,1,0:T(8,128)(2,1)S(1)} %all_to_all.10.refs_0_), channel_id=1, source_target_pairs={{0,24},{24,0},{48,72},{72,48},{96,120},{120,96},{144,168},{168,144... | collective-permute-start | bytes 2359304 | tf_op jit(solution)/shard_map/ppermute | solution.py:121
  63.2 4.0 %collective-permute-done.2.refs_3_ = bf16[24,128,128]{2,1,0:T(8,128)(2,1)S(1)} collective-permute-done((bf16[24,128,128]{2,1,0:T(8,128)(2,1)S(1)}, bf16[24,128,128]{2,1,0:T(8,128)(2,1)S(1)}, u32[]{:S(2)}, u32[]{:S(2)}) %collective-permute-start.2) | collective-permute-done | bytes 786464 | tf_op jit(solution)/shard_map/ppermute | solution.py:120
  67.2 1.9 %collective-permute-start.6 = (bf16[24,128,128]{2,1,0:T(8,128)(2,1)S(1)}, bf16[24,128,128]{2,1,0:T(8,128)(2,1)S(1)}, u32[]{:S(2)}, u32[]{:S(2)}) collective-permute-start(bf16[24,128,128]{2,1,0:T(8,128)(2,1)S(1)} %collective-permute-done.2.refs_3_), channel_id=1, source_target_pairs={{0,24},{24,0},{48,72},{72,48},{96,120},{120,96},{144,168},{168,144... | collective-permute-start | bytes 2359304 | tf_op jit(solution)/shard_map/ppermute | solution.py:121
  69.1 1.7 %collective-permute-done.1.refs_2_ = bf16[24,128,128]{2,1,0:T(8,128)(2,1)S(1)} collective-permute-done((bf16[24,128,128]{2,1,0:T(8,128)(2,1)S(1)}, bf16[24,128,128]{2,1,0:T(8,128)(2,1)S(1)}, u32[]{:S(2)}, u32[]{:S(2)}) %collective-permute-start.1) | collective-permute-done | bytes 786464 | tf_op jit(solution)/shard_map/ppermute | solution.py:120
  70.7 1.9 %collective-permute-start.5 = (bf16[24,128,128]{2,1,0:T(8,128)(2,1)S(1)}, bf16[24,128,128]{2,1,0:T(8,128)(2,1)S(1)}, u32[]{:S(2)}, u32[]{:S(2)}) collective-permute-start(bf16[24,128,128]{2,1,0:T(8,128)(2,1)S(1)} %collective-permute-done.1.refs_2_), channel_id=1, source_target_pairs={{0,24},{24,0},{48,72},{72,48},{96,120},{120,96},{144,168},{168,144... | collective-permute-start | bytes 2359304 | tf_op jit(solution)/shard_map/ppermute | solution.py:121
  72.7 0.0 collective-permute-done.refs_1_
  72.7 2.4 %collective-permute-start.4 = (bf16[24,128,128]{2,1,0:T(8,128)(2,1)S(1)}, bf16[24,128,128]{2,1,0:T(8,128)(2,1)S(1)}, u32[]{:S(2)}, u32[]{:S(2)}) collective-permute-start(bf16[24,128,128]{2,1,0:T(8,128)(2,1)S(1)} %collective-permute-done.refs_1_), channel_id=1, source_target_pairs={{0,24},{24,0},{48,72},{72,48},{96,120},{120,96},{144,168},{168,144... | collective-permute-start | bytes 2359304 | tf_op jit(solution)/shard_map/ppermute | solution.py:121
  75.1 0.0 collective-permute-done.3.refs_4_
  75.1 0.0 collective-permute-done.6.refs_7_
  75.1 0.0 collective-permute-done.5.refs_6_
  75.1 1.9 %collective-permute-done.4.refs_5_ = bf16[24,128,128]{2,1,0:T(8,128)(2,1)S(1)} collective-permute-done((bf16[24,128,128]{2,1,0:T(8,128)(2,1)S(1)}, bf16[24,128,128]{2,1,0:T(8,128)(2,1)S(1)}, u32[]{:S(2)}, u32[]{:S(2)}) %collective-permute-start.4) | collective-permute-done | bytes 786464 | tf_op jit(solution)/shard_map/ppermute | solution.py:121
  77.0 0.0 copy-done.4
  77.0 0.0 copy-done.3
  77.0 0.0 copy-done.2
  77.0 0.0 copy-done.5
  77.0 0.0 copy-done
  77.0 0.0 copy-done.1
  77.0 10.4 %product.1 = bf16[64,128,128]{2,1,0:T(8,128)(2,1)S(1)} custom-call(s32[2]{0:T(128)S(1)} %copy-done.1, s32[48]{0:T(128)S(1)} %copy-done.5, s32[192]{0:T(256)S(1)} %copy-done.2, s32[2,24]{1,0:T(2,128)S(1)} %copy-done.3, s32[2,24]{1,0:T(2,128)S(1)} %bitcast.5, bf16[48,128,128]{2,1,0:T(8,128)(2,1)S(1)} %copy-done, bf16[24,128,128]{2,1,0:T(8,128)(2,1)S(1)} %all_to_all.10.refs_0_, ...), custom_call_target="tpu_custom_call" | custom-call | tf_op jit(solution)/shard_map/product/pallas_call | solution.py:122
  87.4 59.1 %all_to_all.11 = bf16[32,2,128,128]{3,2,1,0:T(8,128)(2,1)S(1)} all-to-all(bf16[32,2,128,128]{3,2,1,0:T(8,128)(2,1)S(1)} %bitcast.4), channel_id=1, replica_groups=mesh['row'=32,'col'=24] {'row'}, dimensions={0} | all-to-all | bytes 4194304 | tf_op jit(solution)/shard_map/all_to_all | solution.py:138
  146.5 1.3 copy.8
Async XLA Ops:
  0.0 77.0 %copy-start.4 = (s32[2,24,1]{1,2,0:T(1,128)S(1)}, s32[2,24,1]{1,2,0:T(1,128)}, u32[]{:S(2)}) copy-start(s32[2,24,1]{1,2,0:T(1,128)} %param.11) | copy-start | bytes 580
  0.0 77.0 %copy-start.3 = (s32[2,24]{1,0:T(2,128)S(1)}, s32[2,24]{1,0:T(2,128)}, u32[]{:S(2)}) copy-start(s32[2,24]{1,0:T(2,128)} %keep.1) | copy-start | bytes 580
  0.0 77.0 %copy-start.2 = (s32[192]{0:T(256)S(1)}, s32[192]{0:T(256)}, u32[]{:S(2)}) copy-start(s32[192]{0:T(256)} %rows.1) | copy-start | bytes 2308
  0.0 77.0 %copy-start.5 = (s32[48]{0:T(128)S(1)}, s32[48]{0:T(128)}, u32[]{:S(2)}) copy-start(s32[48]{0:T(128)} %pos.1) | copy-start | bytes 580
  0.0 77.0 %copy-start = (bf16[48,128,128]{2,1,0:T(8,128)(2,1)S(1)}, bf16[48,128,128]{2,1,0:T(8,128)(2,1)}, u32[]{:S(2)}) copy-start(bf16[48,128,128]{2,1,0:T(8,128)(2,1)} %p_hbm.1) | copy-start | bytes 4718596
  0.6 76.4 %copy-start.1 = (s32[2]{0:T(128)S(1)}, s32[2]{0:T(128)}, u32[]{:S(2)}) copy-start(s32[2]{0:T(128)} %pad_add_fusion.where) | copy-start | bytes 28
  53.3 13.9 %collective-permute-start.2 = (bf16[24,128,128]{2,1,0:T(8,128)(2,1)S(1)}, bf16[24,128,128]{2,1,0:T(8,128)(2,1)S(1)}, u32[]{:S(2)}, u32[]{:S(2)}) collective-permute-start(bf16[24,128,128]{2,1,0:T(8,128)(2,1)S(1)} %all_to_all.10.refs_0_), channel_id=1, source_target_pairs={{48,0},{360,24},{49,1},{361,25},{50,2},{362,26},{51,3},{363,27},{5... | collective-permute-start | bytes 2359304 | tf_op jit(solution)/shard_map/ppermute | solution.py:120
  55.6 15.1 %collective-permute-start.1 = (bf16[24,128,128]{2,1,0:T(8,128)(2,1)S(1)}, bf16[24,128,128]{2,1,0:T(8,128)(2,1)S(1)}, u32[]{:S(2)}, u32[]{:S(2)}) collective-permute-start(bf16[24,128,128]{2,1,0:T(8,128)(2,1)S(1)} %all_to_all.10.refs_0_), channel_id=1, source_target_pairs={{11,0},{420,24},{0,1},{421,25},{1,2},{422,26},{2,3},{423,27},{3,4}... | collective-permute-start | bytes 2359304 | tf_op jit(solution)/shard_map/ppermute | solution.py:120
  57.6 15.1 %collective-permute-start = (bf16[24,128,128]{2,1,0:T(8,128)(2,1)S(1)}, bf16[24,128,128]{2,1,0:T(8,128)(2,1)S(1)}, u32[]{:S(2)}, u32[]{:S(2)}) collective-permute-start(bf16[24,128,128]{2,1,0:T(8,128)(2,1)S(1)} %all_to_all.10.refs_0_), channel_id=1, source_target_pairs={{384,0},{25,24},{385,1},{26,25},{386,2},{27,26},{387,3},{28,27},{3... | collective-permute-start | bytes 2359304 | tf_op jit(solution)/shard_map/ppermute | solution.py:120
  61.3 13.8 %collective-permute-start.3 = (bf16[24,128,128]{2,1,0:T(8,128)(2,1)S(1)}, bf16[24,128,128]{2,1,0:T(8,128)(2,1)S(1)}, u32[]{:S(2)}, u32[]{:S(2)}) collective-permute-start(bf16[24,128,128]{2,1,0:T(8,128)(2,1)S(1)} %all_to_all.10.refs_0_), channel_id=1, source_target_pairs={{0,24},{24,0},{48,72},{72,48},{96,120},{120,96},{144,168},{168,144... | collective-permute-start | bytes 2359304 | tf_op jit(solution)/shard_map/ppermute | solution.py:121
  67.2 7.9 %collective-permute-start.6 = (bf16[24,128,128]{2,1,0:T(8,128)(2,1)S(1)}, bf16[24,128,128]{2,1,0:T(8,128)(2,1)S(1)}, u32[]{:S(2)}, u32[]{:S(2)}) collective-permute-start(bf16[24,128,128]{2,1,0:T(8,128)(2,1)S(1)} %collective-permute-done.2.refs_3_), channel_id=1, source_target_pairs={{0,24},{24,0},{48,72},{72,48},{96,120},{120,96},{144,168},{168,144... | collective-permute-start | bytes 2359304 | tf_op jit(solution)/shard_map/ppermute | solution.py:121
  70.7 4.4 %collective-permute-start.5 = (bf16[24,128,128]{2,1,0:T(8,128)(2,1)S(1)}, bf16[24,128,128]{2,1,0:T(8,128)(2,1)S(1)}, u32[]{:S(2)}, u32[]{:S(2)}) collective-permute-start(bf16[24,128,128]{2,1,0:T(8,128)(2,1)S(1)} %collective-permute-done.1.refs_2_), channel_id=1, source_target_pairs={{0,24},{24,0},{48,72},{72,48},{96,120},{120,96},{144,168},{168,144... | collective-permute-start | bytes 2359304 | tf_op jit(solution)/shard_map/ppermute | solution.py:121
  72.7 4.3 %collective-permute-start.4 = (bf16[24,128,128]{2,1,0:T(8,128)(2,1)S(1)}, bf16[24,128,128]{2,1,0:T(8,128)(2,1)S(1)}, u32[]{:S(2)}, u32[]{:S(2)}) collective-permute-start(bf16[24,128,128]{2,1,0:T(8,128)(2,1)S(1)} %collective-permute-done.refs_1_), channel_id=1, source_target_pairs={{0,24},{24,0},{48,72},{72,48},{96,120},{120,96},{144,168},{168,144... | collective-permute-start | bytes 2359304 | tf_op jit(solution)/shard_map/ppermute | solution.py:121

commit v2 on v1

--- a/solution.py
+++ b/solution.py
@@ -39,17 +39,27 @@
 MINUS_ONE = pull(((0, 0, -1), (-1, 0, 0)))
 PLUS_TWO = pull(((0, 1, 0), (0, -1, 0)))
 OTHER_CORE = [(r, r ^ 1) for r in range(NRG)]
+UP_Z = pull(((-1, 0, 1), (-1, 0, 1)))
+DOWN_Z = pull(((1, 0, -1), (1, 0, -1)))
+STRIDE = 3
+PER = NCB // STRIDE
+THIRDS = [[h * NZ + m + STRIDE * i for h in range(2) for i in range(NZ // STRIDE)] for m in range(STRIDE)]
 
 
 def colour(x, y, z):
     return lax.rem(x + 2 * y + z, 4)
 
 
+def place_of(where):
+    row, col = where[0], where[1]
+    return 2 * (col // NZ) + row // (2 * NY), lax.rem(row // 2, NY), lax.rem(col, NZ), lax.rem(row, 2)
+
+
 def pick_kernel(where, h_ref, out_ref):
-    row = where[0]
-    x_lo, y, core = row // (2 * NY), (row // 2) % NY, row % 2
-    for d in range(NCB):
-        c = colour(2 * (d // NZ) + x_lo, y, d % NZ)
+    x, y, z, core = place_of(where)
+    x, z = lax.rem(x, 2), lax.rem(z, STRIDE)
+    for d in range(PER):
+        c = colour(2 * (d // (PER // 2)) + x, y, z + STRIDE * (d % (PER // 2)))
         out_ref[d] = h_ref[2 * c + core]
 
 
@@ -60,63 +70,61 @@
     p_all[NP] = jnp.zeros((BS, BS), jnp.bfloat16)
     out_ref[...] = jnp.zeros_like(out_ref)
 
-    row, col = where[0], where[1]
-    x, y, z, core = 2 * (col // NZ) + row // (2 * NY), (row // 2) % NY, col % NZ, row % 2
+    x, y, z, core = place_of(where)
     c = colour(x, y, z)
-    listed = []
+    listed, first = [], []
     for k in (core, 1 - core):
-        for step in (0, 1, 3, 2):
+        for step, dz in ((0, 0), (1, k), (3, 2 * (1 - k)), (2, 0)):
             listed.append(2 * lax.rem(c + step, 4) + k)
+            first.append(lax.rem(z + dz, STRIDE))
 
-    def clear(i, carry):
+    for i in range(RB * KB):
         place[i] = NP
-        return carry
-
-    lax.fori_loop(0, RB * KB, clear, 0)
-
-    def note(i, carry):
+    for i in range(NP):
         place[pos[i]] = i
-        return carry
-
-    lax.fori_loop(0, NP, note, 0)
-
-    def reset(i, carry):
+    for i in range(NRG):
         count[i] = 0
-        return carry
-
-    lax.fori_loop(0, NRG, reset, 0)
-
-    def rank(i, carry):
+    for i in range(RB * NCB):
         to = owner[i // NCB, i % NCB]
         used = count[to]
         count[to] = used + 1
         slot[i] = to * CAP + used
-        return carry
-
-    lax.fori_loop(0, RB * NCB, rank, 0)
     load.wait()
 
     def column(j, carry):
+        jz = lax.rem(j, NZ)
+        base = (j // NZ) * (PER // 2) + jz // STRIDE
+        at = [lax.rem(jz + STRIDE - f, STRIDE) * PER + base for f in first]
         inner = [rows[j * NH + n] for n in listed]
-        right = jnp.concatenate([panel[j] for panel in panels], axis=0)
+        right = jnp.concatenate([panel[u] for panel, u in zip(panels, at)], axis=0)
+        left = jnp.concatenate(
+            [
+                jnp.concatenate([p_all[place[i * KB + r]] for r in inner], axis=1)
+                for i in range(RB)
+            ],
+            axis=0,
+        )
+        both = jnp.dot(left, right, preferred_element_type=jnp.float32).astype(jnp.bfloat16)
         for i in range(RB):
-            left = jnp.concatenate([p_all[place[i * KB + r]] for r in inner], axis=1)
-            block = jnp.dot(left, right, preferred_element_type=jnp.float32).astype(jnp.bfloat16)
+            block = both[i * BS : (i + 1) * BS]
             out_ref[slot[i * NCB + j]] = jnp.where(keep[i, j] == 1, block, jnp.zeros_like(block))
         return carry
 
-    lax.fori_loop(0, NCB, column, 0)
+    lax.fori_loop(0, NCB, column, 0, unroll=4)
 
 
 def local(p_blocks, p_positions, h_blocks, h_rows, keep_mask, owner_ids):
     where = jnp.stack([lax.axis_index("row"), lax.axis_index("col")])
     smem = pl.BlockSpec(memory_space=pltpu.SMEM)
     vmem = pl.BlockSpec(memory_space=pltpu.VMEM)
-    panel = jax.ShapeDtypeStruct((NCB, BS, BS), jnp.bfloat16)
+    panel = jax.ShapeDtypeStruct((PER, BS, BS), jnp.bfloat16)
     picked = pl.pallas_call(
         pick_kernel, out_shape=panel, in_specs=[smem, vmem], out_specs=vmem, name="pick"
     )(where, h_blocks)
-    own = lax.all_to_all(picked, "col", split_axis=0, concat_axis=0, tiled=True)
+    third = lax.all_to_all(
+        picked, "col", split_axis=0, concat_axis=0, axis_index_groups=THIRDS, tiled=True
+    )
+    own = jnp.concatenate([third] + [lax.ppermute(third, BOTH, pairs) for pairs in (UP_Z, DOWN_Z)])
     mine = [own] + [lax.ppermute(own, BOTH, pairs) for pairs in (PLUS_ONE, MINUS_ONE, PLUS_TWO)]
     theirs = [lax.ppermute(block, "row", OTHER_CORE) for block in mine]
     outgoing = pl.pallas_call(

time: 148 us -> 143 us (0.966)
  the two profiles are of different devices: /device:TPU:8 before, /device:TPU:12 now
where the time goes in v2:
time: 143 us; the launch traced here: 142 us
  blocking collectives  89.9 us (63%)
  starting transfers between devices  27.6 us (19%)
  waiting for transfers between devices  15 us (10%)
  Pallas kernels  7.35 us (5%)
  local copies, waits for them, and re-layouts  1.43 us (1%)
    all_to_all x1, blocking collectives, local(): lax.all_to_all(outgoing, 'row', split_axis=0, concat_axis=0, tiled=True)  61.8 us
    all_to_all x1, blocking collectives, local(): lax.all_to_all(picked, 'col', split_axis=0, concat_axis=0, axis_index_gro...  28.1 us
    ppermute x2, starting transfers between devices, local(): lax.ppermute(third, BOTH, pairs)  11.6 us
    ppermute x4, starting transfers between devices, local(): theirs = [lax.ppermute(block, 'row', OTHER_CORE) for block in mine]  8.95 us
    ppermute x2, waiting for transfers between devices, local(): lax.ppermute(third, BOTH, pairs)  7.32 us
    ppermute x3, starting transfers between devices, local(): lax.ppermute(own, BOTH, pairs)  7.02 us
    ppermute x3, waiting for transfers between devices, local(): lax.ppermute(own, BOTH, pairs)  5.78 us
    pallas_call x1, Pallas kernels, local(): pl.pallas_call(product_kernel, out_shape=jax.ShapeDtypeStruct((NRG * CAP,...  5.64 us
  transfers between devices with their start and end apart: 9, of which 5 were waited for; matrix products, arithmetic and copies ran while one was open for 0% of the time, Pallas kernels for 0%

profile of v2, /device:TPU:12, one launch (start us, length us, event | category | flops | bytes accessed | tf_op | source)
XLA Modules:
  0.0 142.0 jit_solution(15332192566386406465)
XLA Ops:
  0.0 0.0 copy-start.4
  0.0 0.0 copy-start.3
  0.0 0.0 copy-start.2
  0.0 0.0 copy-start.5
  0.0 0.0 copy-start
  0.0 0.6 pad_add_fusion.where
  0.7 0.0 copy-start.1
  0.7 1.7 %pick.1 = bf16[8,128,128]{2,1,0:T(8,128)(2,1)} custom-call(s32[2]{0:T(128)} %pad_add_fusion.where, bf16[8,128,128]{2,1,0:T(8,128)(2,1)} %h_ref.1), custom_call_target="tpu_custom_call" | custom-call | tf_op jit(solution)/shard_map/pick/pallas_call | solution.py:121
  2.4 28.1 %all_to_all.10 = bf16[8,128,128]{2,1,0:T(8,128)(2,1)S(1)} all-to-all(bf16[8,128,128]{2,1,0:T(8,128)(2,1)} %pick.1), channel_id=1, replica_groups={{0,3,6,9,12,15,18,21},{1,4,7,10,13,16,19,22},{2,5,8,11,14,17,20,23},{24..., dimensions={0} | all-to-all | bytes 524288 | tf_op jit(solution)/shard_map/all_to_all | solution.py:124
  30.5 8.0 %collective-permute-start = (bf16[8,128,128]{2,1,0:T(8,128)(2,1)S(1)}, bf16[8,128,128]{2,1,0:T(8,128)(2,1)S(1)}, u32[]{:S(2)}, u32[]{:S(2)}) collective-permute-start(bf16[8,128,128]{2,1,0:T(8,128)(2,1)S(1)} %all_to_all.10), channel_id=1, source_target_pairs={{397,0},{421,24},{398,1},{422,25},{399,2},{423,26},{400,3},{424,27... | collective-permute-start | bytes 786440 | tf_op jit(solution)/shard_map/ppermute | solution.py:127
  38.6 3.6 %collective-permute-start.1 = (bf16[8,128,128]{2,1,0:T(8,128)(2,1)S(1)}, bf16[8,128,128]{2,1,0:T(8,128)(2,1)S(1)}, u32[]{:S(2)}, u32[]{:S(2)}) collective-permute-start(bf16[8,128,128]{2,1,0:T(8,128)(2,1)S(1)} %all_to_all.10), channel_id=1, source_target_pairs={{395,0},{419,24},{384,1},{408,25},{385,2},{409,26},{386,3},{410,27... | collective-permute-start | bytes 786440 | tf_op jit(solution)/shard_map/ppermute | solution.py:127
  42.2 2.4 %collective-permute-done = bf16[8,128,128]{2,1,0:T(8,128)(2,1)S(1)} collective-permute-done((bf16[8,128,128]{2,1,0:T(8,128)(2,1)S(1)}, bf16[8,128,128]{2,1,0:T(8,128)(2,1)S(1)}, u32[]{:S(2)}, u32[]{:S(2)}) %collective-permute-start) | collective-permute-done | bytes 262176 | tf_op jit(solution)/shard_map/ppermute | solution.py:127
  44.6 4.9 %collective-permute-done.1 = bf16[8,128,128]{2,1,0:T(8,128)(2,1)S(1)} collective-permute-done((bf16[8,128,128]{2,1,0:T(8,128)(2,1)S(1)}, bf16[8,128,128]{2,1,0:T(8,128)(2,1)S(1)}, u32[]{:S(2)}, u32[]{:S(2)}) %collective-permute-start.1) | collective-permute-done | bytes 262176 | tf_op jit(solution)/shard_map/ppermute | solution.py:127
  49.6 2.4 %collective-permute-start.4 = (bf16[24,128,128]{2,1,0:T(8,128)(2,1)S(1)}, bf16[24,128,128]{2,1,0:T(8,128)(2,1)S(1)}, u32[]{:S(2)}, u32[]{:S(2)}) collective-permute-start(bf16[24,128,128]{2,1,0:T(8,128)(2,1)S(1)} %constant_dynamic-update-slice_fusion.refs_0_), channel_id=1, source_target_pairs={{48,0},{360,24},{49,1},{361,25},{50,2},{362,26},{51,3},{363,27},{5... | collective-permute-start | bytes 2359304 | tf_op jit(solution)/shard_map/ppermute | solution.py:128
  51.9 1.9 %collective-permute-start.3 = (bf16[24,128,128]{2,1,0:T(8,128)(2,1)S(1)}, bf16[24,128,128]{2,1,0:T(8,128)(2,1)S(1)}, u32[]{:S(2)}, u32[]{:S(2)}) collective-permute-start(bf16[24,128,128]{2,1,0:T(8,128)(2,1)S(1)} %constant_dynamic-update-slice_fusion.refs_0_), channel_id=1, source_target_pairs={{11,0},{420,24},{0,1},{421,25},{1,2},{422,26},{2,3},{423,27},{3,4}... | collective-permute-start | bytes 2359304 | tf_op jit(solution)/shard_map/ppermute | solution.py:128
  53.9 2.7 %collective-permute-start.2 = (bf16[24,128,128]{2,1,0:T(8,128)(2,1)S(1)}, bf16[24,128,128]{2,1,0:T(8,128)(2,1)S(1)}, u32[]{:S(2)}, u32[]{:S(2)}) collective-permute-start(bf16[24,128,128]{2,1,0:T(8,128)(2,1)S(1)} %constant_dynamic-update-slice_fusion.refs_0_), channel_id=1, source_target_pairs={{384,0},{25,24},{385,1},{26,25},{386,2},{27,26},{387,3},{28,27},{3... | collective-permute-start | bytes 2359304 | tf_op jit(solution)/shard_map/ppermute | solution.py:128
  56.6 2.7 %collective-permute-start.5 = (bf16[24,128,128]{2,1,0:T(8,128)(2,1)S(1)}, bf16[24,128,128]{2,1,0:T(8,128)(2,1)S(1)}, u32[]{:S(2)}, u32[]{:S(2)}) collective-permute-start(bf16[24,128,128]{2,1,0:T(8,128)(2,1)S(1)} %constant_dynamic-update-slice_fusion.refs_0_), channel_id=1, source_target_pairs={{0,24},{24,0},{48,72},{72,48},{96,120},{120,96},{144,168},{168,144... | collective-permute-start | bytes 2359304 | tf_op jit(solution)/shard_map/ppermute | solution.py:129
  59.3 4.1 %collective-permute-done.4.refs_3_ = bf16[24,128,128]{2,1,0:T(8,128)(2,1)S(1)} collective-permute-done((bf16[24,128,128]{2,1,0:T(8,128)(2,1)S(1)}, bf16[24,128,128]{2,1,0:T(8,128)(2,1)S(1)}, u32[]{:S(2)}, u32[]{:S(2)}) %collective-permute-start.4) | collective-permute-done | bytes 786464 | tf_op jit(solution)/shard_map/ppermute | solution.py:128
  63.5 1.9 %collective-permute-start.8 = (bf16[24,128,128]{2,1,0:T(8,128)(2,1)S(1)}, bf16[24,128,128]{2,1,0:T(8,128)(2,1)S(1)}, u32[]{:S(2)}, u32[]{:S(2)}) collective-permute-start(bf16[24,128,128]{2,1,0:T(8,128)(2,1)S(1)} %collective-permute-done.4.refs_3_), channel_id=1, source_target_pairs={{0,24},{24,0},{48,72},{72,48},{96,120},{120,96},{144,168},{168,144... | collective-permute-start | bytes 2359304 | tf_op jit(solution)/shard_map/ppermute | solution.py:129
  65.4 1.7 %collective-permute-done.3.refs_2_ = bf16[24,128,128]{2,1,0:T(8,128)(2,1)S(1)} collective-permute-done((bf16[24,128,128]{2,1,0:T(8,128)(2,1)S(1)}, bf16[24,128,128]{2,1,0:T(8,128)(2,1)S(1)}, u32[]{:S(2)}, u32[]{:S(2)}) %collective-permute-start.3) | collective-permute-done | bytes 786464 | tf_op jit(solution)/shard_map/ppermute | solution.py:128
  67.0 1.9 %collective-permute-start.7 = (bf16[24,128,128]{2,1,0:T(8,128)(2,1)S(1)}, bf16[24,128,128]{2,1,0:T(8,128)(2,1)S(1)}, u32[]{:S(2)}, u32[]{:S(2)}) collective-permute-start(bf16[24,128,128]{2,1,0:T(8,128)(2,1)S(1)} %collective-permute-done.3.refs_2_), channel_id=1, source_target_pairs={{0,24},{24,0},{48,72},{72,48},{96,120},{120,96},{144,168},{168,144... | collective-permute-start | bytes 2359304 | tf_op jit(solution)/shard_map/ppermute | solution.py:129
  69.0 0.0 collective-permute-done.2.refs_1_
  69.0 2.4 %collective-permute-start.6 = (bf16[24,128,128]{2,1,0:T(8,128)(2,1)S(1)}, bf16[24,128,128]{2,1,0:T(8,128)(2,1)S(1)}, u32[]{:S(2)}, u32[]{:S(2)}) collective-permute-start(bf16[24,128,128]{2,1,0:T(8,128)(2,1)S(1)} %collective-permute-done.2.refs_1_), channel_id=1, source_target_pairs={{0,24},{24,0},{48,72},{72,48},{96,120},{120,96},{144,168},{168,144... | collective-permute-start | bytes 2359304 | tf_op jit(solution)/shard_map/ppermute | solution.py:129
  71.4 0.0 collective-permute-done.5.refs_4_
  71.4 0.0 collective-permute-done.8.refs_7_
  71.4 0.0 collective-permute-done.7.refs_6_
  71.4 1.9 %collective-permute-done.6.refs_5_ = bf16[24,128,128]{2,1,0:T(8,128)(2,1)S(1)} collective-permute-done((bf16[24,128,128]{2,1,0:T(8,128)(2,1)S(1)}, bf16[24,128,128]{2,1,0:T(8,128)(2,1)S(1)}, u32[]{:S(2)}, u32[]{:S(2)}) %collective-permute-start.6) | collective-permute-done | bytes 786464 | tf_op jit(solution)/shard_map/ppermute | solution.py:129
  73.3 0.0 copy-done.4
  73.3 0.0 copy-done.3
  73.3 0.0 copy-done.2
  73.3 0.0 copy-done.5
  73.3 0.0 copy-done
  73.3 0.0 copy-done.1
  73.3 5.6 %product.1 = bf16[64,128,128]{2,1,0:T(8,128)(2,1)S(1)} custom-call(s32[2]{0:T(128)S(1)} %copy-done.1, s32[48]{0:T(128)S(1)} %copy-done.5, s32[192]{0:T(256)S(1)} %copy-done.2, s32[2,24]{1,0:T(2,128)S(1)} %copy-done.3, s32[2,24]{1,0:T(2,128)S(1)} %bitcast.5, bf16[48,128,128]{2,1,0:T(8,128)(2,1)S(1)} %copy-done, ...), custom_call_target="tpu_custom_call" | custom-call | tf_op jit(solution)/shard_map/product/pallas_call | solution.py:130
  79.0 61.8 %all_to_all.11 = bf16[32,2,128,128]{3,2,1,0:T(8,128)(2,1)S(1)} all-to-all(bf16[32,2,128,128]{3,2,1,0:T(8,128)(2,1)S(1)} %bitcast.4), channel_id=1, replica_groups=mesh['row'=32,'col'=24] {'row'}, dimensions={0} | all-to-all | bytes 4194304 | tf_op jit(solution)/shard_map/all_to_all | solution.py:146
  140.7 1.3 copy.10
  (3 shorter events, 0.1 us)
Async XLA Ops:
  0.0 73.3 %copy-start.4 = (s32[2,24,1]{1,2,0:T(1,128)S(1)}, s32[2,24,1]{1,2,0:T(1,128)}, u32[]{:S(2)}) copy-start(s32[2,24,1]{1,2,0:T(1,128)} %param.11) | copy-start | bytes 580
  0.0 73.3 %copy-start.3 = (s32[2,24]{1,0:T(2,128)S(1)}, s32[2,24]{1,0:T(2,128)}, u32[]{:S(2)}) copy-start(s32[2,24]{1,0:T(2,128)} %keep.1) | copy-start | bytes 580
  0.0 73.3 %copy-start.2 = (s32[192]{0:T(256)S(1)}, s32[192]{0:T(256)}, u32[]{:S(2)}) copy-start(s32[192]{0:T(256)} %rows.1) | copy-start | bytes 2308
  0.0 73.3 %copy-start.5 = (s32[48]{0:T(128)S(1)}, s32[48]{0:T(128)}, u32[]{:S(2)}) copy-start(s32[48]{0:T(128)} %pos.1) | copy-start | bytes 580
  0.0 73.3 %copy-start = (bf16[48,128,128]{2,1,0:T(8,128)(2,1)S(1)}, bf16[48,128,128]{2,1,0:T(8,128)(2,1)}, u32[]{:S(2)}) copy-start(bf16[48,128,128]{2,1,0:T(8,128)(2,1)} %p_hbm.1) | copy-start | bytes 4718596
  0.7 72.6 %copy-start.1 = (s32[2]{0:T(128)S(1)}, s32[2]{0:T(128)}, u32[]{:S(2)}) copy-start(s32[2]{0:T(128)} %pad_add_fusion.where) | copy-start | bytes 28
  30.5 14.0 %collective-permute-start = (bf16[8,128,128]{2,1,0:T(8,128)(2,1)S(1)}, bf16[8,128,128]{2,1,0:T(8,128)(2,1)S(1)}, u32[]{:S(2)}, u32[]{:S(2)}) collective-permute-start(bf16[8,128,128]{2,1,0:T(8,128)(2,1)S(1)} %all_to_all.10), channel_id=1, source_target_pairs={{397,0},{421,24},{398,1},{422,25},{399,2},{423,26},{400,3},{424,27... | collective-permute-start | bytes 786440 | tf_op jit(solution)/shard_map/ppermute | solution.py:127
  38.6 11.0 %collective-permute-start.1 = (bf16[8,128,128]{2,1,0:T(8,128)(2,1)S(1)}, bf16[8,128,128]{2,1,0:T(8,128)(2,1)S(1)}, u32[]{:S(2)}, u32[]{:S(2)}) collective-permute-start(bf16[8,128,128]{2,1,0:T(8,128)(2,1)S(1)} %all_to_all.10), channel_id=1, source_target_pairs={{395,0},{419,24},{384,1},{408,25},{385,2},{409,26},{386,3},{410,27... | collective-permute-start | bytes 786440 | tf_op jit(solution)/shard_map/ppermute | solution.py:127
  49.6 13.9 %collective-permute-start.4 = (bf16[24,128,128]{2,1,0:T(8,128)(2,1)S(1)}, bf16[24,128,128]{2,1,0:T(8,128)(2,1)S(1)}, u32[]{:S(2)}, u32[]{:S(2)}) collective-permute-start(bf16[24,128,128]{2,1,0:T(8,128)(2,1)S(1)} %constant_dynamic-update-slice_fusion.refs_0_), channel_id=1, source_target_pairs={{48,0},{360,24},{49,1},{361,25},{50,2},{362,26},{51,3},{363,27},{5... | collective-permute-start | bytes 2359304 | tf_op jit(solution)/shard_map/ppermute | solution.py:128
  51.9 15.1 %collective-permute-start.3 = (bf16[24,128,128]{2,1,0:T(8,128)(2,1)S(1)}, bf16[24,128,128]{2,1,0:T(8,128)(2,1)S(1)}, u32[]{:S(2)}, u32[]{:S(2)}) collective-permute-start(bf16[24,128,128]{2,1,0:T(8,128)(2,1)S(1)} %constant_dynamic-update-slice_fusion.refs_0_), channel_id=1, source_target_pairs={{11,0},{420,24},{0,1},{421,25},{1,2},{422,26},{2,3},{423,27},{3,4}... | collective-permute-start | bytes 2359304 | tf_op jit(solution)/shard_map/ppermute | solution.py:128
  53.9 15.1 %collective-permute-start.2 = (bf16[24,128,128]{2,1,0:T(8,128)(2,1)S(1)}, bf16[24,128,128]{2,1,0:T(8,128)(2,1)S(1)}, u32[]{:S(2)}, u32[]{:S(2)}) collective-permute-start(bf16[24,128,128]{2,1,0:T(8,128)(2,1)S(1)} %constant_dynamic-update-slice_fusion.refs_0_), channel_id=1, source_target_pairs={{384,0},{25,24},{385,1},{26,25},{386,2},{27,26},{387,3},{28,27},{3... | collective-permute-start | bytes 2359304 | tf_op jit(solution)/shard_map/ppermute | solution.py:128
  56.6 14.8 %collective-permute-start.5 = (bf16[24,128,128]{2,1,0:T(8,128)(2,1)S(1)}, bf16[24,128,128]{2,1,0:T(8,128)(2,1)S(1)}, u32[]{:S(2)}, u32[]{:S(2)}) collective-permute-start(bf16[24,128,128]{2,1,0:T(8,128)(2,1)S(1)} %constant_dynamic-update-slice_fusion.refs_0_), channel_id=1, source_target_pairs={{0,24},{24,0},{48,72},{72,48},{96,120},{120,96},{144,168},{168,144... | collective-permute-start | bytes 2359304 | tf_op jit(solution)/shard_map/ppermute | solution.py:129
  63.5 7.9 %collective-permute-start.8 = (bf16[24,128,128]{2,1,0:T(8,128)(2,1)S(1)}, bf16[24,128,128]{2,1,0:T(8,128)(2,1)S(1)}, u32[]{:S(2)}, u32[]{:S(2)}) collective-permute-start(bf16[24,128,128]{2,1,0:T(8,128)(2,1)S(1)} %collective-permute-done.4.refs_3_), channel_id=1, source_target_pairs={{0,24},{24,0},{48,72},{72,48},{96,120},{120,96},{144,168},{168,144... | collective-permute-start | bytes 2359304 | tf_op jit(solution)/shard_map/ppermute | solution.py:129
  67.0 4.4 %collective-permute-start.7 = (bf16[24,128,128]{2,1,0:T(8,128)(2,1)S(1)}, bf16[24,128,128]{2,1,0:T(8,128)(2,1)S(1)}, u32[]{:S(2)}, u32[]{:S(2)}) collective-permute-start(bf16[24,128,128]{2,1,0:T(8,128)(2,1)S(1)} %collective-permute-done.3.refs_2_), channel_id=1, source_target_pairs={{0,24},{24,0},{48,72},{72,48},{96,120},{120,96},{144,168},{168,144... | collective-permute-start | bytes 2359304 | tf_op jit(solution)/shard_map/ppermute | solution.py:129
  69.0 4.3 %collective-permute-start.6 = (bf16[24,128,128]{2,1,0:T(8,128)(2,1)S(1)}, bf16[24,128,128]{2,1,0:T(8,128)(2,1)S(1)}, u32[]{:S(2)}, u32[]{:S(2)}) collective-permute-start(bf16[24,128,128]{2,1,0:T(8,128)(2,1)S(1)} %collective-permute-done.2.refs_1_), channel_id=1, source_target_pairs={{0,24},{24,0},{48,72},{72,48},{96,120},{120,96},{144,168},{168,144... | collective-permute-start | bytes 2359304 | tf_op jit(solution)/shard_map/ppermute | solution.py:129

commit v3 on v2

--- a/solution.py
+++ b/solution.py
@@ -39,11 +39,13 @@
 MINUS_ONE = pull(((0, 0, -1), (-1, 0, 0)))
 PLUS_TWO = pull(((0, 1, 0), (0, -1, 0)))
 OTHER_CORE = [(r, r ^ 1) for r in range(NRG)]
-UP_Z = pull(((-1, 0, 1), (-1, 0, 1)))
-DOWN_Z = pull(((1, 0, -1), (1, 0, -1)))
-STRIDE = 3
+NEXT_Z = pull(((-1, 0, 1), (1, 0, -1)))
+STRIDE = 2
 PER = NCB // STRIDE
-THIRDS = [[h * NZ + m + STRIDE * i for h in range(2) for i in range(NZ // STRIDE)] for m in range(STRIDE)]
+HALVES = [
+    [h * NZ + m + STRIDE * i for p in range(2) for h in range(2) for i in range(p ^ h, NZ // STRIDE, 2)]
+    for m in range(STRIDE)
+]
 
 
 def colour(x, y, z):
@@ -55,12 +57,12 @@
     return 2 * (col // NZ) + row // (2 * NY), lax.rem(row // 2, NY), lax.rem(col, NZ), lax.rem(row, 2)
 
 
-def pick_kernel(where, h_ref, out_ref):
-    x, y, z, core = place_of(where)
-    x, z = lax.rem(x, 2), lax.rem(z, STRIDE)
-    for d in range(PER):
-        c = colour(2 * (d // (PER // 2)) + x, y, z + STRIDE * (d % (PER // 2)))
-        out_ref[d] = h_ref[2 * c + core]
+def pick(row, col, h_blocks):
+    c = (row >> 4) + (row & 14) + (col & 1)
+    first, second = (
+        lax.dynamic_index_in_dim(h_blocks, 2 * (k & 3) + (row & 1), axis=0) for k in (c, c + 2)
+    )
+    return jnp.where(jnp.arange(PER)[:, None, None] < PER // 2, first, second)
 
 
 def product_kernel(where, pos, rows, keep, owner, p_hbm, *refs):
@@ -74,7 +76,7 @@
     c = colour(x, y, z)
     listed, first = [], []
     for k in (core, 1 - core):
-        for step, dz in ((0, 0), (1, k), (3, 2 * (1 - k)), (2, 0)):
+        for step, dz in ((0, 0), (1, k), (3, 1 - k), (2, 0)):
             listed.append(2 * lax.rem(c + step, 4) + k)
             first.append(lax.rem(z + dz, STRIDE))
 
@@ -93,7 +95,8 @@
 
     def column(j, carry):
         jz = lax.rem(j, NZ)
-        base = (j // NZ) * (PER // 2) + jz // STRIDE
+        h, i = j // NZ, jz // STRIDE
+        base = lax.rem(h + i, 2) * (PER // 2) + h * (PER // 4) + i // 2
         at = [lax.rem(jz + STRIDE - f, STRIDE) * PER + base for f in first]
         inner = [rows[j * NH + n] for n in listed]
         right = jnp.concatenate([panel[u] for panel, u in zip(panels, at)], axis=0)
@@ -110,21 +113,22 @@
             out_ref[slot[i * NCB + j]] = jnp.where(keep[i, j] == 1, block, jnp.zeros_like(block))
         return carry
 
-    lax.fori_loop(0, NCB, column, 0, unroll=4)
+    lax.fori_loop(0, NCB, column, 0, unroll=12)
 
 
 def local(p_blocks, p_positions, h_blocks, h_rows, keep_mask, owner_ids):
-    where = jnp.stack([lax.axis_index("row"), lax.axis_index("col")])
+    row, col = lax.axis_index("row"), lax.axis_index("col")
     smem = pl.BlockSpec(memory_space=pltpu.SMEM)
     vmem = pl.BlockSpec(memory_space=pltpu.VMEM)
-    panel = jax.ShapeDtypeStruct((PER, BS, BS), jnp.bfloat16)
-    picked = pl.pallas_call(
-        pick_kernel, out_shape=panel, in_specs=[smem, vmem], out_specs=vmem, name="pick"
-    )(where, h_blocks)
-    third = lax.all_to_all(
-        picked, "col", split_axis=0, concat_axis=0, axis_index_groups=THIRDS, tiled=True
+    half = lax.all_to_all(
+        pick(row, col, h_blocks),
+        "col",
+        split_axis=0,
+        concat_axis=0,
+        axis_index_groups=HALVES,
+        tiled=True,
     )
-    own = jnp.concatenate([third] + [lax.ppermute(third, BOTH, pairs) for pairs in (UP_Z, DOWN_Z)])
+    own = jnp.concatenate([half, lax.ppermute(half, BOTH, NEXT_Z)])
     mine = [own] + [lax.ppermute(own, BOTH, pairs) for pairs in (PLUS_ONE, MINUS_ONE, PLUS_TWO)]
     theirs = [lax.ppermute(block, "row", OTHER_CORE) for block in mine]
     outgoing = pl.pallas_call(
@@ -141,7 +145,7 @@
         ],
         compiler_params=pltpu.CompilerParams(vmem_limit_bytes=24 * 1024 * 1024),
         name="product",
-    )(where, p_positions, h_rows, keep_mask, owner_ids.reshape(RB, NCB), p_blocks, *mine, *theirs)
+    )(jnp.stack([row, col]), p_positions, h_rows, keep_mask, owner_ids.reshape(RB, NCB), p_blocks, *mine, *theirs)
     outgoing = outgoing.reshape(NRG, CAP, BS, BS)
     return lax.all_to_all(outgoing, "row", split_axis=0, concat_axis=0, tiled=True)
 

time: 143 us -> 142 us (level)
  the two profiles are of different devices: /device:TPU:12 before, /device:TPU:8 now
where the time goes in v3:
time: 142 us; the launch traced here: 141 us
  blocking collectives  97.2 us (68%)
  starting transfers between devices  21.1 us (15%)
  waiting for transfers between devices  15.2 us (11%)
  Pallas kernels  4.99 us (4%)
  local copies, waits for them, and re-layouts  2.32 us (2%)
    all_to_all x1, blocking collectives, local(): lax.all_to_all(outgoing, 'row', split_axis=0, concat_axis=0, tiled=True)  59.1 us
    all_to_all x1, blocking collectives, local(): lax.all_to_all(pick(row, col, h_blocks), 'col', split_axis=0, concat_axis...  38.1 us
    ppermute x4, starting transfers between devices, local(): theirs = [lax.ppermute(block, 'row', OTHER_CORE) for block in mine]  8.27 us
    ppermute x3, starting transfers between devices, local(): lax.ppermute(own, BOTH, pairs)  7.88 us
    ppermute x1, waiting for transfers between devices, local(): own = jnp.concatenate([half, lax.ppermute(half, BOTH, NEXT_Z)])  6.78 us
    ppermute x3, waiting for transfers between devices, local(): lax.ppermute(own, BOTH, pairs)  6.59 us
    pallas_call x1, Pallas kernels, local(): pl.pallas_call(product_kernel, out_shape=jax.ShapeDtypeStruct((NRG * CAP,...  4.99 us
    ppermute x1, starting transfers between devices, local(): own = jnp.concatenate([half, lax.ppermute(half, BOTH, NEXT_Z)])  4.94 us
  transfers between devices with their start and end apart: 8, of which 4 were waited for; matrix products, arithmetic and copies ran while one was open for 0% of the time, Pallas kernels for 0%

profile of v3, /device:TPU:8, one launch (start us, length us, event | category | flops | bytes accessed | tf_op | source)
XLA Modules:
  0.0 141.1 jit_solution(814800159201495000)
XLA Ops:
  0.0 0.0 copy-start.3
  0.0 0.0 copy-start.2
  0.0 0.0 copy-start.1
  0.0 0.0 copy-start.4
  0.0 0.0 copy-start
  0.1 0.9 dynamic-slice_bitcast_fusion.1
  1.0 0.1 broadcast_select_fusion
  1.1 38.1 %all_to_all.10 = bf16[12,128,128]{2,1,0:T(8,128)(2,1)S(1)} all-to-all(bf16[12,128,128]{2,1,0:T(8,128)(2,1)S(1)} %broadcast_select_fusion), channel_id=1, replica_groups={{0,4,8,14,18,22,2,6,10,12,16,20},{1,5,9,15,19,23,3,7,11,13,17,21},{24,2..., dimensions={0} | all-to-all | bytes 786432 | tf_op jit(solution)/shard_map/all_to_all | solution.py:123
  39.1 4.9 %collective-permute-start = (bf16[12,128,128]{2,1,0:T(8,128)(2,1)S(1)}, bf16[12,128,128]{2,1,0:T(8,128)(2,1)S(1)}, u32[]{:S(2)}, u32[]{:S(2)}) collective-permute-start(bf16[12,128,128]{2,1,0:T(8,128)(2,1)S(1)} %all_to_all.10), channel_id=1, source_target_pairs={{397,0},{419,24},{398,1},{408,25},{399,2},{409,26},{400,3},{410,27... | collective-permute-start | bytes 1179656 | tf_op jit(solution)/shard_map/ppermute | solution.py:131
  44.1 6.8 %collective-permute-done = bf16[12,128,128]{2,1,0:T(8,128)(2,1)S(1)} collective-permute-done((bf16[12,128,128]{2,1,0:T(8,128)(2,1)S(1)}, bf16[12,128,128]{2,1,0:T(8,128)(2,1)S(1)}, u32[]{:S(2)}, u32[]{:S(2)}) %collective-permute-start) | collective-permute-done | bytes 393248 | tf_op jit(solution)/shard_map/ppermute | solution.py:131
  50.9 0.1 constant_dynamic-update-slice_fusion.refs_0_
  51.0 2.4 %collective-permute-start.3 = (bf16[24,128,128]{2,1,0:T(8,128)(2,1)S(1)}, bf16[24,128,128]{2,1,0:T(8,128)(2,1)S(1)}, u32[]{:S(2)}, u32[]{:S(2)}) collective-permute-start(bf16[24,128,128]{2,1,0:T(8,128)(2,1)S(1)} %constant_dynamic-update-slice_fusion.refs_0_), channel_id=1, source_target_pairs={{48,0},{360,24},{49,1},{361,25},{50,2},{362,26},{51,3},{363,27},{5... | collective-permute-start | bytes 2359304 | tf_op jit(solution)/shard_map/ppermute | solution.py:132
  53.3 2.1 %collective-permute-start.2 = (bf16[24,128,128]{2,1,0:T(8,128)(2,1)S(1)}, bf16[24,128,128]{2,1,0:T(8,128)(2,1)S(1)}, u32[]{:S(2)}, u32[]{:S(2)}) collective-permute-start(bf16[24,128,128]{2,1,0:T(8,128)(2,1)S(1)} %constant_dynamic-update-slice_fusion.refs_0_), channel_id=1, source_target_pairs={{11,0},{420,24},{0,1},{421,25},{1,2},{422,26},{2,3},{423,27},{3,4}... | collective-permute-start | bytes 2359304 | tf_op jit(solution)/shard_map/ppermute | solution.py:132
  55.4 3.4 %collective-permute-start.1 = (bf16[24,128,128]{2,1,0:T(8,128)(2,1)S(1)}, bf16[24,128,128]{2,1,0:T(8,128)(2,1)S(1)}, u32[]{:S(2)}, u32[]{:S(2)}) collective-permute-start(bf16[24,128,128]{2,1,0:T(8,128)(2,1)S(1)} %constant_dynamic-update-slice_fusion.refs_0_), channel_id=1, source_target_pairs={{384,0},{25,24},{385,1},{26,25},{386,2},{27,26},{387,3},{28,27},{3... | collective-permute-start | bytes 2359304 | tf_op jit(solution)/shard_map/ppermute | solution.py:132
  58.9 2.0 %collective-permute-start.4 = (bf16[24,128,128]{2,1,0:T(8,128)(2,1)S(1)}, bf16[24,128,128]{2,1,0:T(8,128)(2,1)S(1)}, u32[]{:S(2)}, u32[]{:S(2)}) collective-permute-start(bf16[24,128,128]{2,1,0:T(8,128)(2,1)S(1)} %constant_dynamic-update-slice_fusion.refs_0_), channel_id=1, source_target_pairs={{0,24},{24,0},{48,72},{72,48},{96,120},{120,96},{144,168},{168,144... | collective-permute-start | bytes 2359304 | tf_op jit(solution)/shard_map/ppermute | solution.py:133
  60.9 3.9 %collective-permute-done.3.refs_3_ = bf16[24,128,128]{2,1,0:T(8,128)(2,1)S(1)} collective-permute-done((bf16[24,128,128]{2,1,0:T(8,128)(2,1)S(1)}, bf16[24,128,128]{2,1,0:T(8,128)(2,1)S(1)}, u32[]{:S(2)}, u32[]{:S(2)}) %collective-permute-start.3) | collective-permute-done | bytes 786464 | tf_op jit(solution)/shard_map/ppermute | solution.py:132
  64.9 1.9 %collective-permute-start.7 = (bf16[24,128,128]{2,1,0:T(8,128)(2,1)S(1)}, bf16[24,128,128]{2,1,0:T(8,128)(2,1)S(1)}, u32[]{:S(2)}, u32[]{:S(2)}) collective-permute-start(bf16[24,128,128]{2,1,0:T(8,128)(2,1)S(1)} %collective-permute-done.3.refs_3_), channel_id=1, source_target_pairs={{0,24},{24,0},{48,72},{72,48},{96,120},{120,96},{144,168},{168,144... | collective-permute-start | bytes 2359304 | tf_op jit(solution)/shard_map/ppermute | solution.py:133
  66.8 2.7 %collective-permute-done.2.refs_2_ = bf16[24,128,128]{2,1,0:T(8,128)(2,1)S(1)} collective-permute-done((bf16[24,128,128]{2,1,0:T(8,128)(2,1)S(1)}, bf16[24,128,128]{2,1,0:T(8,128)(2,1)S(1)}, u32[]{:S(2)}, u32[]{:S(2)}) %collective-permute-start.2) | collective-permute-done | bytes 786464 | tf_op jit(solution)/shard_map/ppermute | solution.py:132
  69.4 1.9 %collective-permute-start.6 = (bf16[24,128,128]{2,1,0:T(8,128)(2,1)S(1)}, bf16[24,128,128]{2,1,0:T(8,128)(2,1)S(1)}, u32[]{:S(2)}, u32[]{:S(2)}) collective-permute-start(bf16[24,128,128]{2,1,0:T(8,128)(2,1)S(1)} %collective-permute-done.2.refs_2_), channel_id=1, source_target_pairs={{0,24},{24,0},{48,72},{72,48},{96,120},{120,96},{144,168},{168,144... | collective-permute-start | bytes 2359304 | tf_op jit(solution)/shard_map/ppermute | solution.py:133
  71.3 0.0 collective-permute-done.1.refs_1_
  71.4 2.4 %collective-permute-start.5 = (bf16[24,128,128]{2,1,0:T(8,128)(2,1)S(1)}, bf16[24,128,128]{2,1,0:T(8,128)(2,1)S(1)}, u32[]{:S(2)}, u32[]{:S(2)}) collective-permute-start(bf16[24,128,128]{2,1,0:T(8,128)(2,1)S(1)} %collective-permute-done.1.refs_1_), channel_id=1, source_target_pairs={{0,24},{24,0},{48,72},{72,48},{96,120},{120,96},{144,168},{168,144... | collective-permute-start | bytes 2359304 | tf_op jit(solution)/shard_map/ppermute | solution.py:133
  73.8 0.1 pad_add_fusion.where
  73.9 0.0 collective-permute-done.4.refs_4_
  73.9 0.0 collective-permute-done.7.refs_7_
  73.9 0.0 collective-permute-done.6.refs_6_
  73.9 1.8 %collective-permute-done.5.refs_5_ = bf16[24,128,128]{2,1,0:T(8,128)(2,1)S(1)} collective-permute-done((bf16[24,128,128]{2,1,0:T(8,128)(2,1)S(1)}, bf16[24,128,128]{2,1,0:T(8,128)(2,1)S(1)}, u32[]{:S(2)}, u32[]{:S(2)}) %collective-permute-start.5) | collective-permute-done | bytes 786464 | tf_op jit(solution)/shard_map/ppermute | solution.py:133
  75.7 0.0 copy-done.3
  75.7 0.0 copy-done.2
  75.7 0.0 copy-done.1
  75.7 0.0 copy-done.4
  75.7 0.0 copy-done
  75.7 5.0 %product.1 = bf16[64,128,128]{2,1,0:T(8,128)(2,1)S(1)} custom-call(s32[2]{0:T(128)S(1)} %pad_add_fusion.where, s32[48]{0:T(128)S(1)} %copy-done.4, s32[192]{0:T(256)S(1)} %copy-done.1, s32[2,24]{1,0:T(2,128)S(1)} %copy-done.2, s32[2,24]{1,0:T(2,128)S(1)} %bitcast.9, bf16[48,128,128]{2,1,0:T(8,128)(2,1)S(1)} %copy-done, ...), custom_call_target="tpu_custom_call" | custom-call | tf_op jit(solution)/shard_map/product/pallas_call | solution.py:134
  80.7 59.1 %all_to_all.11 = bf16[32,2,128,128]{3,2,1,0:T(8,128)(2,1)S(1)} all-to-all(bf16[32,2,128,128]{3,2,1,0:T(8,128)(2,1)S(1)} %bitcast.8), channel_id=1, replica_groups=mesh['row'=32,'col'=24] {'row'}, dimensions={0} | all-to-all | bytes 4194304 | tf_op jit(solution)/shard_map/all_to_all | solution.py:150
  139.8 1.3 copy.9
  (2 shorter events, 0.0 us)
Async XLA Ops:
  0.0 75.7 %copy-start.3 = (s32[2,24,1]{1,2,0:T(1,128)S(1)}, s32[2,24,1]{1,2,0:T(1,128)}, u32[]{:S(2)}) copy-start(s32[2,24,1]{1,2,0:T(1,128)} %param.11) | copy-start | bytes 580
  0.0 75.7 %copy-start.2 = (s32[2,24]{1,0:T(2,128)S(1)}, s32[2,24]{1,0:T(2,128)}, u32[]{:S(2)}) copy-start(s32[2,24]{1,0:T(2,128)} %keep.1) | copy-start | bytes 580
  0.0 75.7 %copy-start.1 = (s32[192]{0:T(256)S(1)}, s32[192]{0:T(256)}, u32[]{:S(2)}) copy-start(s32[192]{0:T(256)} %rows.1) | copy-start | bytes 2308
  0.0 75.7 %copy-start.4 = (s32[48]{0:T(128)S(1)}, s32[48]{0:T(128)}, u32[]{:S(2)}) copy-start(s32[48]{0:T(128)} %pos.1) | copy-start | bytes 580
  0.0 75.7 %copy-start = (bf16[48,128,128]{2,1,0:T(8,128)(2,1)S(1)}, bf16[48,128,128]{2,1,0:T(8,128)(2,1)}, u32[]{:S(2)}) copy-start(bf16[48,128,128]{2,1,0:T(8,128)(2,1)} %p_hbm.1) | copy-start | bytes 4718596
  39.1 11.8 %collective-permute-start = (bf16[12,128,128]{2,1,0:T(8,128)(2,1)S(1)}, bf16[12,128,128]{2,1,0:T(8,128)(2,1)S(1)}, u32[]{:S(2)}, u32[]{:S(2)}) collective-permute-start(bf16[12,128,128]{2,1,0:T(8,128)(2,1)S(1)} %all_to_all.10), channel_id=1, source_target_pairs={{397,0},{419,24},{398,1},{408,25},{399,2},{409,26},{400,3},{410,27... | collective-permute-start | bytes 1179656 | tf_op jit(solution)/shard_map/ppermute | solution.py:131
  51.0 13.9 %collective-permute-start.3 = (bf16[24,128,128]{2,1,0:T(8,128)(2,1)S(1)}, bf16[24,128,128]{2,1,0:T(8,128)(2,1)S(1)}, u32[]{:S(2)}, u32[]{:S(2)}) collective-permute-start(bf16[24,128,128]{2,1,0:T(8,128)(2,1)S(1)} %constant_dynamic-update-slice_fusion.refs_0_), channel_id=1, source_target_pairs={{48,0},{360,24},{49,1},{361,25},{50,2},{362,26},{51,3},{363,27},{5... | collective-permute-start | bytes 2359304 | tf_op jit(solution)/shard_map/ppermute | solution.py:132
  53.3 16.1 %collective-permute-start.2 = (bf16[24,128,128]{2,1,0:T(8,128)(2,1)S(1)}, bf16[24,128,128]{2,1,0:T(8,128)(2,1)S(1)}, u32[]{:S(2)}, u32[]{:S(2)}) collective-permute-start(bf16[24,128,128]{2,1,0:T(8,128)(2,1)S(1)} %constant_dynamic-update-slice_fusion.refs_0_), channel_id=1, source_target_pairs={{11,0},{420,24},{0,1},{421,25},{1,2},{422,26},{2,3},{423,27},{3,4}... | collective-permute-start | bytes 2359304 | tf_op jit(solution)/shard_map/ppermute | solution.py:132
  55.4 15.9 %collective-permute-start.1 = (bf16[24,128,128]{2,1,0:T(8,128)(2,1)S(1)}, bf16[24,128,128]{2,1,0:T(8,128)(2,1)S(1)}, u32[]{:S(2)}, u32[]{:S(2)}) collective-permute-start(bf16[24,128,128]{2,1,0:T(8,128)(2,1)S(1)} %constant_dynamic-update-slice_fusion.refs_0_), channel_id=1, source_target_pairs={{384,0},{25,24},{385,1},{26,25},{386,2},{27,26},{387,3},{28,27},{3... | collective-permute-start | bytes 2359304 | tf_op jit(solution)/shard_map/ppermute | solution.py:132
  58.9 15.0 %collective-permute-start.4 = (bf16[24,128,128]{2,1,0:T(8,128)(2,1)S(1)}, bf16[24,128,128]{2,1,0:T(8,128)(2,1)S(1)}, u32[]{:S(2)}, u32[]{:S(2)}) collective-permute-start(bf16[24,128,128]{2,1,0:T(8,128)(2,1)S(1)} %constant_dynamic-update-slice_fusion.refs_0_), channel_id=1, source_target_pairs={{0,24},{24,0},{48,72},{72,48},{96,120},{120,96},{144,168},{168,144... | collective-permute-start | bytes 2359304 | tf_op jit(solution)/shard_map/ppermute | solution.py:133
  64.9 9.0 %collective-permute-start.7 = (bf16[24,128,128]{2,1,0:T(8,128)(2,1)S(1)}, bf16[24,128,128]{2,1,0:T(8,128)(2,1)S(1)}, u32[]{:S(2)}, u32[]{:S(2)}) collective-permute-start(bf16[24,128,128]{2,1,0:T(8,128)(2,1)S(1)} %collective-permute-done.3.refs_3_), channel_id=1, source_target_pairs={{0,24},{24,0},{48,72},{72,48},{96,120},{120,96},{144,168},{168,144... | collective-permute-start | bytes 2359304 | tf_op jit(solution)/shard_map/ppermute | solution.py:133
  69.4 4.4 %collective-permute-start.6 = (bf16[24,128,128]{2,1,0:T(8,128)(2,1)S(1)}, bf16[24,128,128]{2,1,0:T(8,128)(2,1)S(1)}, u32[]{:S(2)}, u32[]{:S(2)}) collective-permute-start(bf16[24,128,128]{2,1,0:T(8,128)(2,1)S(1)} %collective-permute-done.2.refs_2_), channel_id=1, source_target_pairs={{0,24},{24,0},{48,72},{72,48},{96,120},{120,96},{144,168},{168,144... | collective-permute-start | bytes 2359304 | tf_op jit(solution)/shard_map/ppermute | solution.py:133
  71.4 4.3 %collective-permute-start.5 = (bf16[24,128,128]{2,1,0:T(8,128)(2,1)S(1)}, bf16[24,128,128]{2,1,0:T(8,128)(2,1)S(1)}, u32[]{:S(2)}, u32[]{:S(2)}) collective-permute-start(bf16[24,128,128]{2,1,0:T(8,128)(2,1)S(1)} %collective-permute-done.1.refs_1_), channel_id=1, source_target_pairs={{0,24},{24,0},{48,72},{72,48},{96,120},{120,96},{144,168},{168,144... | collective-permute-start | bytes 2359304 | tf_op jit(solution)/shard_map/ppermute | solution.py:133

commit v4 on v3

v4 whole, which is shorter than its diff:
```python
import jax
import jax.numpy as jnp
from jax import lax
from jax.experimental import pallas as pl
from jax.experimental.pallas import tpu as pltpu
from jax.sharding import PartitionSpec as P

NX, NY, NZ = 4, 8, 12
BS = 128
KB = 64
RB = 2
NH = 8
NCB = 24
NRG = 32
NP = 48
CAP = 2
PER = NCB // 2
BOTH = ("row", "col")


def device_of(x, y, z, core):
    x, y, z = x % NX, y % NY, z % NZ
    return ((x % 2) * 2 * NY + y * 2 + core) * NCB + (x // 2) * NZ + z


def pull(steps):
    return [
        (device_of(x + steps[k][0], y + steps[k][1], z + steps[k][2], k), device_of(x, y, z, k))
        for x in range(NX)
        for y in range(NY)
        for z in range(NZ)
        for k in range(2)
    ]


NEXT_Z = pull(((-1, 0, 1), (1, 0, -1)))
ALONG_X = pull(((1, 0, 0), (-1, 0, 0)))
ALONG_Z = pull(((0, 0, -1), (0, 0, 1)))
ALONG_Y = pull(((0, 1, 0), (0, -1, 0)))
OTHER_CORE = [(r, r ^ 1) for r in range(NRG)]
HALVES = [
    [h * NZ + m + 2 * i for p in range(2) for h in range(2) for i in range(p ^ h, NZ // 2, 2)]
    for m in range(2)
]


def pick(row, col, h_blocks):
    c = (row >> 4) + (row & 14) + (col & 1)
    first, second = (
        lax.dynamic_index_in_dim(h_blocks, 2 * (k & 3) + (row & 1), axis=0) for k in (c, c + 2)
    )
    return jnp.where(jnp.arange(PER)[:, None, None] < PER // 2, first, second)


def prepare_kernel(pos, owner, p_ref, _, p_all, out_ref, table, count):
    p_all[:NP] = p_ref[...]
    p_all[NP] = jnp.zeros((BS, BS), jnp.bfloat16)
    out_ref[...] = jnp.zeros_like(out_ref)
    for i in range(RB * KB):
        table[i] = NP
    for i in range(NP):
        table[pos[i]] = i
    for i in range(NRG):
        count[i] = 0
    for i in range(RB * NCB):
        to = owner[i // NCB, i % NCB]
        used = count[to]
        count[to] = used + 1
        table[RB * KB + i] = to * CAP + used


def listed_blocks(where):
    row, col = where[0], where[1]
    core = lax.rem(row, 2)
    high = col // NZ
    z = col - NZ * high
    c = 2 * high + row // (2 * NY) + 2 * lax.rem(row // 2, NY) + z
    listed = [
        2 * lax.rem(c + step, 4) + k
        for k in (core, 1 - core)
        for step in (0, 1 + 2 * k, 3 - 2 * k, 2)
    ]
    return listed, lax.rem(z, 2)


def units(parity):
    for q in range(2):
        for h in range(2):
            for i in range(NZ // 2):
                at = ((h + i) % 2) * (PER // 2) + h * (PER // 4) + i // 2
                yield h * NZ + 2 * i + lax.rem(parity + q, 2), q, at


def p_columns(p_all, table, inner):
    return jnp.concatenate(
        [
            jnp.concatenate([p_all[table[r * KB + b]] for b in inner], axis=1)
            for r in range(RB)
        ],
        axis=0,
    )


def most_kernel(where, rows, table, p_all, own, ax, bz, cy, t1, t2, t3, total):
    listed, parity = listed_blocks(where)
    for u, (j, q, at) in enumerate(units(parity)):
        same, other = q * PER + at, (1 - q) * PER + at
        panels = [own[same], ax[same], bz[other], cy[same]]
        panels += [t2[at] if q else t1[at], t2[PER + same], t3[other]]
        left = p_columns(p_all, table, [rows[j * NH + n] for n in listed[:-1]])
        total[u] = jnp.dot(left, jnp.concatenate(panels, axis=0), preferred_element_type=jnp.float32)


def rest_kernel(where, rows, keep, table, p_all, total, t4, _, out_ref):
    listed, parity = listed_blocks(where)
    for u, (j, q, at) in enumerate(units(parity)):
        left = p_columns(p_all, table, [rows[j * NH + listed[-1]]])
        both = total[u] + jnp.dot(left, t4[q * PER + at], preferred_element_type=jnp.float32)
        both = both.astype(jnp.bfloat16)
        for r in range(RB):
            block = both[r * BS : (r + 1) * BS]
            out_ref[table[RB * KB + r * NCB + j]] = jnp.where(
                keep[r, j] == 1, block, jnp.zeros_like(block)
            )


def local(p_blocks, p_positions, h_blocks, h_rows, keep_mask, owner_ids):
    row, col = lax.axis_index("row"), lax.axis_index("col")
    smem = pl.BlockSpec(memory_space=pltpu.SMEM)
    vmem = pl.BlockSpec(memory_space=pltpu.VMEM)
    half = lax.all_to_all(
        pick(row, col, h_blocks),
        "col",
        split_axis=0,
        concat_axis=0,
        axis_index_groups=HALVES,
        tiled=True,
    )
    where = jnp.stack([row, col])
    rest = lax.ppermute(half, BOTH, NEXT_Z)
    t1 = lax.ppermute(half, "row", OTHER_CORE)
    limit = pltpu.CompilerParams(vmem_limit_bytes=24 * 1024 * 1024)
    p_all, empty, table = pl.pallas_call(
        prepare_kernel,
        out_shape=[
            jax.ShapeDtypeStruct((NP + 1, BS, BS), jnp.bfloat16),
            jax.ShapeDtypeStruct((NRG * CAP, BS, BS), jnp.bfloat16),
            jax.ShapeDtypeStruct((RB * KB + RB * NCB,), jnp.int32),
        ],
        in_specs=[smem, smem, vmem, pl.BlockSpec(memory_space=pl.ANY)],
        out_specs=[vmem, vmem, smem],
        scratch_shapes=[pltpu.SMEM((NRG,), jnp.int32)],
        compiler_params=limit,
        name="prepare",
    )(p_positions, owner_ids.reshape(RB, NCB), p_blocks, half)
    own, t1, p_all, empty, table = lax.optimization_barrier(
        (jnp.concatenate([half, rest]), t1, p_all, empty, table)
    )
    ax, bz, cy = (lax.ppermute(own, BOTH, pairs) for pairs in (ALONG_X, ALONG_Z, ALONG_Y))
    t2, t3, t4 = (
        lax.ppermute(x, "row", OTHER_CORE) for x in (jnp.concatenate([rest, ax]), bz, cy)
    )
    total = pl.pallas_call(
        most_kernel,
        out_shape=jax.ShapeDtypeStruct((NCB, RB * BS, BS), jnp.float32),
        in_specs=[smem] * 3 + [vmem] * 8,
        out_specs=vmem,
        compiler_params=limit,
        cost_estimate=pl.CostEstimate(flops=1_400_000_000, bytes_accessed=10_000_000, transcendentals=0),
        name="most",
    )(where, h_rows, table, p_all, own, ax, bz, cy, t1, t2, t3)
    outgoing = pl.pallas_call(
        rest_kernel,
        out_shape=jax.ShapeDtypeStruct((NRG * CAP, BS, BS), jnp.bfloat16),
        in_specs=[smem] * 4 + [vmem] * 4,
        out_specs=vmem,
        input_output_aliases={7: 0},
        compiler_params=limit,
        cost_estimate=pl.CostEstimate(flops=200_000_000, bytes_accessed=5_000_000, transcendentals=0),
        name="rest",
    )(where, h_rows, keep_mask, table, p_all, total, t4, empty)
    outgoing = outgoing.reshape(NRG, CAP, BS, BS)
    return lax.all_to_all(outgoing, "row", split_axis=0, concat_axis=0, tiled=True)


def solution(mesh):
    return jax.shard_map(
        local,
        mesh=mesh,
        in_specs=(
            P(("row", "col"), None, None),
            P(("row", "col")),
            P("col", None, None),
            P(),
            P(("row", "col"), None),
            P(("row", "col"), None, None),
        ),
        out_specs=P(("row", "col"), None, None, None),
        check_vma=False,
    )
```

time: 142 us -> 140 us (0.986)
  waiting for transfers between devices: 15.2 us -> 8.57 us
  local copies, waits for them, and re-layouts: 2.32 us -> 4.84 us
  Pallas kernels: 4.99 us -> 6.63 us
    ppermute x5, waiting for transfers between devices: 8.59 us -> 0.34 us  [the longest x1 0.33 us: local(): rest = lax.ppermute(half, BOTH, NEXT_Z)]
    unnamed x12 -> x11, local copies, waits for them, and re-layouts: 1.37 us -> 4.07 us
    ppermute x3, waiting for transfers between devices: 6.59 us -> 8.24 us  [local(): lax.ppermute(own, BOTH, pairs)]
    pallas_call x1 -> x3, Pallas kernels: 4.99 us -> 6.63 us  [the longest x1 3.64 us: local(): pl.pallas_call(most_kernel, out_shape=jax.ShapeDtypeStruct((NCB, RB * BS,...]
  transfers between devices with their start and end apart: 8 -> 8, of which waited for: 4 -> 3; matrix products, arithmetic and copies ran while one was open for 0% -> 0% of each run, Pallas kernels for 0% -> 4%
where the time goes in v4:
time: 140 us
  blocking collectives  97.2 us (69%)
  starting transfers between devices  22.2 us (16%)
  waiting for transfers between devices  8.57 us (6%)
  Pallas kernels  6.63 us (5%)
  local copies, waits for them, and re-layouts  4.84 us (3%)
    all_to_all x1, blocking collectives, local(): lax.all_to_all(outgoing, 'row', split_axis=0, concat_axis=0, tiled=True)  59.1 us
    all_to_all x1, blocking collectives, local(): lax.all_to_all(pick(row, col, h_blocks), 'col', split_axis=0, concat_axis...  38.1 us
    ppermute x3, starting transfers between devices, local(): lax.ppermute(own, BOTH, pairs)  8.52 us
    ppermute x3, waiting for transfers between devices, local(): lax.ppermute(own, BOTH, pairs)  8.24 us
    ppermute x3, starting transfers between devices, local(): lax.ppermute(x, 'row', OTHER_CORE)  6.77 us
    ppermute x1, starting transfers between devices, local(): rest = lax.ppermute(half, BOTH, NEXT_Z)  4.94 us
    unnamed x11, local copies, waits for them, and re-layouts  4.07 us
    pallas_call x1, Pallas kernels, local(): pl.pallas_call(most_kernel, out_shape=jax.ShapeDtypeStruct((NCB, RB * BS,...  3.64 us
  transfers between devices with their start and end apart: 8, of which 3 were waited for; matrix products, arithmetic and copies ran while one was open for 0% of the time, Pallas kernels for 4%

profile of v4, /device:TPU:8, one launch (start us, length us, event | category | flops | bytes accessed | tf_op | source)
XLA Modules:
  0.0 139.9 jit_solution(8841300498426547291)
XLA Ops:
  0.0 0.8 dynamic-slice_bitcast_fusion.1
  0.8 0.1 broadcast_select_fusion
  0.9 38.1 %all_to_all.10._ = bf16[12,128,128]{2,1,0:T(8,128)(2,1)S(1)} all-to-all(bf16[12,128,128]{2,1,0:T(8,128)(2,1)S(1)} %broadcast_select_fusion), channel_id=1, replica_groups={{0,4,8,14,18,22,2,6,10,12,16,20},{1,5,9,15,19,23,3,7,11,13,17,21},{24,2..., dimensions={0} | all-to-all | bytes 786432 | tf_op jit(solution)/shard_map/all_to_all | solution.py:131
  39.0 4.9 %collective-permute-start = (bf16[12,128,128]{2,1,0:T(8,128)(2,1)S(1)}, bf16[12,128,128]{2,1,0:T(8,128)(2,1)S(1)}, u32[]{:S(2)}, u32[]{:S(2)}) collective-permute-start(bf16[12,128,128]{2,1,0:T(8,128)(2,1)S(1)} %all_to_all.10._), channel_id=1, source_target_pairs={{397,0},{419,24},{398,1},{408,25},{399,2},{409,26},{400,3},{410,27... | collective-permute-start | bytes 1179656 | tf_op jit(solution)/shard_map/ppermute | solution.py:140
  43.9 1.9 %collective-permute-start.1 = (bf16[12,128,128]{2,1,0:T(8,128)(2,1)S(1)}, bf16[12,128,128]{2,1,0:T(8,128)(2,1)S(1)}, u32[]{:S(2)}, u32[]{:S(2)}) collective-permute-start(bf16[12,128,128]{2,1,0:T(8,128)(2,1)S(1)} %all_to_all.10._), channel_id=1, source_target_pairs={{0,24},{24,0},{48,72},{72,48},{96,120},{120,96},{144,168},{168,144... | collective-permute-start | bytes 1179656 | tf_op jit(solution)/shard_map/ppermute | solution.py:141
  45.8 0.0 copy-start
  45.9 1.4 %copy-done = bf16[48,128,128]{2,1,0:T(8,128)(2,1)S(1)} copy-done((bf16[48,128,128]{2,1,0:T(8,128)(2,1)S(1)}, bf16[48,128,128]{2,1,0:T(8,128)(2,1)}, u32[]{:S(2)}) %copy-start) | copy-done | bytes 1572888
  47.3 0.0 copy-start.2
  47.3 0.7 copy-done.2
  47.9 0.0 copy-start.4
  47.9 0.7 copy-done.4
  48.6 1.8 %prepare.1 = (bf16[49,128,128]{2,1,0:T(8,128)(2,1)S(1)}, bf16[64,128,128]{2,1,0:T(8,128)(2,1)S(1)}, s32[176]{0:T(256)S(1)}) custom-call(s32[48]{0:T(128)S(1)} %copy-done.4, s32[2,24]{1,0:T(2,128)S(1)} %bitcast.9, bf16[48,128,128]{2,1,0:T(8,128)(2,1)S(1)} %copy-done, bf16[12,128,128]{2,1,0:T(8,128)(2,1)S(1)} %all_to_all.10._), custom_call_target="tpu_custom_call" | custom-call | tf_op jit(solution)/shard_map/prepare/pallas_call | solution.py:143
  50.4 0.0 copy-start.1
  50.4 0.3 collective-permute-done
  50.7 0.1 pad_maximum_fusion.1.own
  50.8 0.0 collective-permute-done.1.t1
  50.8 4.2 %collective-permute-start.2 = (bf16[24,128,128]{2,1,0:T(8,128)(2,1)S(1)}, bf16[24,128,128]{2,1,0:T(8,128)(2,1)S(1)}, u32[]{:S(2)}, u32[]{:S(2)}) collective-permute-start(bf16[24,128,128]{2,1,0:T(8,128)(2,1)S(1)} %pad_maximum_fusion.1.own), channel_id=1, source_target_pairs={{384,0},{420,24},{385,1},{421,25},{386,2},{422,26},{387,3},{423,27... | collective-permute-start | bytes 2359304 | tf_op jit(solution)/shard_map/ppermute | solution.py:159
  55.1 1.9 %collective-permute-start.3 = (bf16[24,128,128]{2,1,0:T(8,128)(2,1)S(1)}, bf16[24,128,128]{2,1,0:T(8,128)(2,1)S(1)}, u32[]{:S(2)}, u32[]{:S(2)}) collective-permute-start(bf16[24,128,128]{2,1,0:T(8,128)(2,1)S(1)} %pad_maximum_fusion.1.own), channel_id=1, source_target_pairs={{11,0},{25,24},{0,1},{26,25},{1,2},{27,26},{2,3},{28,27},{3,4},{29... | collective-permute-start | bytes 2359304 | tf_op jit(solution)/shard_map/ppermute | solution.py:159
  57.0 2.4 %collective-permute-start.4 = (bf16[24,128,128]{2,1,0:T(8,128)(2,1)S(1)}, bf16[24,128,128]{2,1,0:T(8,128)(2,1)S(1)}, u32[]{:S(2)}, u32[]{:S(2)}) collective-permute-start(bf16[24,128,128]{2,1,0:T(8,128)(2,1)S(1)} %pad_maximum_fusion.1.own), channel_id=1, source_target_pairs={{48,0},{360,24},{49,1},{361,25},{50,2},{362,26},{51,3},{363,27},{5... | collective-permute-start | bytes 2359304 | tf_op jit(solution)/shard_map/ppermute | solution.py:159
  59.4 5.3 %collective-permute-done.2.ax = bf16[24,128,128]{2,1,0:T(8,128)(2,1)S(1)} collective-permute-done((bf16[24,128,128]{2,1,0:T(8,128)(2,1)S(1)}, bf16[24,128,128]{2,1,0:T(8,128)(2,1)S(1)}, u32[]{:S(2)}, u32[]{:S(2)}) %collective-permute-start.2) | collective-permute-done | bytes 786464 | tf_op jit(solution)/shard_map/ppermute | solution.py:159
  64.7 0.1 pad_maximum_fusion
  64.8 2.5 %collective-permute-start.5 = (bf16[36,128,128]{2,1,0:T(8,128)(2,1)S(1)}, bf16[36,128,128]{2,1,0:T(8,128)(2,1)S(1)}, u32[]{:S(2)}, u32[]{:S(2)}) collective-permute-start(bf16[36,128,128]{2,1,0:T(8,128)(2,1)S(1)} %pad_maximum_fusion), channel_id=1, source_target_pairs={{0,24},{24,0},{48,72},{72,48},{96,120},{120,96},{144,168},{168,144... | collective-permute-start | bytes 3538952 | tf_op jit(solution)/shard_map/ppermute | solution.py:161
  67.3 2.9 %collective-permute-done.3.bz = bf16[24,128,128]{2,1,0:T(8,128)(2,1)S(1)} collective-permute-done((bf16[24,128,128]{2,1,0:T(8,128)(2,1)S(1)}, bf16[24,128,128]{2,1,0:T(8,128)(2,1)S(1)}, u32[]{:S(2)}, u32[]{:S(2)}) %collective-permute-start.3) | collective-permute-done | bytes 786464 | tf_op jit(solution)/shard_map/ppermute | solution.py:159
  70.2 1.9 %collective-permute-start.6 = (bf16[24,128,128]{2,1,0:T(8,128)(2,1)S(1)}, bf16[24,128,128]{2,1,0:T(8,128)(2,1)S(1)}, u32[]{:S(2)}, u32[]{:S(2)}) collective-permute-start(bf16[24,128,128]{2,1,0:T(8,128)(2,1)S(1)} %collective-permute-done.3.bz), channel_id=1, source_target_pairs={{0,24},{24,0},{48,72},{72,48},{96,120},{120,96},{144,168},{168,144... | collective-permute-start | bytes 2359304 | tf_op jit(solution)/shard_map/ppermute | solution.py:161
  72.1 0.0 collective-permute-done.4.cy
  72.1 2.4 %collective-permute-start.7 = (bf16[24,128,128]{2,1,0:T(8,128)(2,1)S(1)}, bf16[24,128,128]{2,1,0:T(8,128)(2,1)S(1)}, u32[]{:S(2)}, u32[]{:S(2)}) collective-permute-start(bf16[24,128,128]{2,1,0:T(8,128)(2,1)S(1)} %collective-permute-done.4.cy), channel_id=1, source_target_pairs={{0,24},{24,0},{48,72},{72,48},{96,120},{120,96},{144,168},{168,144... | collective-permute-start | bytes 2359304 | tf_op jit(solution)/shard_map/ppermute | solution.py:161
  74.5 0.1 pad_add_fusion.where
  74.6 0.0 copy-start.3
  74.6 0.0 collective-permute-done.6.t3
  74.6 0.0 collective-permute-done.5.t2
  74.6 0.0 copy-done.1
  74.6 3.6 %most.1.total = f32[24,256,128]{2,1,0:T(8,128)S(1)} custom-call(s32[2]{0:T(128)S(1)} %pad_add_fusion.where, s32[192]{0:T(256)S(1)} %copy-done.1, s32[176]{0:T(256)S(1)} %get-tuple-element.16.table, bf16[49,128,128]{2,1,0:T(8,128)(2,1)S(1)} %get-tuple-element.17.p_all, bf16[24,128,128]{2,1,0:T(8,128)(2,1)S(1)} %pad_maximum_fusion.1.own, ...), custom_call_target="tpu_custom_call" | custom-call | flops 1400000000 | bytes 10000000 | tf_op jit(solution)/shard_map/most/pallas_call | solution.py:163
  78.2 0.0 collective-permute-done.7.t4
  78.3 0.0 copy-done.3
  78.3 1.2 rest.1
  79.5 59.1 %all_to_all.11 = bf16[32,2,128,128]{3,2,1,0:T(8,128)(2,1)S(1)} all-to-all(bf16[32,2,128,128]{3,2,1,0:T(8,128)(2,1)S(1)} %bitcast.8), channel_id=1, replica_groups=mesh['row'=32,'col'=24] {'row'}, dimensions={0} | all-to-all | bytes 4194304 | tf_op jit(solution)/shard_map/all_to_all | solution.py:183
  138.6 1.3 copy.10
  (1 shorter events, 0.0 us)
Async XLA Ops:
  39.0 11.8 %collective-permute-start = (bf16[12,128,128]{2,1,0:T(8,128)(2,1)S(1)}, bf16[12,128,128]{2,1,0:T(8,128)(2,1)S(1)}, u32[]{:S(2)}, u32[]{:S(2)}) collective-permute-start(bf16[12,128,128]{2,1,0:T(8,128)(2,1)S(1)} %all_to_all.10._), channel_id=1, source_target_pairs={{397,0},{419,24},{398,1},{408,25},{399,2},{409,26},{400,3},{410,27... | collective-permute-start | bytes 1179656 | tf_op jit(solution)/shard_map/ppermute | solution.py:140
  43.9 6.9 %collective-permute-start.1 = (bf16[12,128,128]{2,1,0:T(8,128)(2,1)S(1)}, bf16[12,128,128]{2,1,0:T(8,128)(2,1)S(1)}, u32[]{:S(2)}, u32[]{:S(2)}) collective-permute-start(bf16[12,128,128]{2,1,0:T(8,128)(2,1)S(1)} %all_to_all.10._), channel_id=1, source_target_pairs={{0,24},{24,0},{48,72},{72,48},{96,120},{120,96},{144,168},{168,144... | collective-permute-start | bytes 1179656 | tf_op jit(solution)/shard_map/ppermute | solution.py:141
  45.8 1.4 %copy-start = (bf16[48,128,128]{2,1,0:T(8,128)(2,1)S(1)}, bf16[48,128,128]{2,1,0:T(8,128)(2,1)}, u32[]{:S(2)}) copy-start(bf16[48,128,128]{2,1,0:T(8,128)(2,1)} %p_ref.1) | copy-start | bytes 4718596
  47.3 0.7 copy-start.2
  47.9 0.7 copy-start.4
  50.4 24.2 %copy-start.1 = (s32[192]{0:T(256)S(1)}, s32[192]{0:T(256)}, u32[]{:S(2)}) copy-start(s32[192]{0:T(256)} %rows.3) | copy-start | bytes 2308
  50.8 13.9 %collective-permute-start.2 = (bf16[24,128,128]{2,1,0:T(8,128)(2,1)S(1)}, bf16[24,128,128]{2,1,0:T(8,128)(2,1)S(1)}, u32[]{:S(2)}, u32[]{:S(2)}) collective-permute-start(bf16[24,128,128]{2,1,0:T(8,128)(2,1)S(1)} %pad_maximum_fusion.1.own), channel_id=1, source_target_pairs={{384,0},{420,24},{385,1},{421,25},{386,2},{422,26},{387,3},{423,27... | collective-permute-start | bytes 2359304 | tf_op jit(solution)/shard_map/ppermute | solution.py:159
  55.1 15.1 %collective-permute-start.3 = (bf16[24,128,128]{2,1,0:T(8,128)(2,1)S(1)}, bf16[24,128,128]{2,1,0:T(8,128)(2,1)S(1)}, u32[]{:S(2)}, u32[]{:S(2)}) collective-permute-start(bf16[24,128,128]{2,1,0:T(8,128)(2,1)S(1)} %pad_maximum_fusion.1.own), channel_id=1, source_target_pairs={{11,0},{25,24},{0,1},{26,25},{1,2},{27,26},{2,3},{28,27},{3,4},{29... | collective-permute-start | bytes 2359304 | tf_op jit(solution)/shard_map/ppermute | solution.py:159
  57.0 15.1 %collective-permute-start.4 = (bf16[24,128,128]{2,1,0:T(8,128)(2,1)S(1)}, bf16[24,128,128]{2,1,0:T(8,128)(2,1)S(1)}, u32[]{:S(2)}, u32[]{:S(2)}) collective-permute-start(bf16[24,128,128]{2,1,0:T(8,128)(2,1)S(1)} %pad_maximum_fusion.1.own), channel_id=1, source_target_pairs={{48,0},{360,24},{49,1},{361,25},{50,2},{362,26},{51,3},{363,27},{5... | collective-permute-start | bytes 2359304 | tf_op jit(solution)/shard_map/ppermute | solution.py:159
  64.8 9.8 %collective-permute-start.5 = (bf16[36,128,128]{2,1,0:T(8,128)(2,1)S(1)}, bf16[36,128,128]{2,1,0:T(8,128)(2,1)S(1)}, u32[]{:S(2)}, u32[]{:S(2)}) collective-permute-start(bf16[36,128,128]{2,1,0:T(8,128)(2,1)S(1)} %pad_maximum_fusion), channel_id=1, source_target_pairs={{0,24},{24,0},{48,72},{72,48},{96,120},{120,96},{144,168},{168,144... | collective-permute-start | bytes 3538952 | tf_op jit(solution)/shard_map/ppermute | solution.py:161
  70.2 4.4 %collective-permute-start.6 = (bf16[24,128,128]{2,1,0:T(8,128)(2,1)S(1)}, bf16[24,128,128]{2,1,0:T(8,128)(2,1)S(1)}, u32[]{:S(2)}, u32[]{:S(2)}) collective-permute-start(bf16[24,128,128]{2,1,0:T(8,128)(2,1)S(1)} %collective-permute-done.3.bz), channel_id=1, source_target_pairs={{0,24},{24,0},{48,72},{72,48},{96,120},{120,96},{144,168},{168,144... | collective-permute-start | bytes 2359304 | tf_op jit(solution)/shard_map/ppermute | solution.py:161
  72.1 6.2 %collective-permute-start.7 = (bf16[24,128,128]{2,1,0:T(8,128)(2,1)S(1)}, bf16[24,128,128]{2,1,0:T(8,128)(2,1)S(1)}, u32[]{:S(2)}, u32[]{:S(2)}) collective-permute-start(bf16[24,128,128]{2,1,0:T(8,128)(2,1)S(1)} %collective-permute-done.4.cy), channel_id=1, source_target_pairs={{0,24},{24,0},{48,72},{72,48},{96,120},{120,96},{144,168},{168,144... | collective-permute-start | bytes 2359304 | tf_op jit(solution)/shard_map/ppermute | solution.py:161
  74.6 3.7 %copy-start.3 = (s32[2,24]{1,0:T(2,128)S(1)}, s32[2,24]{1,0:T(2,128)}, u32[]{:S(2)}) copy-start(s32[2,24]{1,0:T(2,128)} %keep.1) | copy-start | bytes 580

commit v5 on v4

v5 whole, which is shorter than its diff:
```python
import jax
import jax.numpy as jnp
from jax import lax
from jax.experimental import pallas as pl
from jax.experimental.pallas import tpu as pltpu
from jax.sharding import PartitionSpec as P

NX, NY, NZ = 4, 8, 12
BS = 128
KB = 64
RB = 2
NH = 8
NCB = 24
NRG = 32
NP = 48
CAP = 2
PARTS = 3
PER = NCB // PARTS
BOTH = ("row", "col")


def device_of(x, y, z, core):
    x, y, z = x % NX, y % NY, z % NZ
    return ((x % 2) * 2 * NY + y * 2 + core) * NCB + (x // 2) * NZ + z


def pull(steps):
    return [
        (device_of(x + steps[k][0], y + steps[k][1], z + steps[k][2], k), device_of(x, y, z, k))
        for x in range(NX)
        for y in range(NY)
        for z in range(NZ)
        for k in range(2)
    ]


UP_Z = pull(((-1, 0, 1), (-1, 0, 1)))
DOWN_Z = pull(((1, 0, -1), (1, 0, -1)))
ALONG_X = pull(((1, 0, 0), (-1, 0, 0)))
ALONG_Z = pull(((0, 0, -1), (0, 0, 1)))
ALONG_Y = pull(((0, 1, 0), (0, -1, 0)))
OTHER_CORE = [(r, r ^ 1) for r in range(NRG)]
THIRDS = [
    [
        h * NZ + m + PARTS * i
        for step in range(4)
        for h in range(2)
        for i in range(NZ // PARTS)
        if (2 * h + 3 * i) % 4 == step
    ]
    for m in range(PARTS)
]


def pick(row, col, h_blocks):
    c = (row >> 4) + (row & 14) + lax.rem(jnp.where(col < NZ, col, col - NZ), PARTS)
    blocks = [
        lax.dynamic_index_in_dim(h_blocks, 2 * ((c + step) & 3) + (row & 1), axis=0)
        for step in range(4)
    ]
    member = jnp.arange(PER)[:, None, None]
    low = jnp.where(member < 2, blocks[0], blocks[1])
    high = jnp.where(member < 6, blocks[2], blocks[3])
    return jnp.where(member < 4, low, high)


def prepare_kernel(pos, owner, _, out_ref, table, count):
    out_ref[...] = jnp.zeros_like(out_ref)
    for i in range(RB * KB):
        table[i] = -1
    for i in range(NP):
        table[pos[i]] = i
    for i in range(NRG):
        count[i] = 0
    for i in range(RB * NCB):
        to = owner[i // NCB, i % NCB]
        used = count[to]
        count[to] = used + 1
        table[RB * KB + i] = to * CAP + used


def listed_blocks(where):
    row, col = where[0], where[1]
    core = lax.rem(row, 2)
    high = col // NZ
    z = col - NZ * high
    c = 2 * high + row // (2 * NY) + 2 * lax.rem(row // 2, NY) + z
    listed = [
        2 * lax.rem(c + step, 4) + k
        for k in (core, 1 - core)
        for step in (0, 1 + 2 * k, 3 - 2 * k, 2)
    ]
    return listed, z, core


def units(z):
    for q in range(PARTS):
        for h in range(2):
            for i in range(NZ // PARTS):
                at = 2 * ((2 * h + 3 * i) % 4) + h
                yield h * NZ + PARTS * i + lax.rem(z + q, PARTS), q, at


def p_columns(p_ref, table, inner):
    def block(place):
        listed = p_ref[jnp.maximum(place, 0)]
        return jnp.where(place >= 0, listed, jnp.zeros_like(listed))

    return jnp.concatenate(
        [
            jnp.concatenate([block(table[r * KB + b]) for b in inner], axis=1)
            for r in range(RB)
        ],
        axis=0,
    )


def most_kernel(where, rows, table, p_ref, own, ax, bz, cy, t1, t2, t3, total):
    listed, z, core = listed_blocks(where)
    for u, (j, q, at) in enumerate(units(z)):
        same = q * PER + at
        below, above = (q + 1) % PARTS * PER + at, (q + 2) % PARTS * PER + at
        from_z = [jnp.where(core == 0, below, above), jnp.where(core == 0, above, below)]
        panels = [own[same], ax[same], bz[from_z[0]], cy[same]]
        panels += [t2[same - PER] if q else t1[at], t2[2 * PER + same], t3[from_z[1]]]
        left = p_columns(p_ref, table, [rows[j * NH + n] for n in listed[:-1]])
        total[u] = jnp.dot(left, jnp.concatenate(panels, axis=0), preferred_element_type=jnp.float32)


def rest_kernel(where, rows, keep, table, p_ref, total, t4, _, out_ref):
    listed, z, _core = listed_blocks(where)
    for u, (j, q, at) in enumerate(units(z)):
        left = p_columns(p_ref, table, [rows[j * NH + listed[-1]]])
        both = total[u] + jnp.dot(left, t4[q * PER + at], preferred_element_type=jnp.float32)
        both = both.astype(jnp.bfloat16)
        for r in range(RB):
            block = both[r * BS : (r + 1) * BS]
            out_ref[table[RB * KB + r * NCB + j]] = jnp.where(
                keep[r, j] == 1, block, jnp.zeros_like(block)
            )


def local(p_blocks, p_positions, h_blocks, h_rows, keep_mask, owner_ids):
    row, col = lax.axis_index("row"), lax.axis_index("col")
    smem = pl.BlockSpec(memory_space=pltpu.SMEM)
    vmem = pl.BlockSpec(memory_space=pltpu.VMEM)
    third = lax.all_to_all(
        pick(row, col, h_blocks),
        "col",
        split_axis=0,
        concat_axis=0,
        axis_index_groups=THIRDS,
        tiled=True,
    )
    where = jnp.stack([row, col])
    rest = [lax.ppermute(third, BOTH, pairs) for pairs in (UP_Z, DOWN_Z)]
    t1 = lax.ppermute(third, "row", OTHER_CORE)
    own, t1 = lax.optimization_barrier((jnp.concatenate([third] + rest), t1))
    ax, bz, cy = (lax.ppermute(own, BOTH, pairs) for pairs in (ALONG_X, ALONG_Z, ALONG_Y))
    limit = pltpu.CompilerParams(vmem_limit_bytes=24 * 1024 * 1024)
    empty, table = pl.pallas_call(
        prepare_kernel,
        out_shape=[
            jax.ShapeDtypeStruct((NRG * CAP, BS, BS), jnp.bfloat16),
            jax.ShapeDtypeStruct((RB * KB + RB * NCB,), jnp.int32),
        ],
        in_specs=[smem, smem, pl.BlockSpec(memory_space=pl.ANY)],
        out_specs=[vmem, smem],
        scratch_shapes=[pltpu.SMEM((NRG,), jnp.int32)],
        compiler_params=limit,
        name="prepare",
    )(p_positions, owner_ids.reshape(RB, NCB), own)
    ax, empty, table = lax.optimization_barrier((ax, empty, table))
    t2, t3, t4 = (
        lax.ppermute(x, "row", OTHER_CORE) for x in (jnp.concatenate(rest + [ax]), bz, cy)
    )
    total = pl.pallas_call(
        most_kernel,
        out_shape=jax.ShapeDtypeStruct((NCB, RB * BS, BS), jnp.float32),
        in_specs=[smem] * 3 + [vmem] * 8,
        out_specs=vmem,
        compiler_params=limit,
        cost_estimate=pl.CostEstimate(flops=1_400_000_000, bytes_accessed=10_000_000, transcendentals=0),
        name="most",
    )(where, h_rows, table, p_blocks, own, ax, bz, cy, t1, t2, t3)
    outgoing = pl.pallas_call(
        rest_kernel,
        out_shape=jax.ShapeDtypeStruct((NRG * CAP, BS, BS), jnp.bfloat16),
        in_specs=[smem] * 4 + [vmem] * 4,
        out_specs=vmem,
        input_output_aliases={7: 0},
        compiler_params=limit,
        cost_estimate=pl.CostEstimate(flops=200_000_000, bytes_accessed=5_000_000, transcendentals=0),
        name="rest",
    )(where, h_rows, keep_mask, table, p_blocks, total, t4, empty)
    outgoing = outgoing.reshape(NRG, CAP, BS, BS)
    return lax.all_to_all(outgoing, "row", split_axis=0, concat_axis=0, tiled=True)


def solution(mesh):
    return jax.shard_map(
        local,
        mesh=mesh,
        in_specs=(
            P(("row", "col"), None, None),
            P(("row", "col")),
            P("col", None, None),
            P(),
            P(("row", "col"), None),
            P(("row", "col"), None, None),
        ),
        out_specs=P(("row", "col"), None, None, None),
        check_vma=False,
    )
```

time: 140 us -> 140 us (level)
  blocking collectives: 97.2 us -> 91 us
  starting transfers between devices: 22.2 us -> 26.6 us
  waiting for transfers between devices: 8.57 us -> 12.2 us
  local copies, waits for them, and re-layouts: 4.84 us -> 2.17 us
    all_to_all x1, blocking collectives: 38.1 us -> 32.1 us  [local(): lax.all_to_all(pick(row, col, h_blocks), 'col', split_axis=0, concat_axis...]
    ppermute x2 -> x3, waiting for transfers between devices: 0.33 us -> 5.31 us  [the longest x2 5.31 us: local(): rest = [lax.ppermute(third, BOTH, pairs) for pairs in (UP_Z, DOWN_Z)]]
    ppermute x2 -> x3, starting transfers between devices: 6.87 us -> 10.2 us  [the longest x2 8.31 us: local(): rest = [lax.ppermute(third, BOTH, pairs) for pairs in (UP_Z, DOWN_Z)]]
    unnamed x11, local copies, waits for them, and re-layouts: 4.07 us -> 1.34 us
    ppermute x3, starting transfers between devices: 8.52 us -> 10 us  [local(): lax.ppermute(own, BOTH, pairs)]
  transfers between devices with their start and end apart: 8 -> 9, of which waited for: 3 -> 4; matrix products, arithmetic and copies ran while one was open for 0% -> 0% of each run, Pallas kernels for 4% -> 4%
where the time goes in v5:
time: 140 us; the launch traced here: 139 us
  blocking collectives  91 us (65%)
  starting transfers between devices  26.6 us (19%)
  waiting for transfers between devices  12.2 us (9%)
  Pallas kernels  6.76 us (5%)
  local copies, waits for them, and re-layouts  2.17 us (2%)
    all_to_all x1, blocking collectives, local(): lax.all_to_all(outgoing, 'row', split_axis=0, concat_axis=0, tiled=True)  59 us
    all_to_all x1, blocking collectives, local(): lax.all_to_all(pick(row, col, h_blocks), 'col', split_axis=0, concat_axis...  32.1 us
    ppermute x3, starting transfers between devices, local(): lax.ppermute(own, BOTH, pairs)  10 us
    ppermute x2, starting transfers between devices, local(): rest = [lax.ppermute(third, BOTH, pairs) for pairs in (UP_Z, DOWN_Z)]  8.31 us
    ppermute x3, waiting for transfers between devices, local(): lax.ppermute(own, BOTH, pairs)  6.87 us
    ppermute x3, starting transfers between devices, local(): lax.ppermute(x, 'row', OTHER_CORE)  6.37 us
    ppermute x2, waiting for transfers between devices, local(): rest = [lax.ppermute(third, BOTH, pairs) for pairs in (UP_Z, DOWN_Z)]  5.31 us
    pallas_call x1, Pallas kernels, local(): pl.pallas_call(most_kernel, out_shape=jax.ShapeDtypeStruct((NCB, RB * BS,...  3.73 us
  transfers between devices with their start and end apart: 9, of which 4 were waited for; matrix products, arithmetic and copies ran while one was open for 0% of the time, Pallas kernels for 4%

profile of v5, /device:TPU:8, one launch (start us, length us, event | category | flops | bytes accessed | tf_op | source)
XLA Modules:
  0.0 139.4 jit_solution(12933377005938289520)
XLA Ops:
  0.0 0.8 dynamic-slice_bitcast_fusion.3
  0.8 0.0 copy-start.2
  0.9 0.0 copy-start.4
  0.9 0.1 select_select_fusion
  1.0 32.1 %all_to_all.10 = bf16[8,128,128]{2,1,0:T(8,128)(2,1)S(1)} all-to-all(bf16[8,128,128]{2,1,0:T(8,128)(2,1)S(1)} %select_select_fusion), channel_id=1, replica_groups={{0,18,9,15,6,12,3,21},{1,19,10,16,7,13,4,22},{2,20,11,17,8,14,5,23},{24..., dimensions={0} | all-to-all | bytes 524288 | tf_op jit(solution)/shard_map/all_to_all | solution.py:147
  33.1 5.1 %collective-permute-start = (bf16[8,128,128]{2,1,0:T(8,128)(2,1)S(1)}, bf16[8,128,128]{2,1,0:T(8,128)(2,1)S(1)}, u32[]{:S(2)}, u32[]{:S(2)}) collective-permute-start(bf16[8,128,128]{2,1,0:T(8,128)(2,1)S(1)} %all_to_all.10), channel_id=1, source_target_pairs={{397,0},{421,24},{398,1},{422,25},{399,2},{423,26},{400,3},{424,27... | collective-permute-start | bytes 786440 | tf_op jit(solution)/shard_map/ppermute | solution.py:156
  38.1 3.2 %collective-permute-start.1 = (bf16[8,128,128]{2,1,0:T(8,128)(2,1)S(1)}, bf16[8,128,128]{2,1,0:T(8,128)(2,1)S(1)}, u32[]{:S(2)}, u32[]{:S(2)}) collective-permute-start(bf16[8,128,128]{2,1,0:T(8,128)(2,1)S(1)} %all_to_all.10), channel_id=1, source_target_pairs={{395,0},{419,24},{384,1},{408,25},{385,2},{409,26},{386,3},{410,27... | collective-permute-start | bytes 786440 | tf_op jit(solution)/shard_map/ppermute | solution.py:156
  41.4 1.9 %collective-permute-start.2 = (bf16[8,128,128]{2,1,0:T(8,128)(2,1)S(1)}, bf16[8,128,128]{2,1,0:T(8,128)(2,1)S(1)}, u32[]{:S(2)}, u32[]{:S(2)}) collective-permute-start(bf16[8,128,128]{2,1,0:T(8,128)(2,1)S(1)} %all_to_all.10), channel_id=1, source_target_pairs={{0,24},{24,0},{48,72},{72,48},{96,120},{120,96},{144,168},{168,144... | collective-permute-start | bytes 786440 | tf_op jit(solution)/shard_map/ppermute | solution.py:157
  43.3 2.1 %collective-permute-done = bf16[8,128,128]{2,1,0:T(8,128)(2,1)S(1)} collective-permute-done((bf16[8,128,128]{2,1,0:T(8,128)(2,1)S(1)}, bf16[8,128,128]{2,1,0:T(8,128)(2,1)S(1)}, u32[]{:S(2)}, u32[]{:S(2)}) %collective-permute-start) | collective-permute-done | bytes 262176 | tf_op jit(solution)/shard_map/ppermute | solution.py:156
  45.4 3.2 %collective-permute-done.1 = bf16[8,128,128]{2,1,0:T(8,128)(2,1)S(1)} collective-permute-done((bf16[8,128,128]{2,1,0:T(8,128)(2,1)S(1)}, bf16[8,128,128]{2,1,0:T(8,128)(2,1)S(1)}, u32[]{:S(2)}, u32[]{:S(2)}) %collective-permute-start.1) | collective-permute-done | bytes 262176 | tf_op jit(solution)/shard_map/ppermute | solution.py:156
  48.6 0.1 pad_maximum_fusion.1._.own
  48.7 0.0 collective-permute-done.2.t1
  48.7 5.8 %collective-permute-start.3 = (bf16[24,128,128]{2,1,0:T(8,128)(2,1)S(1)}, bf16[24,128,128]{2,1,0:T(8,128)(2,1)S(1)}, u32[]{:S(2)}, u32[]{:S(2)}) collective-permute-start(bf16[24,128,128]{2,1,0:T(8,128)(2,1)S(1)} %pad_maximum_fusion.1._.own), channel_id=1, source_target_pairs={{384,0},{420,24},{385,1},{421,25},{386,2},{422,26},{387,3},{423,27... | collective-permute-start | bytes 2359304 | tf_op jit(solution)/shard_map/ppermute | solution.py:159
  54.5 1.9 %collective-permute-start.4 = (bf16[24,128,128]{2,1,0:T(8,128)(2,1)S(1)}, bf16[24,128,128]{2,1,0:T(8,128)(2,1)S(1)}, u32[]{:S(2)}, u32[]{:S(2)}) collective-permute-start(bf16[24,128,128]{2,1,0:T(8,128)(2,1)S(1)} %pad_maximum_fusion.1._.own), channel_id=1, source_target_pairs={{11,0},{25,24},{0,1},{26,25},{1,2},{27,26},{2,3},{28,27},{3,4},{29... | collective-permute-start | bytes 2359304 | tf_op jit(solution)/shard_map/ppermute | solution.py:159
  56.4 2.4 %collective-permute-start.5 = (bf16[24,128,128]{2,1,0:T(8,128)(2,1)S(1)}, bf16[24,128,128]{2,1,0:T(8,128)(2,1)S(1)}, u32[]{:S(2)}, u32[]{:S(2)}) collective-permute-start(bf16[24,128,128]{2,1,0:T(8,128)(2,1)S(1)} %pad_maximum_fusion.1._.own), channel_id=1, source_target_pairs={{48,0},{360,24},{49,1},{361,25},{50,2},{362,26},{51,3},{363,27},{5... | collective-permute-start | bytes 2359304 | tf_op jit(solution)/shard_map/ppermute | solution.py:159
  58.8 0.0 copy-done.2
  58.8 0.0 copy-done.4
  58.8 1.7 %prepare.1 = (bf16[64,128,128]{2,1,0:T(8,128)(2,1)S(1)}, s32[176]{0:T(256)S(1)}) custom-call(s32[48]{0:T(128)S(1)} %copy-done.4, s32[2,24]{1,0:T(2,128)S(1)} %bitcast.13, bf16[24,128,128]{2,1,0:T(8,128)(2,1)S(1)} %pad_maximum_fusion.1._.own), custom_call_target="tpu_custom_call" | custom-call | tf_op jit(solution)/shard_map/prepare/pallas_call | solution.py:161
  60.5 3.5 %collective-permute-done.3.ax = bf16[24,128,128]{2,1,0:T(8,128)(2,1)S(1)} collective-permute-done((bf16[24,128,128]{2,1,0:T(8,128)(2,1)S(1)}, bf16[24,128,128]{2,1,0:T(8,128)(2,1)S(1)}, u32[]{:S(2)}, u32[]{:S(2)}) %collective-permute-start.3) | collective-permute-done | bytes 786464 | tf_op jit(solution)/shard_map/ppermute | solution.py:159
  64.0 0.0 copy-start
  64.0 0.0 copy-start.1
  64.0 0.1 pad_maximum_fusion
  64.1 2.1 %collective-permute-start.6 = (bf16[40,128,128]{2,1,0:T(8,128)(2,1)S(1)}, bf16[40,128,128]{2,1,0:T(8,128)(2,1)S(1)}, u32[]{:S(2)}, u32[]{:S(2)}) collective-permute-start(bf16[40,128,128]{2,1,0:T(8,128)(2,1)S(1)} %pad_maximum_fusion), channel_id=1, source_target_pairs={{0,24},{24,0},{48,72},{72,48},{96,120},{120,96},{144,168},{168,144... | collective-permute-start | bytes 3932168 | tf_op jit(solution)/shard_map/ppermute | solution.py:175
  66.2 3.4 %collective-permute-done.4.bz = bf16[24,128,128]{2,1,0:T(8,128)(2,1)S(1)} collective-permute-done((bf16[24,128,128]{2,1,0:T(8,128)(2,1)S(1)}, bf16[24,128,128]{2,1,0:T(8,128)(2,1)S(1)}, u32[]{:S(2)}, u32[]{:S(2)}) %collective-permute-start.4) | collective-permute-done | bytes 786464 | tf_op jit(solution)/shard_map/ppermute | solution.py:159
  69.6 1.9 %collective-permute-start.7 = (bf16[24,128,128]{2,1,0:T(8,128)(2,1)S(1)}, bf16[24,128,128]{2,1,0:T(8,128)(2,1)S(1)}, u32[]{:S(2)}, u32[]{:S(2)}) collective-permute-start(bf16[24,128,128]{2,1,0:T(8,128)(2,1)S(1)} %collective-permute-done.4.bz), channel_id=1, source_target_pairs={{0,24},{24,0},{48,72},{72,48},{96,120},{120,96},{144,168},{168,144... | collective-permute-start | bytes 2359304 | tf_op jit(solution)/shard_map/ppermute | solution.py:175
  71.5 0.0 collective-permute-done.5.cy
  71.5 2.4 %collective-permute-start.8 = (bf16[24,128,128]{2,1,0:T(8,128)(2,1)S(1)}, bf16[24,128,128]{2,1,0:T(8,128)(2,1)S(1)}, u32[]{:S(2)}, u32[]{:S(2)}) collective-permute-start(bf16[24,128,128]{2,1,0:T(8,128)(2,1)S(1)} %collective-permute-done.5.cy), channel_id=1, source_target_pairs={{0,24},{24,0},{48,72},{72,48},{96,120},{120,96},{144,168},{168,144... | collective-permute-start | bytes 2359304 | tf_op jit(solution)/shard_map/ppermute | solution.py:175
  73.9 0.1 pad_add_fusion.where
  74.0 0.0 copy-start.3
  74.0 0.0 collective-permute-done.7.t3
  74.0 0.0 collective-permute-done.6.t2
  74.0 0.0 copy-done
  74.0 0.0 copy-done.1
  74.0 3.7 %most.1.total = f32[24,256,128]{2,1,0:T(8,128)S(1)} custom-call(s32[2]{0:T(128)S(1)} %pad_add_fusion.where, s32[192]{0:T(256)S(1)} %copy-done.1, s32[176]{0:T(256)S(1)} %get-tuple-element.15.table, bf16[48,128,128]{2,1,0:T(8,128)(2,1)S(1)} %copy-done, bf16[24,128,128]{2,1,0:T(8,128)(2,1)S(1)} %pad_maximum_fusion.1._.own, ...), custom_call_target="tpu_custom_call" | custom-call | flops 1400000000 | bytes 10000000 | tf_op jit(solution)/shard_map/most/pallas_call | solution.py:177
  77.8 0.0 collective-permute-done.8.t4
  77.8 0.0 copy-done.3
  77.8 1.3 rest.1
  79.1 59.0 %all_to_all.11 = bf16[32,2,128,128]{3,2,1,0:T(8,128)(2,1)S(1)} all-to-all(bf16[32,2,128,128]{3,2,1,0:T(8,128)(2,1)S(1)} %bitcast.12), channel_id=1, replica_groups=mesh['row'=32,'col'=24] {'row'}, dimensions={0} | all-to-all | bytes 4194304 | tf_op jit(solution)/shard_map/all_to_all | solution.py:197
  138.1 1.3 copy.10
  (2 shorter events, 0.0 us)
Async XLA Ops:
  0.8 58.0 %copy-start.2 = (s32[2,24,1]{1,2,0:T(1,128)S(1)}, s32[2,24,1]{1,2,0:T(1,128)}, u32[]{:S(2)}) copy-start(s32[2,24,1]{1,2,0:T(1,128)} %param.11) | copy-start | bytes 580
  0.9 57.9 %copy-start.4 = (s32[48]{0:T(128)S(1)}, s32[48]{0:T(128)}, u32[]{:S(2)}) copy-start(s32[48]{0:T(128)} %pos.1) | copy-start | bytes 580
  33.1 12.4 %collective-permute-start = (bf16[8,128,128]{2,1,0:T(8,128)(2,1)S(1)}, bf16[8,128,128]{2,1,0:T(8,128)(2,1)S(1)}, u32[]{:S(2)}, u32[]{:S(2)}) collective-permute-start(bf16[8,128,128]{2,1,0:T(8,128)(2,1)S(1)} %all_to_all.10), channel_id=1, source_target_pairs={{397,0},{421,24},{398,1},{422,25},{399,2},{423,26},{400,3},{424,27... | collective-permute-start | bytes 786440 | tf_op jit(solution)/shard_map/ppermute | solution.py:156
  38.1 10.5 %collective-permute-start.1 = (bf16[8,128,128]{2,1,0:T(8,128)(2,1)S(1)}, bf16[8,128,128]{2,1,0:T(8,128)(2,1)S(1)}, u32[]{:S(2)}, u32[]{:S(2)}) collective-permute-start(bf16[8,128,128]{2,1,0:T(8,128)(2,1)S(1)} %all_to_all.10), channel_id=1, source_target_pairs={{395,0},{419,24},{384,1},{408,25},{385,2},{409,26},{386,3},{410,27... | collective-permute-start | bytes 786440 | tf_op jit(solution)/shard_map/ppermute | solution.py:156
  41.4 7.3 %collective-permute-start.2 = (bf16[8,128,128]{2,1,0:T(8,128)(2,1)S(1)}, bf16[8,128,128]{2,1,0:T(8,128)(2,1)S(1)}, u32[]{:S(2)}, u32[]{:S(2)}) collective-permute-start(bf16[8,128,128]{2,1,0:T(8,128)(2,1)S(1)} %all_to_all.10), channel_id=1, source_target_pairs={{0,24},{24,0},{48,72},{72,48},{96,120},{120,96},{144,168},{168,144... | collective-permute-start | bytes 786440 | tf_op jit(solution)/shard_map/ppermute | solution.py:157
  48.7 15.3 %collective-permute-start.3 = (bf16[24,128,128]{2,1,0:T(8,128)(2,1)S(1)}, bf16[24,128,128]{2,1,0:T(8,128)(2,1)S(1)}, u32[]{:S(2)}, u32[]{:S(2)}) collective-permute-start(bf16[24,128,128]{2,1,0:T(8,128)(2,1)S(1)} %pad_maximum_fusion.1._.own), channel_id=1, source_target_pairs={{384,0},{420,24},{385,1},{421,25},{386,2},{422,26},{387,3},{423,27... | collective-permute-start | bytes 2359304 | tf_op jit(solution)/shard_map/ppermute | solution.py:159
  54.5 15.1 %collective-permute-start.4 = (bf16[24,128,128]{2,1,0:T(8,128)(2,1)S(1)}, bf16[24,128,128]{2,1,0:T(8,128)(2,1)S(1)}, u32[]{:S(2)}, u32[]{:S(2)}) collective-permute-start(bf16[24,128,128]{2,1,0:T(8,128)(2,1)S(1)} %pad_maximum_fusion.1._.own), channel_id=1, source_target_pairs={{11,0},{25,24},{0,1},{26,25},{1,2},{27,26},{2,3},{28,27},{3,4},{29... | collective-permute-start | bytes 2359304 | tf_op jit(solution)/shard_map/ppermute | solution.py:159
  56.4 15.1 %collective-permute-start.5 = (bf16[24,128,128]{2,1,0:T(8,128)(2,1)S(1)}, bf16[24,128,128]{2,1,0:T(8,128)(2,1)S(1)}, u32[]{:S(2)}, u32[]{:S(2)}) collective-permute-start(bf16[24,128,128]{2,1,0:T(8,128)(2,1)S(1)} %pad_maximum_fusion.1._.own), channel_id=1, source_target_pairs={{48,0},{360,24},{49,1},{361,25},{50,2},{362,26},{51,3},{363,27},{5... | collective-permute-start | bytes 2359304 | tf_op jit(solution)/shard_map/ppermute | solution.py:159
  64.0 10.0 %copy-start = (bf16[48,128,128]{2,1,0:T(8,128)(2,1)S(1)}, bf16[48,128,128]{2,1,0:T(8,128)(2,1)}, u32[]{:S(2)}) copy-start(bf16[48,128,128]{2,1,0:T(8,128)(2,1)} %p_ref.3) | copy-start | bytes 4718596
  64.0 10.0 %copy-start.1 = (s32[192]{0:T(256)S(1)}, s32[192]{0:T(256)}, u32[]{:S(2)}) copy-start(s32[192]{0:T(256)} %rows.3) | copy-start | bytes 2308
  64.1 9.9 %collective-permute-start.6 = (bf16[40,128,128]{2,1,0:T(8,128)(2,1)S(1)}, bf16[40,128,128]{2,1,0:T(8,128)(2,1)S(1)}, u32[]{:S(2)}, u32[]{:S(2)}) collective-permute-start(bf16[40,128,128]{2,1,0:T(8,128)(2,1)S(1)} %pad_maximum_fusion), channel_id=1, source_target_pairs={{0,24},{24,0},{48,72},{72,48},{96,120},{120,96},{144,168},{168,144... | collective-permute-start | bytes 3932168 | tf_op jit(solution)/shard_map/ppermute | solution.py:175
  69.6 4.4 %collective-permute-start.7 = (bf16[24,128,128]{2,1,0:T(8,128)(2,1)S(1)}, bf16[24,128,128]{2,1,0:T(8,128)(2,1)S(1)}, u32[]{:S(2)}, u32[]{:S(2)}) collective-permute-start(bf16[24,128,128]{2,1,0:T(8,128)(2,1)S(1)} %collective-permute-done.4.bz), channel_id=1, source_target_pairs={{0,24},{24,0},{48,72},{72,48},{96,120},{120,96},{144,168},{168,144... | collective-permute-start | bytes 2359304 | tf_op jit(solution)/shard_map/ppermute | solution.py:175
  71.5 6.3 %collective-permute-start.8 = (bf16[24,128,128]{2,1,0:T(8,128)(2,1)S(1)}, bf16[24,128,128]{2,1,0:T(8,128)(2,1)S(1)}, u32[]{:S(2)}, u32[]{:S(2)}) collective-permute-start(bf16[24,128,128]{2,1,0:T(8,128)(2,1)S(1)} %collective-permute-done.5.cy), channel_id=1, source_target_pairs={{0,24},{24,0},{48,72},{72,48},{96,120},{120,96},{144,168},{168,144... | collective-permute-start | bytes 2359304 | tf_op jit(solution)/shard_map/ppermute | solution.py:175
  74.0 3.8 %copy-start.3 = (s32[2,24]{1,0:T(2,128)S(1)}, s32[2,24]{1,0:T(2,128)}, u32[]{:S(2)}) copy-start(s32[2,24]{1,0:T(2,128)} %keep.1) | copy-start | bytes 580

commit v6 on v5

--- a/solution.py
+++ b/solution.py
@@ -115,23 +115,35 @@
     )
 
 
-def most_kernel(where, rows, table, p_ref, own, ax, bz, cy, t1, t2, t3, total):
+def z_panel(core, q, at):
+    return jnp.where(core == 0, (q + 1) % PARTS, (q + 2) % PARTS) * PER + at
+
+
+def most_kernel(where, rows, table, p_ref, own, ax, bz, cy, t1, t3, total):
     listed, z, core = listed_blocks(where)
     for u, (j, q, at) in enumerate(units(z)):
         same = q * PER + at
-        below, above = (q + 1) % PARTS * PER + at, (q + 2) % PARTS * PER + at
-        from_z = [jnp.where(core == 0, below, above), jnp.where(core == 0, above, below)]
-        panels = [own[same], ax[same], bz[from_z[0]], cy[same]]
-        panels += [t2[same - PER] if q else t1[at], t2[2 * PER + same], t3[from_z[1]]]
-        left = p_columns(p_ref, table, [rows[j * NH + n] for n in listed[:-1]])
+        panels = [own[same], ax[same], bz[z_panel(core, q, at)], cy[same]]
+        panels += [t3[z_panel(1 - core, q, at)], t3[NCB + same]]
+        held = listed[:4] + listed[6:]
+        if q == 0:
+            panels.append(t1[at])
+            held.append(listed[4])
+        left = p_columns(p_ref, table, [rows[j * NH + n] for n in held])
         total[u] = jnp.dot(left, jnp.concatenate(panels, axis=0), preferred_element_type=jnp.float32)
 
 
-def rest_kernel(where, rows, keep, table, p_ref, total, t4, _, out_ref):
+def rest_kernel(where, rows, keep, table, p_ref, total, t2, _, out_ref):
     listed, z, _core = listed_blocks(where)
     for u, (j, q, at) in enumerate(units(z)):
-        left = p_columns(p_ref, table, [rows[j * NH + listed[-1]]])
-        both = total[u] + jnp.dot(left, t4[q * PER + at], preferred_element_type=jnp.float32)
+        panels, held = [t2[(PARTS - 1 + q) * PER + at]], [listed[5]]
+        if q:
+            panels.append(t2[(q - 1) * PER + at])
+            held.append(listed[4])
+        left = p_columns(p_ref, table, [rows[j * NH + n] for n in held])
+        both = total[u] + jnp.dot(
+            left, jnp.concatenate(panels, axis=0), preferred_element_type=jnp.float32
+        )
         both = both.astype(jnp.bfloat16)
         for r in range(RB):
             block = both[r * BS : (r + 1) * BS]
@@ -170,19 +182,19 @@
         compiler_params=limit,
         name="prepare",
     )(p_positions, owner_ids.reshape(RB, NCB), own)
-    ax, empty, table = lax.optimization_barrier((ax, empty, table))
-    t2, t3, t4 = (
-        lax.ppermute(x, "row", OTHER_CORE) for x in (jnp.concatenate(rest + [ax]), bz, cy)
+    bz, empty, table = lax.optimization_barrier((bz, empty, table))
+    t2, t3 = (
+        lax.ppermute(jnp.concatenate(x), "row", OTHER_CORE) for x in (rest + [ax], [bz, cy])
     )
     total = pl.pallas_call(
         most_kernel,
         out_shape=jax.ShapeDtypeStruct((NCB, RB * BS, BS), jnp.float32),
-        in_specs=[smem] * 3 + [vmem] * 8,
+        in_specs=[smem] * 3 + [vmem] * 7,
         out_specs=vmem,
         compiler_params=limit,
-        cost_estimate=pl.CostEstimate(flops=1_400_000_000, bytes_accessed=10_000_000, transcendentals=0),
+        cost_estimate=pl.CostEstimate(flops=1_200_000_000, bytes_accessed=10_000_000, transcendentals=0),
         name="most",
-    )(where, h_rows, table, p_blocks, own, ax, bz, cy, t1, t2, t3)
+    )(where, h_rows, table, p_blocks, own, ax, bz, cy, t1, t3)
     outgoing = pl.pallas_call(
         rest_kernel,
         out_shape=jax.ShapeDtypeStruct((NRG * CAP, BS, BS), jnp.bfloat16),
@@ -190,9 +202,9 @@
         out_specs=vmem,
         input_output_aliases={7: 0},
         compiler_params=limit,
-        cost_estimate=pl.CostEstimate(flops=200_000_000, bytes_accessed=5_000_000, transcendentals=0),
+        cost_estimate=pl.CostEstimate(flops=400_000_000, bytes_accessed=5_000_000, transcendentals=0),
         name="rest",
-    )(where, h_rows, keep_mask, table, p_blocks, total, t4, empty)
+    )(where, h_rows, keep_mask, table, p_blocks, total, t2, empty)
     outgoing = outgoing.reshape(NRG, CAP, BS, BS)
     return lax.all_to_all(outgoing, "row", split_axis=0, concat_axis=0, tiled=True)
 

time: 140 us -> 138 us (0.986)
  the two profiles are of different devices: /device:TPU:8 before, /device:TPU:12 now
where the time goes in v6:
time: 138 us
  blocking collectives  90.4 us (66%)
  starting transfers between devices  21.2 us (15%)
  waiting for transfers between devices  16.3 us (12%)
  Pallas kernels  6.75 us (5%)
  local copies, waits for them, and re-layouts  2.17 us (2%)
    all_to_all x1, blocking collectives, local(): lax.all_to_all(outgoing, 'row', split_axis=0, concat_axis=0, tiled=True)  61.8 us
    all_to_all x1, blocking collectives, local(): lax.all_to_all(pick(row, col, h_blocks), 'col', split_axis=0, concat_axis...  28.5 us
    ppermute x3, waiting for transfers between devices, local(): lax.ppermute(own, BOTH, pairs)  9.12 us
    ppermute x2, starting transfers between devices, local(): rest = [lax.ppermute(third, BOTH, pairs) for pairs in (UP_Z, DOWN_Z)]  8.55 us
    ppermute x2, waiting for transfers between devices, local(): rest = [lax.ppermute(third, BOTH, pairs) for pairs in (UP_Z, DOWN_Z)]  7.21 us
    ppermute x3, starting transfers between devices, local(): lax.ppermute(own, BOTH, pairs)  6.76 us
    ppermute x2, starting transfers between devices, local(): lax.ppermute(jnp.concatenate(x), 'row', OTHER_CORE)  3.97 us
    pallas_call x1, Pallas kernels, local(): pl.pallas_call(most_kernel, out_shape=jax.ShapeDtypeStruct((NCB, RB * BS,...  3.43 us
  transfers between devices with their start and end apart: 8, of which 5 were waited for; matrix products, arithmetic and copies ran while one was open for 0% of the time, Pallas kernels for 4%

profile of v6, /device:TPU:12, one launch (start us, length us, event | category | flops | bytes accessed | tf_op | source)
XLA Modules:
  0.0 137.6 jit_solution(15642003517598288257)
XLA Ops:
  0.0 0.0 copy-start.2
  0.0 0.0 copy-start.4
  0.0 0.8 dynamic-slice_bitcast_fusion.3
  0.9 0.1 select_select_fusion
  1.0 28.5 %all_to_all.10 = bf16[8,128,128]{2,1,0:T(8,128)(2,1)S(1)} all-to-all(bf16[8,128,128]{2,1,0:T(8,128)(2,1)S(1)} %select_select_fusion), channel_id=1, replica_groups={{0,18,9,15,6,12,3,21},{1,19,10,16,7,13,4,22},{2,20,11,17,8,14,5,23},{24..., dimensions={0} | all-to-all | bytes 524288 | tf_op jit(solution)/shard_map/all_to_all | solution.py:159
  29.5 6.6 %collective-permute-start = (bf16[8,128,128]{2,1,0:T(8,128)(2,1)S(1)}, bf16[8,128,128]{2,1,0:T(8,128)(2,1)S(1)}, u32[]{:S(2)}, u32[]{:S(2)}) collective-permute-start(bf16[8,128,128]{2,1,0:T(8,128)(2,1)S(1)} %all_to_all.10), channel_id=1, source_target_pairs={{397,0},{421,24},{398,1},{422,25},{399,2},{423,26},{400,3},{424,27... | collective-permute-start | bytes 786440 | tf_op jit(solution)/shard_map/ppermute | solution.py:168
  36.1 1.9 %collective-permute-start.1 = (bf16[8,128,128]{2,1,0:T(8,128)(2,1)S(1)}, bf16[8,128,128]{2,1,0:T(8,128)(2,1)S(1)}, u32[]{:S(2)}, u32[]{:S(2)}) collective-permute-start(bf16[8,128,128]{2,1,0:T(8,128)(2,1)S(1)} %all_to_all.10), channel_id=1, source_target_pairs={{395,0},{419,24},{384,1},{408,25},{385,2},{409,26},{386,3},{410,27... | collective-permute-start | bytes 786440 | tf_op jit(solution)/shard_map/ppermute | solution.py:168
  38.1 1.9 %collective-permute-start.2 = (bf16[8,128,128]{2,1,0:T(8,128)(2,1)S(1)}, bf16[8,128,128]{2,1,0:T(8,128)(2,1)S(1)}, u32[]{:S(2)}, u32[]{:S(2)}) collective-permute-start(bf16[8,128,128]{2,1,0:T(8,128)(2,1)S(1)} %all_to_all.10), channel_id=1, source_target_pairs={{0,24},{24,0},{48,72},{72,48},{96,120},{120,96},{144,168},{168,144... | collective-permute-start | bytes 786440 | tf_op jit(solution)/shard_map/ppermute | solution.py:169
  40.0 0.5 collective-permute-done
  40.5 6.7 %collective-permute-done.1 = bf16[8,128,128]{2,1,0:T(8,128)(2,1)S(1)} collective-permute-done((bf16[8,128,128]{2,1,0:T(8,128)(2,1)S(1)}, bf16[8,128,128]{2,1,0:T(8,128)(2,1)S(1)}, u32[]{:S(2)}, u32[]{:S(2)}) %collective-permute-start.1) | collective-permute-done | bytes 262176 | tf_op jit(solution)/shard_map/ppermute | solution.py:168
  47.2 0.1 pad_maximum_fusion.2._.own
  47.3 0.0 collective-permute-done.2.t1
  47.3 2.5 %collective-permute-start.3 = (bf16[24,128,128]{2,1,0:T(8,128)(2,1)S(1)}, bf16[24,128,128]{2,1,0:T(8,128)(2,1)S(1)}, u32[]{:S(2)}, u32[]{:S(2)}) collective-permute-start(bf16[24,128,128]{2,1,0:T(8,128)(2,1)S(1)} %pad_maximum_fusion.2._.own), channel_id=1, source_target_pairs={{11,0},{25,24},{0,1},{26,25},{1,2},{27,26},{2,3},{28,27},{3,4},{29... | collective-permute-start | bytes 2359304 | tf_op jit(solution)/shard_map/ppermute | solution.py:171
  49.8 2.4 %collective-permute-start.5 = (bf16[24,128,128]{2,1,0:T(8,128)(2,1)S(1)}, bf16[24,128,128]{2,1,0:T(8,128)(2,1)S(1)}, u32[]{:S(2)}, u32[]{:S(2)}) collective-permute-start(bf16[24,128,128]{2,1,0:T(8,128)(2,1)S(1)} %pad_maximum_fusion.2._.own), channel_id=1, source_target_pairs={{48,0},{360,24},{49,1},{361,25},{50,2},{362,26},{51,3},{363,27},{5... | collective-permute-start | bytes 2359304 | tf_op jit(solution)/shard_map/ppermute | solution.py:171
  52.2 1.9 %collective-permute-start.4 = (bf16[24,128,128]{2,1,0:T(8,128)(2,1)S(1)}, bf16[24,128,128]{2,1,0:T(8,128)(2,1)S(1)}, u32[]{:S(2)}, u32[]{:S(2)}) collective-permute-start(bf16[24,128,128]{2,1,0:T(8,128)(2,1)S(1)} %pad_maximum_fusion.2._.own), channel_id=1, source_target_pairs={{384,0},{420,24},{385,1},{421,25},{386,2},{422,26},{387,3},{423,27... | collective-permute-start | bytes 2359304 | tf_op jit(solution)/shard_map/ppermute | solution.py:171
  54.1 0.0 copy-done.2
  54.1 0.0 copy-done.4
  54.1 1.7 %prepare.1 = (bf16[64,128,128]{2,1,0:T(8,128)(2,1)S(1)}, s32[176]{0:T(256)S(1)}) custom-call(s32[48]{0:T(128)S(1)} %copy-done.4, s32[2,24]{1,0:T(2,128)S(1)} %bitcast.13, bf16[24,128,128]{2,1,0:T(8,128)(2,1)S(1)} %pad_maximum_fusion.2._.own), custom_call_target="tpu_custom_call" | custom-call | tf_op jit(solution)/shard_map/prepare/pallas_call | solution.py:173
  55.8 6.6 %collective-permute-done.3.bz = bf16[24,128,128]{2,1,0:T(8,128)(2,1)S(1)} collective-permute-done((bf16[24,128,128]{2,1,0:T(8,128)(2,1)S(1)}, bf16[24,128,128]{2,1,0:T(8,128)(2,1)S(1)}, u32[]{:S(2)}, u32[]{:S(2)}) %collective-permute-start.3) | collective-permute-done | bytes 786464 | tf_op jit(solution)/shard_map/ppermute | solution.py:171
  62.4 1.3 collective-permute-done.5.cy
  63.7 0.1 pad_maximum_fusion
  63.8 0.0 copy-start
  63.8 0.0 copy-start.1
  63.8 2.1 %collective-permute-start.6 = (bf16[48,128,128]{2,1,0:T(8,128)(2,1)S(1)}, bf16[48,128,128]{2,1,0:T(8,128)(2,1)S(1)}, u32[]{:S(2)}, u32[]{:S(2)}) collective-permute-start(bf16[48,128,128]{2,1,0:T(8,128)(2,1)S(1)} %pad_maximum_fusion), channel_id=1, source_target_pairs={{0,24},{24,0},{48,72},{72,48},{96,120},{120,96},{144,168},{168,144... | collective-permute-start | bytes 4718600 | tf_op jit(solution)/shard_map/ppermute | solution.py:187
  65.9 1.3 collective-permute-done.4.ax
  67.2 0.1 pad_maximum_fusion.1
  67.3 1.9 %collective-permute-start.7 = (bf16[40,128,128]{2,1,0:T(8,128)(2,1)S(1)}, bf16[40,128,128]{2,1,0:T(8,128)(2,1)S(1)}, u32[]{:S(2)}, u32[]{:S(2)}) collective-permute-start(bf16[40,128,128]{2,1,0:T(8,128)(2,1)S(1)} %pad_maximum_fusion.1), channel_id=1, source_target_pairs={{0,24},{24,0},{48,72},{72,48},{96,120},{120,96},{144,168},{168,144... | collective-permute-start | bytes 3932168 | tf_op jit(solution)/shard_map/ppermute | solution.py:187
  69.2 0.1 pad_add_fusion.where
  69.3 0.0 copy-start.3
  69.3 0.0 collective-permute-done.6.t3
  69.3 0.0 copy-done
  69.3 0.0 copy-done.1
  69.3 3.4 %most.1.total = f32[24,256,128]{2,1,0:T(8,128)S(1)} custom-call(s32[2]{0:T(128)S(1)} %pad_add_fusion.where, s32[192]{0:T(256)S(1)} %copy-done.1, s32[176]{0:T(256)S(1)} %get-tuple-element.15.table, bf16[48,128,128]{2,1,0:T(8,128)(2,1)S(1)} %copy-done, bf16[24,128,128]{2,1,0:T(8,128)(2,1)S(1)} %pad_maximum_fusion.2._.own, ...), custom_call_target="tpu_custom_call" | custom-call | flops 1200000000 | bytes 10000000 | tf_op jit(solution)/shard_map/most/pallas_call | solution.py:189
  72.8 0.0 collective-permute-done.7.t2
  72.8 0.0 copy-done.3
  72.8 1.6 %rest.1 = bf16[64,128,128]{2,1,0:T(8,128)(2,1)S(1)} custom-call(s32[2]{0:T(128)S(1)} %pad_add_fusion.where, s32[192]{0:T(256)S(1)} %copy-done.1, s32[2,24]{1,0:T(2,128)S(1)} %copy-done.3, s32[176]{0:T(256)S(1)} %get-tuple-element.15.table, bf16[48,128,128]{2,1,0:T(8,128)(2,1)S(1)} %copy-done, ...), custom_call_target="tpu_custom_call", output_to_operand_aliasing={{}: (7, {})} | custom-call | flops 400000000 | bytes 5000000 | tf_op jit(solution)/shard_map/rest/pallas_call | solution.py:198
  74.4 61.8 %all_to_all.11 = bf16[32,2,128,128]{3,2,1,0:T(8,128)(2,1)S(1)} all-to-all(bf16[32,2,128,128]{3,2,1,0:T(8,128)(2,1)S(1)} %bitcast.12), channel_id=1, replica_groups=mesh['row'=32,'col'=24] {'row'}, dimensions={0} | all-to-all | bytes 4194304 | tf_op jit(solution)/shard_map/all_to_all | solution.py:209
  136.2 1.3 copy.10
  (2 shorter events, 0.0 us)
Async XLA Ops:
  0.0 54.1 %copy-start.2 = (s32[2,24,1]{1,2,0:T(1,128)S(1)}, s32[2,24,1]{1,2,0:T(1,128)}, u32[]{:S(2)}) copy-start(s32[2,24,1]{1,2,0:T(1,128)} %param.11) | copy-start | bytes 580
  0.0 54.1 %copy-start.4 = (s32[48]{0:T(128)S(1)}, s32[48]{0:T(128)}, u32[]{:S(2)}) copy-start(s32[48]{0:T(128)} %pos.1) | copy-start | bytes 580
  29.5 11.0 %collective-permute-start = (bf16[8,128,128]{2,1,0:T(8,128)(2,1)S(1)}, bf16[8,128,128]{2,1,0:T(8,128)(2,1)S(1)}, u32[]{:S(2)}, u32[]{:S(2)}) collective-permute-start(bf16[8,128,128]{2,1,0:T(8,128)(2,1)S(1)} %all_to_all.10), channel_id=1, source_target_pairs={{397,0},{421,24},{398,1},{422,25},{399,2},{423,26},{400,3},{424,27... | collective-permute-start | bytes 786440 | tf_op jit(solution)/shard_map/ppermute | solution.py:168
  36.1 11.1 %collective-permute-start.1 = (bf16[8,128,128]{2,1,0:T(8,128)(2,1)S(1)}, bf16[8,128,128]{2,1,0:T(8,128)(2,1)S(1)}, u32[]{:S(2)}, u32[]{:S(2)}) collective-permute-start(bf16[8,128,128]{2,1,0:T(8,128)(2,1)S(1)} %all_to_all.10), channel_id=1, source_target_pairs={{395,0},{419,24},{384,1},{408,25},{385,2},{409,26},{386,3},{410,27... | collective-permute-start | bytes 786440 | tf_op jit(solution)/shard_map/ppermute | solution.py:168
  38.1 9.2 %collective-permute-start.2 = (bf16[8,128,128]{2,1,0:T(8,128)(2,1)S(1)}, bf16[8,128,128]{2,1,0:T(8,128)(2,1)S(1)}, u32[]{:S(2)}, u32[]{:S(2)}) collective-permute-start(bf16[8,128,128]{2,1,0:T(8,128)(2,1)S(1)} %all_to_all.10), channel_id=1, source_target_pairs={{0,24},{24,0},{48,72},{72,48},{96,120},{120,96},{144,168},{168,144... | collective-permute-start | bytes 786440 | tf_op jit(solution)/shard_map/ppermute | solution.py:169
  47.3 15.1 %collective-permute-start.3 = (bf16[24,128,128]{2,1,0:T(8,128)(2,1)S(1)}, bf16[24,128,128]{2,1,0:T(8,128)(2,1)S(1)}, u32[]{:S(2)}, u32[]{:S(2)}) collective-permute-start(bf16[24,128,128]{2,1,0:T(8,128)(2,1)S(1)} %pad_maximum_fusion.2._.own), channel_id=1, source_target_pairs={{11,0},{25,24},{0,1},{26,25},{1,2},{27,26},{2,3},{28,27},{3,4},{29... | collective-permute-start | bytes 2359304 | tf_op jit(solution)/shard_map/ppermute | solution.py:171
  49.8 13.9 %collective-permute-start.5 = (bf16[24,128,128]{2,1,0:T(8,128)(2,1)S(1)}, bf16[24,128,128]{2,1,0:T(8,128)(2,1)S(1)}, u32[]{:S(2)}, u32[]{:S(2)}) collective-permute-start(bf16[24,128,128]{2,1,0:T(8,128)(2,1)S(1)} %pad_maximum_fusion.2._.own), channel_id=1, source_target_pairs={{48,0},{360,24},{49,1},{361,25},{50,2},{362,26},{51,3},{363,27},{5... | collective-permute-start | bytes 2359304 | tf_op jit(solution)/shard_map/ppermute | solution.py:171
  52.2 15.0 %collective-permute-start.4 = (bf16[24,128,128]{2,1,0:T(8,128)(2,1)S(1)}, bf16[24,128,128]{2,1,0:T(8,128)(2,1)S(1)}, u32[]{:S(2)}, u32[]{:S(2)}) collective-permute-start(bf16[24,128,128]{2,1,0:T(8,128)(2,1)S(1)} %pad_maximum_fusion.2._.own), channel_id=1, source_target_pairs={{384,0},{420,24},{385,1},{421,25},{386,2},{422,26},{387,3},{423,27... | collective-permute-start | bytes 2359304 | tf_op jit(solution)/shard_map/ppermute | solution.py:171
  63.8 5.5 %copy-start = (bf16[48,128,128]{2,1,0:T(8,128)(2,1)S(1)}, bf16[48,128,128]{2,1,0:T(8,128)(2,1)}, u32[]{:S(2)}) copy-start(bf16[48,128,128]{2,1,0:T(8,128)(2,1)} %p_ref.3) | copy-start | bytes 4718596
  63.8 5.5 %copy-start.1 = (s32[192]{0:T(256)S(1)}, s32[192]{0:T(256)}, u32[]{:S(2)}) copy-start(s32[192]{0:T(256)} %rows.3) | copy-start | bytes 2308
  63.8 5.5 %collective-permute-start.6 = (bf16[48,128,128]{2,1,0:T(8,128)(2,1)S(1)}, bf16[48,128,128]{2,1,0:T(8,128)(2,1)S(1)}, u32[]{:S(2)}, u32[]{:S(2)}) collective-permute-start(bf16[48,128,128]{2,1,0:T(8,128)(2,1)S(1)} %pad_maximum_fusion), channel_id=1, source_target_pairs={{0,24},{24,0},{48,72},{72,48},{96,120},{120,96},{144,168},{168,144... | collective-permute-start | bytes 4718600 | tf_op jit(solution)/shard_map/ppermute | solution.py:187
  67.3 5.5 %collective-permute-start.7 = (bf16[40,128,128]{2,1,0:T(8,128)(2,1)S(1)}, bf16[40,128,128]{2,1,0:T(8,128)(2,1)S(1)}, u32[]{:S(2)}, u32[]{:S(2)}) collective-permute-start(bf16[40,128,128]{2,1,0:T(8,128)(2,1)S(1)} %pad_maximum_fusion.1), channel_id=1, source_target_pairs={{0,24},{24,0},{48,72},{72,48},{96,120},{120,96},{144,168},{168,144... | collective-permute-start | bytes 3932168 | tf_op jit(solution)/shard_map/ppermute | solution.py:187
  69.3 3.5 %copy-start.3 = (s32[2,24]{1,0:T(2,128)S(1)}, s32[2,24]{1,0:T(2,128)}, u32[]{:S(2)}) copy-start(s32[2,24]{1,0:T(2,128)} %keep.1) | copy-start | bytes 580

commit v7 on v6

--- a/solution.py
+++ b/solution.py
@@ -119,18 +119,27 @@
     return jnp.where(core == 0, (q + 1) % PARTS, (q + 2) % PARTS) * PER + at
 
 
-def most_kernel(where, rows, table, p_ref, own, ax, bz, cy, t1, t3, total):
-    listed, z, core = listed_blocks(where)
+def first_kernel(where, rows, table, p_ref, own, t1, total):
+    listed, z, _core = listed_blocks(where)
     for u, (j, q, at) in enumerate(units(z)):
-        same = q * PER + at
-        panels = [own[same], ax[same], bz[z_panel(core, q, at)], cy[same]]
-        panels += [t3[z_panel(1 - core, q, at)], t3[NCB + same]]
-        held = listed[:4] + listed[6:]
+        panels, held = [own[q * PER + at]], [listed[0]]
         if q == 0:
             panels.append(t1[at])
             held.append(listed[4])
         left = p_columns(p_ref, table, [rows[j * NH + n] for n in held])
         total[u] = jnp.dot(left, jnp.concatenate(panels, axis=0), preferred_element_type=jnp.float32)
+
+
+def most_kernel(where, rows, table, p_ref, ax, bz, cy, t3, before, total):
+    listed, z, core = listed_blocks(where)
+    for u, (j, q, at) in enumerate(units(z)):
+        same = q * PER + at
+        panels = [ax[same], bz[z_panel(core, q, at)], cy[same]]
+        panels += [t3[z_panel(1 - core, q, at)], t3[NCB + same]]
+        left = p_columns(p_ref, table, [rows[j * NH + n] for n in listed[1:4] + listed[6:]])
+        total[u] = before[u] + jnp.dot(
+            left, jnp.concatenate(panels, axis=0), preferred_element_type=jnp.float32
+        )
 
 
 def rest_kernel(where, rows, keep, table, p_ref, total, t2, _, out_ref):
@@ -182,19 +191,31 @@
         compiler_params=limit,
         name="prepare",
     )(p_positions, owner_ids.reshape(RB, NCB), own)
-    bz, empty, table = lax.optimization_barrier((bz, empty, table))
+    where = jnp.stack([row, col])
+    sums = jax.ShapeDtypeStruct((NCB, RB * BS, BS), jnp.float32)
+    before = pl.pallas_call(
+        first_kernel,
+        out_shape=sums,
+        in_specs=[smem] * 3 + [vmem] * 3,
+        out_specs=vmem,
+        compiler_params=limit,
+        cost_estimate=pl.CostEstimate(flops=300_000_000, bytes_accessed=5_000_000, transcendentals=0),
+        name="first",
+    )(where, h_rows, table, p_blocks, own, t1)
+    bz, empty, table, before = lax.optimization_barrier((bz, empty, table, before))
     t2, t3 = (
         lax.ppermute(jnp.concatenate(x), "row", OTHER_CORE) for x in (rest + [ax], [bz, cy])
     )
     total = pl.pallas_call(
         most_kernel,
-        out_shape=jax.ShapeDtypeStruct((NCB, RB * BS, BS), jnp.float32),
-        in_specs=[smem] * 3 + [vmem] * 7,
+        out_shape=sums,
+        in_specs=[smem] * 3 + [vmem] * 6,
         out_specs=vmem,
+        input_output_aliases={8: 0},
         compiler_params=limit,
         cost_estimate=pl.CostEstimate(flops=1_200_000_000, bytes_accessed=10_000_000, transcendentals=0),
         name="most",
-    )(where, h_rows, table, p_blocks, own, ax, bz, cy, t1, t3)
+    )(where, h_rows, table, p_blocks, ax, bz, cy, t3, before)
     outgoing = pl.pallas_call(
         rest_kernel,
         out_shape=jax.ShapeDtypeStruct((NRG * CAP, BS, BS), jnp.bfloat16),

time: 138 us -> 138 us (level)
    pallas_call x1 -> x2, Pallas kernels: 3.43 us -> 4.76 us  [the longest x1 3.47 us: local(): pl.pallas_call(most_kernel, out_shape=sums, in_specs=[smem] * 3 + [vmem]...]
  transfers between devices with their start and end apart: 8 -> 8, of which waited for: 5 -> 5; matrix products, arithmetic and copies ran while one was open for 0% -> 0% of each run, Pallas kernels for 4% -> 5%
where the time goes in v7:
time: 138 us
  blocking collectives  90.5 us (66%)
  starting transfers between devices  21.1 us (15%)
  waiting for transfers between devices  15.1 us (11%)
  Pallas kernels  8.02 us (6%)
  local copies, waits for them, and re-layouts  2.18 us (2%)
    all_to_all x1, blocking collectives, local(): lax.all_to_all(outgoing, 'row', split_axis=0, concat_axis=0, tiled=True)  61.8 us
    all_to_all x1, blocking collectives, local(): lax.all_to_all(pick(row, col, h_blocks), 'col', split_axis=0, concat_axis...  28.6 us
    ppermute x2, starting transfers between devices, local(): rest = [lax.ppermute(third, BOTH, pairs) for pairs in (UP_Z, DOWN_Z)]  8.55 us
    ppermute x3, waiting for transfers between devices, local(): lax.ppermute(own, BOTH, pairs)  7.9 us
    ppermute x2, waiting for transfers between devices, local(): rest = [lax.ppermute(third, BOTH, pairs) for pairs in (UP_Z, DOWN_Z)]  7.21 us
    ppermute x3, starting transfers between devices, local(): lax.ppermute(own, BOTH, pairs)  6.76 us
    ppermute x2, starting transfers between devices, local(): lax.ppermute(jnp.concatenate(x), 'row', OTHER_CORE)  3.84 us
    pallas_call x1, Pallas kernels, local(): pl.pallas_call(most_kernel, out_shape=sums, in_specs=[smem] * 3 + [vmem]...  3.47 us
  transfers between devices with their start and end apart: 8, of which 5 were waited for; matrix products, arithmetic and copies ran while one was open for 0% of the time, Pallas kernels for 5%

profile of v7, /device:TPU:12, one launch (start us, length us, event | category | flops | bytes accessed | tf_op | source)
XLA Modules:
  0.0 137.6 jit_solution(9556934578251268138)
XLA Ops:
  0.0 0.0 copy-start.2
  0.0 0.0 copy-start.4
  0.0 0.8 dynamic-slice_bitcast_fusion.3
  0.9 0.0 copy-start
  0.9 0.0 copy-start.1
  0.9 0.1 select_select_fusion
  1.0 28.6 %all_to_all.10 = bf16[8,128,128]{2,1,0:T(8,128)(2,1)S(1)} all-to-all(bf16[8,128,128]{2,1,0:T(8,128)(2,1)S(1)} %select_select_fusion), channel_id=1, replica_groups={{0,18,9,15,6,12,3,21},{1,19,10,16,7,13,4,22},{2,20,11,17,8,14,5,23},{24..., dimensions={0} | all-to-all | bytes 524288 | tf_op jit(solution)/shard_map/all_to_all | solution.py:168
  29.7 6.6 %collective-permute-start = (bf16[8,128,128]{2,1,0:T(8,128)(2,1)S(1)}, bf16[8,128,128]{2,1,0:T(8,128)(2,1)S(1)}, u32[]{:S(2)}, u32[]{:S(2)}) collective-permute-start(bf16[8,128,128]{2,1,0:T(8,128)(2,1)S(1)} %all_to_all.10), channel_id=1, source_target_pairs={{397,0},{421,24},{398,1},{422,25},{399,2},{423,26},{400,3},{424,27... | collective-permute-start | bytes 786440 | tf_op jit(solution)/shard_map/ppermute | solution.py:177
  36.3 1.9 %collective-permute-start.1 = (bf16[8,128,128]{2,1,0:T(8,128)(2,1)S(1)}, bf16[8,128,128]{2,1,0:T(8,128)(2,1)S(1)}, u32[]{:S(2)}, u32[]{:S(2)}) collective-permute-start(bf16[8,128,128]{2,1,0:T(8,128)(2,1)S(1)} %all_to_all.10), channel_id=1, source_target_pairs={{395,0},{419,24},{384,1},{408,25},{385,2},{409,26},{386,3},{410,27... | collective-permute-start | bytes 786440 | tf_op jit(solution)/shard_map/ppermute | solution.py:177
  38.2 1.9 %collective-permute-start.2 = (bf16[8,128,128]{2,1,0:T(8,128)(2,1)S(1)}, bf16[8,128,128]{2,1,0:T(8,128)(2,1)S(1)}, u32[]{:S(2)}, u32[]{:S(2)}) collective-permute-start(bf16[8,128,128]{2,1,0:T(8,128)(2,1)S(1)} %all_to_all.10), channel_id=1, source_target_pairs={{0,24},{24,0},{48,72},{72,48},{96,120},{120,96},{144,168},{168,144... | collective-permute-start | bytes 786440 | tf_op jit(solution)/shard_map/ppermute | solution.py:178
  40.1 0.5 collective-permute-done
  40.6 6.7 %collective-permute-done.1 = bf16[8,128,128]{2,1,0:T(8,128)(2,1)S(1)} collective-permute-done((bf16[8,128,128]{2,1,0:T(8,128)(2,1)S(1)}, bf16[8,128,128]{2,1,0:T(8,128)(2,1)S(1)}, u32[]{:S(2)}, u32[]{:S(2)}) %collective-permute-start.1) | collective-permute-done | bytes 262176 | tf_op jit(solution)/shard_map/ppermute | solution.py:177
  47.4 0.1 pad_maximum_fusion.2._.own
  47.4 0.0 collective-permute-done.2.t1
  47.5 2.5 %collective-permute-start.3 = (bf16[24,128,128]{2,1,0:T(8,128)(2,1)S(1)}, bf16[24,128,128]{2,1,0:T(8,128)(2,1)S(1)}, u32[]{:S(2)}, u32[]{:S(2)}) collective-permute-start(bf16[24,128,128]{2,1,0:T(8,128)(2,1)S(1)} %pad_maximum_fusion.2._.own), channel_id=1, source_target_pairs={{11,0},{25,24},{0,1},{26,25},{1,2},{27,26},{2,3},{28,27},{3,4},{29... | collective-permute-start | bytes 2359304 | tf_op jit(solution)/shard_map/ppermute | solution.py:180
  49.9 2.4 %collective-permute-start.5 = (bf16[24,128,128]{2,1,0:T(8,128)(2,1)S(1)}, bf16[24,128,128]{2,1,0:T(8,128)(2,1)S(1)}, u32[]{:S(2)}, u32[]{:S(2)}) collective-permute-start(bf16[24,128,128]{2,1,0:T(8,128)(2,1)S(1)} %pad_maximum_fusion.2._.own), channel_id=1, source_target_pairs={{48,0},{360,24},{49,1},{361,25},{50,2},{362,26},{51,3},{363,27},{5... | collective-permute-start | bytes 2359304 | tf_op jit(solution)/shard_map/ppermute | solution.py:180
  52.3 1.9 %collective-permute-start.4 = (bf16[24,128,128]{2,1,0:T(8,128)(2,1)S(1)}, bf16[24,128,128]{2,1,0:T(8,128)(2,1)S(1)}, u32[]{:S(2)}, u32[]{:S(2)}) collective-permute-start(bf16[24,128,128]{2,1,0:T(8,128)(2,1)S(1)} %pad_maximum_fusion.2._.own), channel_id=1, source_target_pairs={{384,0},{420,24},{385,1},{421,25},{386,2},{422,26},{387,3},{423,27... | collective-permute-start | bytes 2359304 | tf_op jit(solution)/shard_map/ppermute | solution.py:180
  54.2 0.1 pad_add_fusion.where
  54.3 0.0 copy-done.2
  54.3 0.0 copy-done.4
  54.3 1.7 %prepare.1 = (bf16[64,128,128]{2,1,0:T(8,128)(2,1)S(1)}, s32[176]{0:T(256)S(1)}) custom-call(s32[48]{0:T(128)S(1)} %copy-done.4, s32[2,24]{1,0:T(2,128)S(1)} %bitcast.13, bf16[24,128,128]{2,1,0:T(8,128)(2,1)S(1)} %pad_maximum_fusion.2._.own), custom_call_target="tpu_custom_call" | custom-call | tf_op jit(solution)/shard_map/prepare/pallas_call | solution.py:182
  56.0 0.0 copy-done
  56.1 0.0 copy-done.1
  56.1 1.3 first.1.before
  57.4 5.2 %collective-permute-done.3.bz = bf16[24,128,128]{2,1,0:T(8,128)(2,1)S(1)} collective-permute-done((bf16[24,128,128]{2,1,0:T(8,128)(2,1)S(1)}, bf16[24,128,128]{2,1,0:T(8,128)(2,1)S(1)}, u32[]{:S(2)}, u32[]{:S(2)}) %collective-permute-start.3) | collective-permute-done | bytes 786464 | tf_op jit(solution)/shard_map/ppermute | solution.py:180
  62.6 1.3 collective-permute-done.5.cy
  63.8 0.1 pad_maximum_fusion
  64.0 1.9 %collective-permute-start.6 = (bf16[48,128,128]{2,1,0:T(8,128)(2,1)S(1)}, bf16[48,128,128]{2,1,0:T(8,128)(2,1)S(1)}, u32[]{:S(2)}, u32[]{:S(2)}) collective-permute-start(bf16[48,128,128]{2,1,0:T(8,128)(2,1)S(1)} %pad_maximum_fusion), channel_id=1, source_target_pairs={{0,24},{24,0},{48,72},{72,48},{96,120},{120,96},{144,168},{168,144... | collective-permute-start | bytes 4718600 | tf_op jit(solution)/shard_map/ppermute | solution.py:207
  65.9 1.4 %collective-permute-done.4.ax = bf16[24,128,128]{2,1,0:T(8,128)(2,1)S(1)} collective-permute-done((bf16[24,128,128]{2,1,0:T(8,128)(2,1)S(1)}, bf16[24,128,128]{2,1,0:T(8,128)(2,1)S(1)}, u32[]{:S(2)}, u32[]{:S(2)}) %collective-permute-start.4) | collective-permute-done | bytes 786464 | tf_op jit(solution)/shard_map/ppermute | solution.py:180
  67.3 0.1 pad_maximum_fusion.1
  67.5 0.0 copy-start.3
  67.5 1.9 %collective-permute-start.7 = (bf16[40,128,128]{2,1,0:T(8,128)(2,1)S(1)}, bf16[40,128,128]{2,1,0:T(8,128)(2,1)S(1)}, u32[]{:S(2)}, u32[]{:S(2)}) collective-permute-start(bf16[40,128,128]{2,1,0:T(8,128)(2,1)S(1)} %pad_maximum_fusion.1), channel_id=1, source_target_pairs={{0,24},{24,0},{48,72},{72,48},{96,120},{120,96},{144,168},{168,144... | collective-permute-start | bytes 3932168 | tf_op jit(solution)/shard_map/ppermute | solution.py:207
  69.4 0.0 collective-permute-done.6.t3
  69.4 3.5 %most.1.total = f32[24,256,128]{2,1,0:T(8,128)S(1)} custom-call(s32[2]{0:T(128)S(1)} %pad_add_fusion.where, s32[192]{0:T(256)S(1)} %copy-done.1, s32[176]{0:T(256)S(1)} %get-tuple-element.17.table, bf16[48,128,128]{2,1,0:T(8,128)(2,1)S(1)} %copy-done, bf16[24,128,128]{2,1,0:T(8,128)(2,1)S(1)} %collective-permute-done.4.ax, ...), custom_call_target="tpu_custom_call", output_to_operand_aliasing={{}: (8, {})} | custom-call | flops 1200000000 | bytes 10000000 | tf_op jit(solution)/shard_map/most/pallas_call | solution.py:209
  72.9 0.0 collective-permute-done.7.t2
  72.9 0.0 copy-done.3
  72.9 1.6 %rest.1 = bf16[64,128,128]{2,1,0:T(8,128)(2,1)S(1)} custom-call(s32[2]{0:T(128)S(1)} %pad_add_fusion.where, s32[192]{0:T(256)S(1)} %copy-done.1, s32[2,24]{1,0:T(2,128)S(1)} %copy-done.3, s32[176]{0:T(256)S(1)} %get-tuple-element.17.table, bf16[48,128,128]{2,1,0:T(8,128)(2,1)S(1)} %copy-done, ...), custom_call_target="tpu_custom_call", output_to_operand_aliasing={{}: (7, {})} | custom-call | flops 400000000 | bytes 5000000 | tf_op jit(solution)/shard_map/rest/pallas_call | solution.py:219
  74.5 61.8 %all_to_all.11 = bf16[32,2,128,128]{3,2,1,0:T(8,128)(2,1)S(1)} all-to-all(bf16[32,2,128,128]{3,2,1,0:T(8,128)(2,1)S(1)} %bitcast.12), channel_id=1, replica_groups=mesh['row'=32,'col'=24] {'row'}, dimensions={0} | all-to-all | bytes 4194304 | tf_op jit(solution)/shard_map/all_to_all | solution.py:230
  136.3 1.3 copy.12
  (2 shorter events, 0.0 us)
Async XLA Ops:
  0.0 54.3 %copy-start.2 = (s32[2,24,1]{1,2,0:T(1,128)S(1)}, s32[2,24,1]{1,2,0:T(1,128)}, u32[]{:S(2)}) copy-start(s32[2,24,1]{1,2,0:T(1,128)} %param.11) | copy-start | bytes 580
  0.0 54.3 %copy-start.4 = (s32[48]{0:T(128)S(1)}, s32[48]{0:T(128)}, u32[]{:S(2)}) copy-start(s32[48]{0:T(128)} %pos.1) | copy-start | bytes 580
  0.9 55.2 %copy-start = (bf16[48,128,128]{2,1,0:T(8,128)(2,1)S(1)}, bf16[48,128,128]{2,1,0:T(8,128)(2,1)}, u32[]{:S(2)}) copy-start(bf16[48,128,128]{2,1,0:T(8,128)(2,1)} %p_ref.5) | copy-start | bytes 4718596
  0.9 55.2 %copy-start.1 = (s32[192]{0:T(256)S(1)}, s32[192]{0:T(256)}, u32[]{:S(2)}) copy-start(s32[192]{0:T(256)} %rows.5) | copy-start | bytes 2308
  29.7 11.0 %collective-permute-start = (bf16[8,128,128]{2,1,0:T(8,128)(2,1)S(1)}, bf16[8,128,128]{2,1,0:T(8,128)(2,1)S(1)}, u32[]{:S(2)}, u32[]{:S(2)}) collective-permute-start(bf16[8,128,128]{2,1,0:T(8,128)(2,1)S(1)} %all_to_all.10), channel_id=1, source_target_pairs={{397,0},{421,24},{398,1},{422,25},{399,2},{423,26},{400,3},{424,27... | collective-permute-start | bytes 786440 | tf_op jit(solution)/shard_map/ppermute | solution.py:177
  36.3 11.1 %collective-permute-start.1 = (bf16[8,128,128]{2,1,0:T(8,128)(2,1)S(1)}, bf16[8,128,128]{2,1,0:T(8,128)(2,1)S(1)}, u32[]{:S(2)}, u32[]{:S(2)}) collective-permute-start(bf16[8,128,128]{2,1,0:T(8,128)(2,1)S(1)} %all_to_all.10), channel_id=1, source_target_pairs={{395,0},{419,24},{384,1},{408,25},{385,2},{409,26},{386,3},{410,27... | collective-permute-start | bytes 786440 | tf_op jit(solution)/shard_map/ppermute | solution.py:177
  38.2 9.2 %collective-permute-start.2 = (bf16[8,128,128]{2,1,0:T(8,128)(2,1)S(1)}, bf16[8,128,128]{2,1,0:T(8,128)(2,1)S(1)}, u32[]{:S(2)}, u32[]{:S(2)}) collective-permute-start(bf16[8,128,128]{2,1,0:T(8,128)(2,1)S(1)} %all_to_all.10), channel_id=1, source_target_pairs={{0,24},{24,0},{48,72},{72,48},{96,120},{120,96},{144,168},{168,144... | collective-permute-start | bytes 786440 | tf_op jit(solution)/shard_map/ppermute | solution.py:178
  47.5 15.1 %collective-permute-start.3 = (bf16[24,128,128]{2,1,0:T(8,128)(2,1)S(1)}, bf16[24,128,128]{2,1,0:T(8,128)(2,1)S(1)}, u32[]{:S(2)}, u32[]{:S(2)}) collective-permute-start(bf16[24,128,128]{2,1,0:T(8,128)(2,1)S(1)} %pad_maximum_fusion.2._.own), channel_id=1, source_target_pairs={{11,0},{25,24},{0,1},{26,25},{1,2},{27,26},{2,3},{28,27},{3,4},{29... | collective-permute-start | bytes 2359304 | tf_op jit(solution)/shard_map/ppermute | solution.py:180
  49.9 13.9 %collective-permute-start.5 = (bf16[24,128,128]{2,1,0:T(8,128)(2,1)S(1)}, bf16[24,128,128]{2,1,0:T(8,128)(2,1)S(1)}, u32[]{:S(2)}, u32[]{:S(2)}) collective-permute-start(bf16[24,128,128]{2,1,0:T(8,128)(2,1)S(1)} %pad_maximum_fusion.2._.own), channel_id=1, source_target_pairs={{48,0},{360,24},{49,1},{361,25},{50,2},{362,26},{51,3},{363,27},{5... | collective-permute-start | bytes 2359304 | tf_op jit(solution)/shard_map/ppermute | solution.py:180
  52.3 15.0 %collective-permute-start.4 = (bf16[24,128,128]{2,1,0:T(8,128)(2,1)S(1)}, bf16[24,128,128]{2,1,0:T(8,128)(2,1)S(1)}, u32[]{:S(2)}, u32[]{:S(2)}) collective-permute-start(bf16[24,128,128]{2,1,0:T(8,128)(2,1)S(1)} %pad_maximum_fusion.2._.own), channel_id=1, source_target_pairs={{384,0},{420,24},{385,1},{421,25},{386,2},{422,26},{387,3},{423,27... | collective-permute-start | bytes 2359304 | tf_op jit(solution)/shard_map/ppermute | solution.py:180
  64.0 5.4 %collective-permute-start.6 = (bf16[48,128,128]{2,1,0:T(8,128)(2,1)S(1)}, bf16[48,128,128]{2,1,0:T(8,128)(2,1)S(1)}, u32[]{:S(2)}, u32[]{:S(2)}) collective-permute-start(bf16[48,128,128]{2,1,0:T(8,128)(2,1)S(1)} %pad_maximum_fusion), channel_id=1, source_target_pairs={{0,24},{24,0},{48,72},{72,48},{96,120},{120,96},{144,168},{168,144... | collective-permute-start | bytes 4718600 | tf_op jit(solution)/shard_map/ppermute | solution.py:207
  67.5 5.4 %copy-start.3 = (s32[2,24]{1,0:T(2,128)S(1)}, s32[2,24]{1,0:T(2,128)}, u32[]{:S(2)}) copy-start(s32[2,24]{1,0:T(2,128)} %keep.1) | copy-start | bytes 580
  67.5 5.4 %collective-permute-start.7 = (bf16[40,128,128]{2,1,0:T(8,128)(2,1)S(1)}, bf16[40,128,128]{2,1,0:T(8,128)(2,1)S(1)}, u32[]{:S(2)}, u32[]{:S(2)}) collective-permute-start(bf16[40,128,128]{2,1,0:T(8,128)(2,1)S(1)} %pad_maximum_fusion.1), channel_id=1, source_target_pairs={{0,24},{24,0},{48,72},{72,48},{96,120},{120,96},{144,168},{168,144... | collective-permute-start | bytes 3932168 | tf_op jit(solution)/shard_map/ppermute | solution.py:207
